TPU v7x, 768 devices: a whole 4x8x12 slice. The times are simulated.
768 devices in a mesh: gx: 12 (over z), gy: 4 (over x), gz: 16 (over y, core).
Axes of the slice: x: 4, y: 8, z: 12, core: 2. Of those that a mesh axis runs over, the one named last changes fastest.
Arguments:
- density: float32 [48, 16, 2048], P('gx', 'gy', 'gz'), may hold values from 0.5 to 2
- velocity: float32 [3, 48, 16, 2048], P(None, 'gx', 'gy', 'gz'), may hold values from -3 to 3
- pressure: float32 [48, 16, 2048], P('gx', 'gy', 'gz'), may hold values from 0.5 to 2
- fine_density: float32 [12, 4, 32, 8, 128], P('gx', 'gy', 'gz'), may hold values from -0.2 to 0.2
- fine_velocity: float32 [3, 12, 4, 32, 8, 128], P(None, 'gx', 'gy', 'gz'), may hold values from -3 to 3
- fine_pressure: float32 [12, 4, 32, 8, 128], P('gx', 'gy', 'gz'), may hold values from -0.2 to 0.2
- box_parent: int32 [12, 4, 32, 1], P('gx', 'gy'), may hold values from 0 to 15; in each aligned block of 2 rows (0 to 1, 2 to 3, ..., all dimensions but the last counted through in order) no two rows name the same one
- box_shift: int32 [12, 4, 32], P('gx', 'gy'), may hold values from 0 to 120
Outputs:
- coarse_state: float32 [5, 48, 16, 2048], P(None, 'gx', 'gy', 'gz')
- fine_state: float32 [5, 12, 4, 32, 8, 128], P(None, 'gx', 'gy', 'gz')
Inputs may be any that keep to these rules, and one draw needn't show every extreme that they name: `box_parent`: among the 2 boxes of one owner (one aligned block), no parent is named more than 1 times, and in some blocks one parent is named exactly 1 times.
All inputs are finite; a program needn't handle non-finite values.
Results may differ from a plain program's by a relative error of at most 0.0003.
Values sent between devices are 32-bit elements; how exact they have to be, the bound alone decides.
No kernel may reach another device: no remote copies, remote signals or barrier semaphores. Data moves between devices by JAX's collectives and lax.ppermute only.
A program may use at most 32 MiB of HBM per device.

v0:
```python
import jax
import jax.numpy as jnp
from jax import lax
from jax.experimental import pallas as pl
from jax.experimental.pallas import tpu as pltpu
from jax.sharding import PartitionSpec as P

F32 = jnp.float32
GROUP = 10
PER_ROW = 12
OLD = 20
TILES = 3


def iota(dim, shape=(8, 128)):
    return lax.broadcasted_iota(jnp.int32, shape, dim)


def roll(value, shift, axis):
    size = value.shape[axis]
    shift = shift % size
    return value if shift == 0 else pltpu.roll(value, shift, axis)


def inverse(value):
    guess = pl.reciprocal(value, approx=True)
    return guess * (2.0 - value * guess)


def root(value):
    return value * lax.rsqrt(jnp.maximum(value, 1e-30))


def conserved(prim):
    rho, u, v, w, p = prim
    return [rho, rho * u, rho * v, rho * w, 2.5 * p + 0.5 * rho * (u * u + v * v + w * w)]


def primitive(cons):
    inv = inverse(cons[0])
    u, v, w = cons[1] * inv, cons[2] * inv, cons[3] * inv
    p = 0.4 * (cons[4] - 0.5 * (cons[1] * u + cons[2] * v + cons[3] * w))
    return [cons[0], u, v, w, p]


def edges(before, here, after):
    down, up = here - before, after - here
    half = 0.5 * (
        jnp.maximum(jnp.minimum(down, up), 0.0) + jnp.minimum(jnp.maximum(down, up), 0.0)
    )
    return here + half, here - half


def hllc(left, right, normal):
    order = [0, 1 + normal] + [1 + d for d in range(3) if d != normal] + [4]
    rho_l, un_l, ut_l, us_l, p_l = [left[k] for k in order]
    rho_r, un_r, ut_r, us_r, p_r = [right[k] for k in order]
    a_l, a_r = p_l * inverse(rho_l), p_r * inverse(rho_r)
    c_l, c_r = root(1.4 * a_l), root(1.4 * a_r)
    s_l = jnp.minimum(un_l - c_l, un_r - c_r)
    s_r = jnp.maximum(un_l + c_l, un_r + c_r)
    m_l, m_r = rho_l * (s_l - un_l), rho_r * (s_r - un_r)
    star = (p_r - p_l + m_l * un_l - m_r * un_r) * inverse(m_l - m_r)
    side = (s_l >= 0.0) | (star >= 0.0)
    pick = lambda one, other: jnp.where(side, one, other)
    rho, un, ut, us, p = (
        pick(rho_l, rho_r),
        pick(un_l, un_r),
        pick(ut_l, ut_r),
        pick(us_l, us_r),
        pick(p_l, p_r),
    )
    a, m, s = pick(a_l, a_r), pick(m_l, m_r), pick(s_l, s_r)
    limited = pick(jnp.minimum(s_l, 0.0), jnp.maximum(s_r, 0.0))
    e = 2.5 * a + 0.5 * (un * un + ut * ut + us * us)
    energy = rho * e
    r = inverse(s - star)
    factor = m * r
    momentum = rho * un
    mass = momentum + limited * (factor - rho)
    force = momentum * un + p + limited * (factor * star - momentum)
    power = (energy + p) * un + limited * (
        factor * e + (star - un) * (factor * star + p * r) - energy
    )
    result = [None] * 5
    for k, part in zip(order, [mass, force, ut * mass, us * mass, power]):
        result[k] = part
    return result


def line_change(fields, axis, normal, wide=None):
    high, low = [], []
    for k in range(5):
        here = fields[k]
        if wide is None:
            after, before = roll(here, -1, axis), roll(here, 1, axis)
        else:
            after, before = roll(wide[k], -1, axis)[0:8], roll(wide[k], 1, axis)[0:8]
        one, other = edges(before, here, after)
        high.append(one)
        low.append(roll(other, -1, axis))
    flux = hllc(high, low, normal)
    return [part - roll(part, 1, axis) for part in flux]


def next_group(tiles, j):
    lane = iota(1, tiles[j][0].shape)
    other = tiles[j + 1] if j + 1 < len(tiles) and tiles[j + 1] is not None else tiles[j]
    return [jnp.where(lane < 96, roll(a, -32, 1), roll(b, -32, 1)) for a, b in zip(tiles[j], other)]


def prior_group(tiles, j):
    lane = iota(1, tiles[j][0].shape)
    other = tiles[j - 1] if j > 0 and tiles[j - 1] is not None else tiles[j]
    return [jnp.where(lane >= 32, roll(a, 32, 1), roll(b, 32, 1)) for a, b in zip(tiles[j], other)]


def group_changes(tiles, wanted):
    high, low, flux = [None] * len(tiles), [None] * len(tiles), [None] * len(tiles)
    for j in wanted:
        pairs = [
            edges(before, here, after)
            for before, here, after in zip(prior_group(tiles, j), tiles[j], next_group(tiles, j))
        ]
        high[j] = [pair[0] for pair in pairs]
        low[j] = [pair[1] for pair in pairs]
    for j in wanted:
        flux[j] = hllc(high[j], next_group(low, j), 0)
    return {
        j: [a - b for a, b in zip(flux[j], prior_group(flux, j))] for j in wanted
    }


def ends_kernel(rho_ref, vel_ref, p_ref, out_ref):
    lane = iota(1, (4, 128))
    for f in range(5):
        total = None
        for x in range(4):
            row = rho_ref[x] if f == 0 else (p_ref[x] if f == 4 else vel_ref[f - 1, x])
            part = lane - 32 * x
            first = roll(row, 32 * x + 8, 1)
            last = roll(row, 32 * x + 24, 1)
            piece = jnp.where(part < 16, first, last)
            total = piece if total is None else jnp.where(part < 0, total, piece)
        out_ref[f] = total


def block_kernel(ends_ref, before_ref, after_ref, rho_ref, vel_ref, p_ref, out_ref, up_ref, down_ref):
    lane = iota(1, (4, 128)) % 32
    for f in range(5):
        edge = jnp.where(
            lane < 8,
            roll(before_ref[f], -16, 1),
            jnp.where(lane >= 24, roll(after_ref[f], 16, 1), ends_ref[f]),
        )
        for copy in range(4):
            out_ref[copy, 20 + f] = edge
        up_ref[5 + f] = edge
        down_ref[5 + f] = edge
        for x in range(4):
            row = rho_ref[x] if f == 0 else (p_ref[x] if f == 4 else vel_ref[f - 1, x])
            for copy in range(4):
                out_ref[copy, 5 * x + f] = row
            if x == 3:
                up_ref[f] = row
            if x == 0:
                down_ref[f] = row


def coarse_kernel(
    place_ref, parent_ref, shift_ref, own_ref, prior_ref, next_ref, far_prior_ref, far_next_ref,
    new_ref, message_ref,
    prim_ref, edge_ref, section_ref, section_edge_ref, made_ref, made_edge_ref,
    old_pack_ref, body_ref, tips_ref,
):
    gy, gz = place_ref[0], place_ref[1]
    for k in range(4):
        source = lax.rem(gy + k, 4)
        for base, ref, tile in ((5, prior_ref, 5), (25, own_ref, 10), (45, next_ref, 15)):
            rows, tips = ref[source, 0:20], ref[source, 20:25]
            if k < 3:
                at = 2 + 4 * k
                prim_ref[base : base + 20, at : at + 4] = rows
                edge_ref[tile : tile + 5, at : at + 4] = tips
            else:
                prim_ref[base : base + 20, 14:16] = rows[:, 0:2]
                prim_ref[base : base + 20, 0:2] = rows[:, 2:4]
                edge_ref[tile : tile + 5, 14:16] = tips[:, 0:2]
                edge_ref[tile : tile + 5, 0:2] = tips[:, 2:4]
    prim_ref[0:5, 2:6] = far_prior_ref[0:5]
    edge_ref[0:5, 2:6] = far_prior_ref[5:10]
    prim_ref[65:70, 2:6] = far_next_ref[0:5]
    edge_ref[20:25, 2:6] = far_next_ref[5:10]

    def prim_row(x):
        return [prim_ref[5 * (x + 5) + f] for f in range(5)]

    def section_row(x, rows=16):
        return [section_ref[5 * (x + 3) + f, 0:rows] for f in range(5)]

    low = flux = high_prior = None
    for x in range(-4, 8):
        here = prim_row(x)
        pairs = [edges(b, h, a) for b, h, a in zip(prim_row(x - 1), here, prim_row(x + 1))]
        low = [pair[1] for pair in pairs]
        if high_prior is not None:
            flux_next = hllc(high_prior, low, 0)
            if flux is not None:
                middle = prim_row(x - 1)
                by_y = line_change(middle, 0, 1)
                by_z = line_change(middle, 1, 2)
                state = conserved(middle)
                section = [
                    state[f] - 0.05 * (flux_next[f] - flux[f] + by_y[f] + by_z[f]) for f in range(5)
                ]
                for f, value in enumerate(primitive(section)):
                    section_ref[5 * (x - 1 + 3) + f] = value
            flux = flux_next
        high_prior = [pair[0] for pair in pairs]
    tiles = [[edge_ref[5 * t + f] for f in range(5)] for t in range(5)]
    by_x = group_changes(tiles, (1, 2, 3))
    for t in (1, 2, 3):
        by_y = line_change(tiles[t], 0, 1)
        by_z = line_change(tiles[t], 1, 2)
        state = conserved(tiles[t])
        section = [state[f] - 0.05 * (by_x[t][f] + by_y[f] + by_z[f]) for f in range(5)]
        for f, value in enumerate(primitive(section)):
            section_edge_ref[5 * (t - 1) + f] = value

    def advance(old, here, changes):
        start, state = conserved(old), conserved(here)
        return [
            0.5 * start[f] + 0.5 * (state[f] - 0.05 * (changes[0][f] + changes[1][f] + changes[2][f]))
            for f in range(5)
        ]

    flux = high_prior = None
    for x in range(-2, 6):
        here = section_row(x, 8)
        pairs = [
            edges(b, h, a) for b, h, a in zip(section_row(x - 1, 8), here, section_row(x + 1, 8))
        ]
        low = [pair[1] for pair in pairs]
        if high_prior is not None:
            flux_next = hllc(high_prior, low, 0)
            if flux is not None:
                middle = section_row(x - 1, 8)
                by_y = line_change(middle, 0, 1, section_row(x - 1))
                by_z = line_change(middle, 1, 2)
                old = [part[0:8] for part in prim_row(x - 1)]
                by_x_row = [b - a for a, b in zip(flux, flux_next)]
                for f, value in enumerate(advance(old, middle, (by_x_row, by_y, by_z))):
                    made_ref[5 * x + f] = value
            flux = flux_next
        high_prior = [pair[0] for pair in pairs]
    wide = [[section_edge_ref[5 * t + f] for f in range(5)] for t in range(3)]
    tiles = [[part[0:8] for part in tile] for tile in wide]
    by_x = group_changes(tiles, (0, 1, 2))
    for t in range(3):
        by_y = line_change(tiles[t], 0, 1, wide[t])
        by_z = line_change(tiles[t], 1, 2)
        old = [edge_ref[5 * (t + 1) + f, 0:8] for f in range(5)]
        for f, value in enumerate(advance(old, tiles[t], (by_x[t], by_y, by_z))):
            made_edge_ref[5 * t + f] = value

    lane, sub = iota(1), iota(0)

    def spot(x):
        return (0, 3) if x < 0 else ((2, 0) if x > 3 else (1, x))

    for f in range(5):
        olds, news = {}, {}
        for x in range(-1, 5):
            tile, group = spot(x)
            main = prim_ref[5 * (x + 5) + f, 0:8]
            tips = edge_ref[5 * (tile + 1) + f, 0:8]
            under, over = roll(tips, -32 * group - 8, 1), roll(tips, 104 - 32 * group, 1)
            olds[x] = (main, jnp.where(lane == 127, under, main), jnp.where(lane == 0, over, main))
            main, tips = made_ref[5 * (x + 1) + f], made_edge_ref[5 * tile + f]
            under, over = roll(tips, -32 * group - 8, 1), roll(tips, 104 - 32 * group, 1)
            main = jnp.where(lane < 4, under, jnp.where(lane >= 124, over, main))
            news[x] = (main, jnp.where(lane == 127, under, main), jnp.where(lane == 0, over, main))
            if 0 <= x < 4:
                new_ref[f, x] = main[2:6]
        inner = (sub >= 2) & (sub < 6)
        for x in range(4):
            face = olds[-1 if x < 2 else 4][0]
            top, bottom = (-2, 4) if x % 2 == 0 else (-4, 2)
            for kind in range(3):
                old_pack_ref[kind, 4 * f + x] = jnp.where(
                    sub == 0,
                    roll(face, top, 0),
                    jnp.where(sub == 7, roll(face, bottom, 0), olds[x][kind]),
                )
        for half, (out, near, far) in enumerate(((-1, 0, 1), (4, 3, 2))):
            body_ref[2 * f + half] = jnp.where(
                inner,
                news[out][0],
                jnp.where(
                    sub == 0,
                    roll(news[far][0], -1, 0),
                    jnp.where(sub == 7, roll(news[far][0], 1, 0), news[near][0]),
                ),
            )
            for kind in range(3):
                tips_ref[kind, 2 * f + half] = jnp.where(
                    inner,
                    news[near][kind],
                    jnp.where(sub < 2, roll(news[far][kind], -2, 0), roll(news[far][kind], 2, 0)),
                )

    def send(owner, carry):
        hit = parent_ref[2 * owner] == gz
        other = parent_ref[2 * owner + 1] == gz
        shift = jnp.where(hit, shift_ref[2 * owner], shift_ref[2 * owner + 1])

        @pl.when(hit | other)
        def _():
            kind = jnp.where(shift == 0, 1, jnp.where(shift == 120, 2, 0))
            for tile in range(TILES):
                total = None
                for j in range(PER_ROW):
                    k = tile * PER_ROW + j
                    if k >= OLD + 10:
                        break
                    amount = lax.rem(GROUP * j + 129 - shift, 128)
                    if k < OLD:
                        piece = pltpu.roll(old_pack_ref[kind, k], amount, 1)
                    else:
                        piece = jnp.where(
                            (lane == GROUP * j) | (lane == GROUP * j + 9),
                            pltpu.roll(tips_ref[kind, k - OLD], amount, 1),
                            pltpu.roll(body_ref[k - OLD], amount, 1),
                        )
                    total = piece if total is None else jnp.where(lane < GROUP * j, total, piece)
                message_ref[owner, tile] = total

        return carry

    lax.fori_loop(0, 16, send, 0)


def fine_kernel(
    place_ref, parent_ref, got_ref, rho_ref, vel_ref, p_ref, out_ref, message_ref, mid_ref, tip_ref
):
    gz = place_ref[1]
    lane, sub = iota(1), iota(0)
    part = lane % 16
    yc, xc = lane // 32, sub // 2
    parents = [parent_ref[2 * gz + box] for box in range(2)]

    for box in range(2):
        for k in range(OLD + 10):
            j = k % PER_ROW
            tile = got_ref[parents[box], k // PER_ROW]
            at = GROUP * j + 1 + part // 2
            mid_ref[box, k] = jnp.take_along_axis(tile, at, axis=1)
            at = GROUP * j + jnp.where(part < 8, 0, 9)
            tip_ref[box, k] = jnp.take_along_axis(tile, at, axis=1)

    def row(ref, box, k, s):
        return jnp.broadcast_to(ref[box, k, s : s + 1, :], (8, 128))

    def by_y(items):
        return jnp.where(
            yc < 2,
            jnp.where(yc == 0, items[0], items[1]),
            jnp.where(yc == 2, items[2], items[3]),
        )

    def by_x(items):
        return jnp.where(
            xc < 2,
            jnp.where(xc == 0, items[0], items[1]),
            jnp.where(xc == 2, items[2], items[3]),
        )

    def inside(box, f):
        return by_x([by_y([row(mid_ref, box, 4 * f + x, 2 + y) for y in range(4)]) for x in range(4)])

    def old_ghosts(box, f):
        low = by_y([row(mid_ref, box, 4 * f + y // 2, 7 * (y % 2)) for y in range(4)])
        high = by_y([row(mid_ref, box, 4 * f + 2 + y // 2, 7 * (y % 2)) for y in range(4)])
        along_x = jnp.where(sub < 4, low, high)
        low = by_x([row(mid_ref, box, 4 * f + x, 1) for x in range(4)])
        high = by_x([row(mid_ref, box, 4 * f + x, 6) for x in range(4)])
        along_y = jnp.where(lane < 64, low, high)
        along_z = by_x(
            [by_y([row(tip_ref, box, 4 * f + x, 2 + y) for y in range(4)]) for x in range(4)]
        )
        return along_x, along_y, along_z

    def new_ghosts(box, f):
        k = OLD + 2 * f
        low = by_y([row(mid_ref, box, k, 2 + y) for y in range(4)])
        high = by_y([row(mid_ref, box, k + 1, 2 + y) for y in range(4)])
        along_x = jnp.where(sub < 4, low, high)
        spots = ((k, 1, 6), (k, 0, 7), (k + 1, 0, 7), (k + 1, 1, 6))
        low = by_x([row(mid_ref, box, at, one) for at, one, _ in spots])
        high = by_x([row(mid_ref, box, at, one) for at, _, one in spots])
        along_y = jnp.where(lane < 64, low, high)
        near, far = (2, 3, 4, 5), (0, 1, 6, 7)
        spots = ((k, near), (k, far), (k + 1, far), (k + 1, near))
        along_z = by_x([by_y([row(tip_ref, box, at, s) for s in rows]) for at, rows in spots])
        return along_x, along_y, along_z

    directions = (
        (0, 1, sub == 0, sub == 7, 4, sub >= 4),
        (1, 16, lane < 16, lane >= 112, 64, lane >= 64),
        (1, 1, part == 0, part == 15, 8, part >= 8),
    )

    def changes(fields, ghosts, bounds):
        total = None
        for normal, (axis, step, first, last, park, parked) in enumerate(directions):
            high, low, up = [[], []], [[], []], [[], []]
            for box in range(2):
                for f in range(5):
                    here, ghost = fields[box][f], ghosts[box][normal][f]
                    after = jnp.where(last, ghost, roll(here, -step, axis))
                    before = jnp.where(first, ghost, roll(here, step, axis))
                    one, other = edges(before, here, after)
                    high[box].append(one)
                    low[box].append(other)
                    up[box].append(jnp.where(last, ghost, roll(other, -step, axis)))
            right = [jnp.where(parked, roll(b, park, axis), a) for a, b in zip(low[0], low[1])]
            bottom = hllc(bounds[normal], right, normal)
            found = []
            for box in range(2):
                flux = hllc(high[box], up[box], normal)
                under = bottom if box == 0 else [roll(item, -park, axis) for item in bottom]
                found.append(
                    [a - jnp.where(first, b, roll(a, step, axis)) for a, b in zip(flux, under)]
                )
            total = (
                found
                if total is None
                else [[a + b for a, b in zip(t, g)] for t, g in zip(total, found)]
            )
        return total

    def lower_bounds(ghosts):
        return [
            [
                jnp.where(parked, roll(ghosts[1][normal][f], park, axis), ghosts[0][normal][f])
                for f in range(5)
            ]
            for normal, (axis, _, _, _, park, parked) in enumerate(directions)
        ]

    def substep(states, fields, ghosts):
        bounds = lower_bounds(ghosts)
        moved = changes(fields, ghosts, bounds)
        section = [[s - 0.05 * m for s, m in zip(states[b], moved[b])] for b in range(2)]
        moved = changes([primitive(item) for item in section], ghosts, bounds)
        return [
            [
                0.5 * s + 0.5 * (t - 0.05 * m)
                for s, t, m in zip(states[b], section[b], moved[b])
            ]
            for b in range(2)
        ]

    ghosts, fields = [], []
    for box in range(2):
        found = [old_ghosts(box, f) for f in range(5)]
        ghosts.append([[found[f][d] for f in range(5)] for d in range(3)])
        details = [rho_ref[box], vel_ref[0, box], vel_ref[1, box], vel_ref[2, box], p_ref[box]]
        fields.append([inside(box, f) + details[f] for f in range(5)])
    states = substep([conserved(item) for item in fields], fields, ghosts)
    later = []
    for box in range(2):
        found = [new_ghosts(box, f) for f in range(5)]
        later.append(
            [
                primitive(
                    [
                        0.5 * (a + b)
                        for a, b in zip(conserved(ghosts[box][d]), [found[f][d] for f in range(5)])
                    ]
                )
                for d in range(3)
            ]
        )
    states = substep(states, [primitive(item) for item in states], later)
    for box in range(2):
        packed = None
        for f in range(5):
            value = states[box][f]
            out_ref[f, box] = value
            value = value + roll(value, -1, 0)
            value = value + roll(value, -1, 1)
            value = (value + roll(value, -16, 1)) * 0.125
            inside_lane = lane % 32
            at = (inside_lane // 8) * 32 + (inside_lane % 8) * 2
            value = jnp.take_along_axis(value, at, axis=1)
            if f == 0:
                packed = value
            elif f < 4:
                packed = jnp.where(lane // 32 == f, value, packed)
            else:
                packed = jnp.where((sub % 2 == 1) & (lane < 32), roll(value, 1, 0), packed)
        message_ref[parents[box]] = packed


def final_kernel(place_ref, parent_ref, shift_ref, new_ref, got_ref, out_ref, sum_ref):
    gz = place_ref[1]
    lane = iota(1)

    def add(owner, carry):
        hit = parent_ref[2 * owner] == gz
        other = parent_ref[2 * owner + 1] == gz
        shift = jnp.where(hit, shift_ref[2 * owner], shift_ref[2 * owner + 1])

        def covered(carry):
            count, sums = carry
            inside = (lane >= shift) & (lane < shift + 8)
            value = got_ref[owner]
            parts = [
                item
                + jnp.where(inside, pltpu.roll(value, lax.rem(shift + 128 - 8 * k, 128), 1), 0.0)
                for k, item in enumerate(sums)
            ]
            return count + jnp.where(inside, 1.0, 0.0), parts

        return lax.cond(hit | other, covered, lambda same: same, carry)

    zero = jnp.zeros((8, 128), F32)
    count, sums = lax.fori_loop(0, 16, add, (zero, [zero] * 16))
    share = inverse(jnp.maximum(count, 1.0))
    for k in range(16):
        sum_ref[8 * k : 8 * k + 8] = sums[k] * share
    for f in range(5):
        for x in range(4):
            start = (0 if f == 4 else 32 * f) + 2 * x + (1 if f == 4 else 0)
            value = sum_ref[pl.ds(start, 4, stride=8)]
            out_ref[f, x] = jnp.where(count[0:4] > 0.0, value, new_ref[f, x])


def shape(*dims):
    return jax.ShapeDtypeStruct(dims, F32)


def call(kernel, outs, scalars, arrays, scratch=()):
    return pl.pallas_call(
        kernel,
        out_shape=outs,
        in_specs=[pl.BlockSpec(memory_space=pltpu.SMEM)] * scalars
        + [pl.BlockSpec(memory_space=pltpu.VMEM)] * arrays,
        out_specs=jax.tree.map(lambda _: pl.BlockSpec(memory_space=pltpu.VMEM), outs),
        scratch_shapes=[pltpu.VMEM(dims, F32) for dims in scratch],
        compiler_params=pltpu.CompilerParams(vmem_limit_bytes=32 * 1024 * 1024),
    )


def shifted(value, axis, step):
    size = lax.axis_size(axis)
    return lax.ppermute(value, axis, [(i, (i + step) % size) for i in range(size)])


def on_device(
    density, velocity, pressure, fine_density, fine_velocity, fine_pressure, box_parent, box_shift
):
    assert density.shape == (4, 4, 128) and fine_density.shape == (1, 1, 2, 8, 128)
    place = jnp.stack([lax.axis_index("gy"), lax.axis_index("gz")]).astype(jnp.int32)
    parents, shifts = box_parent.reshape(32), box_shift.reshape(32)
    ends = call(ends_kernel, shape(5, 4, 128), 0, 3)(density, velocity, pressure)
    before, after = shifted(ends, "gz", 1), shifted(ends, "gz", -1)
    block, for_up, for_down = call(
        block_kernel, (shape(4, 25, 4, 128), shape(10, 4, 128), shape(10, 4, 128)), 0, 6
    )(ends, before, after, density, velocity, pressure)
    far_prior, far_next = shifted(for_up, "gx", 2), shifted(for_down, "gx", -2)
    own = lax.all_to_all(block, "gy", 0, 0, tiled=True)
    prior, following = shifted(own, "gx", 1), shifted(own, "gx", -1)
    updated, message = call(
        coarse_kernel,
        (shape(5, 4, 4, 128), shape(16, TILES, 8, 128)),
        3,
        5,
        (
            (70, 16, 128),
            (25, 16, 128),
            (50, 16, 128),
            (15, 16, 128),
            (30, 8, 128),
            (15, 8, 128),
            (3, 20, 8, 128),
            (10, 8, 128),
            (3, 10, 8, 128),
        ),
    )(place, parents, shifts, own, prior, following, far_prior, far_next)
    got = lax.all_to_all(message, "gz", 0, 0, tiled=True)
    fine, means = call(
        fine_kernel,
        (shape(5, 2, 8, 128), shape(16, 8, 128)),
        2,
        4,
        ((2, 30, 8, 128), (2, 30, 8, 128)),
    )(
        place,
        parents,
        got,
        fine_density.reshape(2, 8, 128),
        fine_velocity.reshape(3, 2, 8, 128),
        fine_pressure.reshape(2, 8, 128),
    )
    incoming = lax.all_to_all(means, "gz", 0, 0, tiled=True)
    coarse = call(final_kernel, shape(5, 4, 4, 128), 3, 2, ((128, 128),))(
        place, parents, shifts, updated, incoming
    )
    return coarse, fine.reshape(5, 1, 1, 2, 8, 128)


def solution(mesh):
    in_specs = (
        P("gx", "gy", "gz"),
        P(None, "gx", "gy", "gz"),
        P("gx", "gy", "gz"),
        P("gx", "gy", "gz", None, None),
        P(None, "gx", "gy", "gz", None, None),
        P("gx", "gy", "gz", None, None),
        P("gx", "gy", None, None),
        P("gx", "gy", None),
    )
    out_specs = (P(None, "gx", "gy", "gz"), P(None, "gx", "gy", "gz", None, None))
    return jax.shard_map(
        on_device, mesh=mesh, in_specs=in_specs, out_specs=out_specs, check_vma=False
    )
```

profile of v0, /device:TPU:1, one launch (start us, length us, event | category | flops | bytes accessed | tf_op | source)
XLA Modules:
  0.0 88.1 jit_solution(5620078169897576465)
XLA Ops:
  0.6 0.0 copy-start
  0.6 0.7 copy-done
  1.4 0.0 copy-start.1
  1.4 0.7 copy-done.1
  2.1 0.0 copy-start.2
  2.1 0.7 copy-done.2
  2.8 0.1 shard_map.95.ends_ref
  2.9 10.5 %collective-permute-start.1 = (f32[5,4,128]{2,1,0:T(4,128)S(1)}, f32[5,4,128]{2,1,0:T(4,128)S(1)}, u32[]{:S(2)}, u32[]{:S(2)}) collective-permute-start(f32[5,4,128]{2,1,0:T(4,128)S(1)} %shard_map.95.ends_ref), channel_id=1, source_target_pairs={{0,15},{1,0},{2,1},{3,2},{4,3},{5,4},{6,5},{7,6},{8,7},{9,8},{10,9... | collective-permute-start | bytes 30728 | tf_op jit(solution)/shard_map/ppermute | solution.py:558
  13.4 0.0 collective-permute-start
  13.4 0.8 collective-permute-done.1.after_ref
  14.2 0.3 collective-permute-done.before_ref
  14.6 0.1 shard_map.96
  14.7 7.6 %all_to_all.15.own_ref = f32[4,25,4,128]{3,2,1,0:T(4,128)S(1)} all-to-all(f32[4,25,4,128]{3,2,1,0:T(4,128)S(1)} %get-tuple-element.9), channel_id=1, replica_groups=mesh['gx'=12,'gy'=4,'gz'=16] {'gy'}, dimensions={0} | all-to-all | bytes 409600 | tf_op jit(solution)/shard_map/all_to_all | solution.py:573
  22.3 9.1 %collective-permute-start.3 = (f32[4,25,4,128]{3,2,1,0:T(4,128)S(1)}, f32[4,25,4,128]{3,2,1,0:T(4,128)S(1)}, u32[]{:S(2)}, u32[]{:S(2)}) collective-permute-start(f32[4,25,4,128]{3,2,1,0:T(4,128)S(1)} %all_to_all.15.own_ref), channel_id=1, source_target_pairs={{0,704},{64,0},{128,64},{192,128},{256,192},{320,256},{384,320},{4... | collective-permute-start | bytes 614408 | tf_op jit(solution)/shard_map/ppermute | solution.py:558
  31.4 1.9 %collective-permute-start.2 = (f32[4,25,4,128]{3,2,1,0:T(4,128)S(1)}, f32[4,25,4,128]{3,2,1,0:T(4,128)S(1)}, u32[]{:S(2)}, u32[]{:S(2)}) collective-permute-start(f32[4,25,4,128]{3,2,1,0:T(4,128)S(1)} %all_to_all.15.own_ref), channel_id=1, source_target_pairs={{0,64},{64,128},{128,192},{192,256},{256,320},{320,384},{384,448},... | collective-permute-start | bytes 614408 | tf_op jit(solution)/shard_map/ppermute | solution.py:558
  33.3 1.9 %collective-permute-start.4 = (f32[10,4,128]{2,1,0:T(4,128)S(1)}, f32[10,4,128]{2,1,0:T(4,128)S(1)}, u32[]{:S(2)}, u32[]{:S(2)}) collective-permute-start(f32[10,4,128]{2,1,0:T(4,128)S(1)} %get-tuple-element.10), channel_id=1, source_target_pairs={{0,128},{64,192},{128,256},{192,320},{256,384},{320,448},{384,512}... | collective-permute-start | bytes 61448 | tf_op jit(solution)/shard_map/ppermute | solution.py:558
  35.3 5.5 %collective-permute-start.5 = (f32[10,4,128]{2,1,0:T(4,128)S(1)}, f32[10,4,128]{2,1,0:T(4,128)S(1)}, u32[]{:S(2)}, u32[]{:S(2)}) collective-permute-start(f32[10,4,128]{2,1,0:T(4,128)S(1)} %get-tuple-element.11), channel_id=1, source_target_pairs={{0,640},{64,704},{128,0},{192,64},{256,128},{320,192},{384,256},{4... | collective-permute-start | bytes 61448 | tf_op jit(solution)/shard_map/ppermute | solution.py:558
  40.7 0.1 pad_add_fusion.place_ref
  40.8 0.0 collective-permute-done.4.far_prior_ref
  40.8 0.9 collective-permute-done.5.far_next_ref
  41.7 0.0 collective-permute-done.3.next_ref
  41.7 0.0 collective-permute-done.2.prior_ref
  41.7 0.0 copy-start.6
  41.7 0.0 copy-start.7
  41.7 0.6 copy-done.6
  42.4 0.0 copy-done.7
  42.4 10.0 %shard_map.97 = (f32[5,4,4,128]{3,2,1,0:T(4,128)S(1)}, f32[16,3,8,128]{3,2,1,0:T(8,128)S(1)}) custom-call(s32[2]{0:T(128)S(1)} %pad_add_fusion.place_ref, s32[32]{0:T(128)S(1)} %bitcast.13, s32[32]{0:T(128)S(1)} %bitcast.16, f32[4,25,4,128]{3,2,1,0:T(4,128)S(1)} %all_to_all.15.own_ref, f32[4,25,4,128]{3,2,1,0:T(4,128)S(1)} %collective-permute-done.2.prior_ref, ...), custom_call_target="tpu_custom_call" | custom-call | tf_op jit(solution)/shard_map/pallas_call | solution.py:575
  52.4 0.0 copy-start.3
  52.4 0.0 copy-start.4
  52.4 0.0 copy-start.5
  52.4 20.7 %all_to_all.16.got_ref = f32[16,3,8,128]{3,2,1,0:T(8,128)S(1)} all-to-all(f32[16,3,8,128]{3,2,1,0:T(8,128)S(1)} %get-tuple-element.13), channel_id=1, replica_groups=mesh['gx'=12,'gy'=4,'gz'=16] {'gz'}, dimensions={0} | all-to-all | bytes 393216 | tf_op jit(solution)/shard_map/all_to_all | solution.py:592
  73.2 0.0 copy-done.3
  73.2 0.0 copy-done.4
  73.2 0.0 copy-done.5
  73.2 2.8 %shard_map.98 = (f32[5,2,8,128]{3,2,1,0:T(8,128)}, f32[16,8,128]{2,1,0:T(8,128)S(1)}) custom-call(s32[2]{0:T(128)S(1)} %pad_add_fusion.place_ref, s32[32]{0:T(128)S(1)} %bitcast.14, f32[16,3,8,128]{3,2,1,0:T(8,128)S(1)} %all_to_all.16.got_ref, f32[2,8,128]{2,1,0:T(8,128)S(1)} %bitcast.11, f32[3,2,8,128]{3,2,1,0:T(8,128)S(1)} %bitcast.10, ...), custom_call_target="tpu_custom_call" | custom-call | tf_op jit(solution)/shard_map/pallas_call | solution.py:593
  76.0 10.5 %all_to_all.17.got_ref = f32[16,8,128]{2,1,0:T(8,128)S(1)} all-to-all(f32[16,8,128]{2,1,0:T(8,128)S(1)} %get-tuple-element.14), channel_id=1, replica_groups=mesh['gx'=12,'gy'=4,'gz'=16] {'gz'}, dimensions={0} | all-to-all | bytes 131072 | tf_op jit(solution)/shard_map/all_to_all | solution.py:607
  86.5 1.7 %shard_map.99 = f32[5,4,4,128]{3,2,1,0:T(4,128)} custom-call(s32[2]{0:T(128)S(1)} %pad_add_fusion.place_ref, s32[32]{0:T(128)S(1)} %bitcast.15, s32[32]{0:T(128)S(1)} %bitcast.17, f32[5,4,4,128]{3,2,1,0:T(4,128)S(1)} %get-tuple-element.12.new_ref, f32[16,8,128]{2,1,0:T(8,128)S(1)} %all_to_all.17.got_ref), custom_call_target="tpu_custom_call" | custom-call | tf_op jit(solution)/shard_map/pallas_call | solution.py:608
Async XLA Ops:
  0.6 0.7 copy-start
  1.4 0.7 copy-start.1
  2.1 0.7 copy-start.2
  2.9 11.4 %collective-permute-start.1 = (f32[5,4,128]{2,1,0:T(4,128)S(1)}, f32[5,4,128]{2,1,0:T(4,128)S(1)}, u32[]{:S(2)}, u32[]{:S(2)}) collective-permute-start(f32[5,4,128]{2,1,0:T(4,128)S(1)} %shard_map.95.ends_ref), channel_id=1, source_target_pairs={{0,15},{1,0},{2,1},{3,2},{4,3},{5,4},{6,5},{7,6},{8,7},{9,8},{10,9... | collective-permute-start | bytes 30728 | tf_op jit(solution)/shard_map/ppermute | solution.py:558
  13.4 1.2 %collective-permute-start = (f32[5,4,128]{2,1,0:T(4,128)S(1)}, f32[5,4,128]{2,1,0:T(4,128)S(1)}, u32[]{:S(2)}, u32[]{:S(2)}) collective-permute-start(f32[5,4,128]{2,1,0:T(4,128)S(1)} %shard_map.95.ends_ref), channel_id=1, source_target_pairs={{0,1},{1,2},{2,3},{3,4},{4,5},{5,6},{6,7},{7,8},{8,9},{9,10},{10,1... | collective-permute-start | bytes 30728 | tf_op jit(solution)/shard_map/ppermute | solution.py:558
  22.3 19.4 %collective-permute-start.3 = (f32[4,25,4,128]{3,2,1,0:T(4,128)S(1)}, f32[4,25,4,128]{3,2,1,0:T(4,128)S(1)}, u32[]{:S(2)}, u32[]{:S(2)}) collective-permute-start(f32[4,25,4,128]{3,2,1,0:T(4,128)S(1)} %all_to_all.15.own_ref), channel_id=1, source_target_pairs={{0,704},{64,0},{128,64},{192,128},{256,192},{320,256},{384,320},{4... | collective-permute-start | bytes 614408 | tf_op jit(solution)/shard_map/ppermute | solution.py:558
  31.4 10.3 %collective-permute-start.2 = (f32[4,25,4,128]{3,2,1,0:T(4,128)S(1)}, f32[4,25,4,128]{3,2,1,0:T(4,128)S(1)}, u32[]{:S(2)}, u32[]{:S(2)}) collective-permute-start(f32[4,25,4,128]{3,2,1,0:T(4,128)S(1)} %all_to_all.15.own_ref), channel_id=1, source_target_pairs={{0,64},{64,128},{128,192},{192,256},{256,320},{320,384},{384,448},... | collective-permute-start | bytes 614408 | tf_op jit(solution)/shard_map/ppermute | solution.py:558
  33.3 7.5 %collective-permute-start.4 = (f32[10,4,128]{2,1,0:T(4,128)S(1)}, f32[10,4,128]{2,1,0:T(4,128)S(1)}, u32[]{:S(2)}, u32[]{:S(2)}) collective-permute-start(f32[10,4,128]{2,1,0:T(4,128)S(1)} %get-tuple-element.10), channel_id=1, source_target_pairs={{0,128},{64,192},{128,256},{192,320},{256,384},{320,448},{384,512}... | collective-permute-start | bytes 61448 | tf_op jit(solution)/shard_map/ppermute | solution.py:558
  35.3 6.4 %collective-permute-start.5 = (f32[10,4,128]{2,1,0:T(4,128)S(1)}, f32[10,4,128]{2,1,0:T(4,128)S(1)}, u32[]{:S(2)}, u32[]{:S(2)}) collective-permute-start(f32[10,4,128]{2,1,0:T(4,128)S(1)} %get-tuple-element.11), channel_id=1, source_target_pairs={{0,640},{64,704},{128,0},{192,64},{256,128},{320,192},{384,256},{4... | collective-permute-start | bytes 61448 | tf_op jit(solution)/shard_map/ppermute | solution.py:558
  41.7 0.7 copy-start.6
  41.7 0.7 copy-start.7
  52.4 20.8 %copy-start.3 = (f32[3,1,1,2,8,128]{5,4,3,2,1,0:T(8,128)S(1)}, f32[3,1,1,2,8,128]{5,4,3,2,1,0:T(8,128)}, u32[]{:S(2)}) copy-start(f32[3,1,1,2,8,128]{5,4,3,2,1,0:T(8,128)} %param.12) | copy-start | bytes 73732
  52.4 20.8 %copy-start.4 = (f32[1,1,2,8,128]{4,3,2,1,0:T(8,128)S(1)}, f32[1,1,2,8,128]{4,3,2,1,0:T(8,128)}, u32[]{:S(2)}) copy-start(f32[1,1,2,8,128]{4,3,2,1,0:T(8,128)} %param.11) | copy-start | bytes 24580
  52.4 20.8 %copy-start.5 = (f32[1,1,2,8,128]{4,3,2,1,0:T(8,128)S(1)}, f32[1,1,2,8,128]{4,3,2,1,0:T(8,128)}, u32[]{:S(2)}) copy-start(f32[1,1,2,8,128]{4,3,2,1,0:T(8,128)} %param.13) | copy-start | bytes 24580
where the time goes:
time: 88.7 us; the launch traced here: 88.1 us
  blocking collectives  38.8 us (44%)
  starting transfers between devices  29 us (33%)
  Pallas kernels  14.7 us (17%)
  local copies, waits for them, and re-layouts  2.81 us (3%)
  waiting for transfers between devices  2.06 us (2%)
    ppermute x6, starting transfers between devices, shifted(): lax.ppermute(value, axis, [(i, (i + step) % size) for i in range(size)])  29 us
    all_to_all x1, blocking collectives, on_device(): got = lax.all_to_all(message, 'gz', 0, 0, tiled=True)  20.7 us
    all_to_all x1, blocking collectives, on_device(): incoming = lax.all_to_all(means, 'gz', 0, 0, tiled=True)  10.5 us
    pallas_call x1, Pallas kernels, on_device(): call(coarse_kernel, (shape(5, 4, 4, 128), shape(16, TILES, 8, 128)), 3, 5...  10 us
    all_to_all x1, blocking collectives, on_device(): own = lax.all_to_all(block, 'gy', 0, 0, tiled=True)  7.59 us
    pallas_call x1, Pallas kernels, on_device(): call(fine_kernel, (shape(5, 2, 8, 128), shape(16, 8, 128)), 2, 4, ((2, 30...  2.83 us
    unnamed x16, local copies, waits for them, and re-layouts  2.81 us
    ppermute x6, waiting for transfers between devices, shifted(): lax.ppermute(value, axis, [(i, (i + step) % size) for i in range(size)])  2.06 us
  transfers between devices with their start and end apart: 6, of which 3 were waited for; matrix products, arithmetic and copies ran while one was open for 0% of the time, Pallas kernels for 0%

commit v1 on v0

--- a/solution.py
+++ b/solution.py
@@ -10,6 +10,8 @@
 PER_ROW = 12
 OLD = 20
 TILES = 3
+FIRST, SECOND = 2, 3
+SENDS, ADDS = 8, 16
 
 
 def iota(dim, shape=(8, 128)):
@@ -131,12 +133,28 @@
     }
 
 
-def ends_kernel(rho_ref, vel_ref, p_ref, out_ref):
+def ends_kernel(
+    rho_hbm, vel_hbm, p_hbm, parent_hbm, shift_hbm, out_ref, main_ref, parent_ref, shift_ref,
+    rho_ref, vel_ref, p_ref, done,
+):
+    pairs = (
+        (rho_hbm, rho_ref),
+        (vel_hbm, vel_ref),
+        (p_hbm, p_ref),
+        (parent_hbm, parent_ref),
+        (shift_hbm, shift_ref),
+    )
+    copies = [pltpu.make_async_copy(a, b, done.at[k]) for k, (a, b) in enumerate(pairs)]
+    for copy in copies:
+        copy.start()
+    for copy in copies:
+        copy.wait()
     lane = iota(1, (4, 128))
     for f in range(5):
         total = None
         for x in range(4):
             row = rho_ref[x] if f == 0 else (p_ref[x] if f == 4 else vel_ref[f - 1, x])
+            main_ref[5 * x + f] = row
             part = lane - 32 * x
             first = roll(row, 32 * x + 8, 1)
             last = roll(row, 32 * x + 24, 1)
@@ -145,8 +163,12 @@
         out_ref[f] = total
 
 
-def block_kernel(ends_ref, before_ref, after_ref, rho_ref, vel_ref, p_ref, out_ref, up_ref, down_ref):
+def block_kernel(ends_ref, before_ref, after_ref, main_ref, out_ref, up_ref, down_ref):
     lane = iota(1, (4, 128)) % 32
+    for copy in range(4):
+        out_ref[copy, 0:20] = main_ref[...]
+    up_ref[0:5] = main_ref[15:20]
+    down_ref[0:5] = main_ref[0:5]
     for f in range(5):
         edge = jnp.where(
             lane < 8,
@@ -157,14 +179,6 @@
             out_ref[copy, 20 + f] = edge
         up_ref[5 + f] = edge
         down_ref[5 + f] = edge
-        for x in range(4):
-            row = rho_ref[x] if f == 0 else (p_ref[x] if f == 4 else vel_ref[f - 1, x])
-            for copy in range(4):
-                out_ref[copy, 5 * x + f] = row
-            if x == 3:
-                up_ref[f] = row
-            if x == 0:
-                down_ref[f] = row
 
 
 def coarse_kernel(
@@ -198,25 +212,35 @@
     def section_row(x, rows=16):
         return [section_ref[5 * (x + 3) + f, 0:rows] for f in range(5)]
 
-    low = flux = high_prior = None
-    for x in range(-4, 8):
-        here = prim_row(x)
-        pairs = [edges(b, h, a) for b, h, a in zip(prim_row(x - 1), here, prim_row(x + 1))]
-        low = [pair[1] for pair in pairs]
-        if high_prior is not None:
-            flux_next = hllc(high_prior, low, 0)
-            if flux is not None:
-                middle = prim_row(x - 1)
-                by_y = line_change(middle, 0, 1)
-                by_z = line_change(middle, 1, 2)
-                state = conserved(middle)
-                section = [
-                    state[f] - 0.05 * (flux_next[f] - flux[f] + by_y[f] + by_z[f]) for f in range(5)
-                ]
-                for f, value in enumerate(primitive(section)):
-                    section_ref[5 * (x - 1 + 3) + f] = value
-            flux = flux_next
-        high_prior = [pair[0] for pair in pairs]
+    def sweep(row, start, rows, at_once, emit):
+        def pairs_of(x):
+            found = [edges(b, h, a) for b, h, a in zip(row(x - 1), row(x), row(x + 1))]
+            return [pair[0] for pair in found], [pair[1] for pair in found]
+
+        def step(i, carry):
+            high, flux = carry
+            for k in range(at_once):
+                x = start + i * at_once + k
+                high_next, low = pairs_of(x + 1)
+                flux_next = hllc(high, low, 0)
+                emit(x, [after - before for before, after in zip(flux, flux_next)])
+                high, flux = high_next, flux_next
+            return high, flux
+
+        high_before, _ = pairs_of(start - 1)
+        high, low = pairs_of(start)
+        lax.fori_loop(0, rows // at_once, step, (high, hllc(high_before, low, 0)))
+
+    def section_of(x, by_x):
+        middle = prim_row(x)
+        by_y = line_change(middle, 0, 1)
+        by_z = line_change(middle, 1, 2)
+        state = conserved(middle)
+        section = [state[f] - 0.05 * (by_x[f] + by_y[f] + by_z[f]) for f in range(5)]
+        for f, value in enumerate(primitive(section)):
+            section_ref[5 * (x + 3) + f] = value
+
+    sweep(prim_row, -3, 10, FIRST, section_of)
     tiles = [[edge_ref[5 * t + f] for f in range(5)] for t in range(5)]
     by_x = group_changes(tiles, (1, 2, 3))
     for t in (1, 2, 3):
@@ -234,25 +258,15 @@
             for f in range(5)
         ]
 
-    flux = high_prior = None
-    for x in range(-2, 6):
-        here = section_row(x, 8)
-        pairs = [
-            edges(b, h, a) for b, h, a in zip(section_row(x - 1, 8), here, section_row(x + 1, 8))
-        ]
-        low = [pair[1] for pair in pairs]
-        if high_prior is not None:
-            flux_next = hllc(high_prior, low, 0)
-            if flux is not None:
-                middle = section_row(x - 1, 8)
-                by_y = line_change(middle, 0, 1, section_row(x - 1))
-                by_z = line_change(middle, 1, 2)
-                old = [part[0:8] for part in prim_row(x - 1)]
-                by_x_row = [b - a for a, b in zip(flux, flux_next)]
-                for f, value in enumerate(advance(old, middle, (by_x_row, by_y, by_z))):
-                    made_ref[5 * x + f] = value
-            flux = flux_next
-        high_prior = [pair[0] for pair in pairs]
+    def updated_of(x, by_x):
+        middle = section_row(x, 8)
+        by_y = line_change(middle, 0, 1, section_row(x))
+        by_z = line_change(middle, 1, 2)
+        old = [part[0:8] for part in prim_row(x)]
+        for f, value in enumerate(advance(old, middle, (by_x, by_y, by_z))):
+            made_ref[5 * (x + 1) + f] = value
+
+    sweep(lambda x: section_row(x, 8), -1, 6, SECOND, updated_of)
     wide = [[section_edge_ref[5 * t + f] for f in range(5)] for t in range(3)]
     tiles = [[part[0:8] for part in tile] for tile in wide]
     by_x = group_changes(tiles, (0, 1, 2))
@@ -309,13 +323,11 @@
                     jnp.where(sub < 2, roll(news[far][kind], -2, 0), roll(news[far][kind], 2, 0)),
                 )
 
-    def send(owner, carry):
-        hit = parent_ref[2 * owner] == gz
-        other = parent_ref[2 * owner + 1] == gz
-        shift = jnp.where(hit, shift_ref[2 * owner], shift_ref[2 * owner + 1])
-
-        @pl.when(hit | other)
-        def _():
+    def send(turn, carry):
+        for k_owner in range(SENDS):
+            owner = SENDS * turn + k_owner
+            hit = parent_ref[2 * owner] == gz
+            shift = jnp.where(hit, shift_ref[2 * owner], shift_ref[2 * owner + 1])
             kind = jnp.where(shift == 0, 1, jnp.where(shift == 120, 2, 0))
             for tile in range(TILES):
                 total = None
@@ -334,14 +346,14 @@
                         )
                     total = piece if total is None else jnp.where(lane < GROUP * j, total, piece)
                 message_ref[owner, tile] = total
-
         return carry
 
-    lax.fori_loop(0, 16, send, 0)
+    lax.fori_loop(0, 16 // SENDS, send, 0)
 
 
 def fine_kernel(
-    place_ref, parent_ref, got_ref, rho_ref, vel_ref, p_ref, out_ref, message_ref, mid_ref, tip_ref
+    place_ref, parent_ref, got_ref, rho_ref, vel_ref, p_ref, out_ref, message_ref,
+    mid_ref, tip_ref, ghost_ref, bound_ref,
 ):
     gz = place_ref[1]
     lane, sub = iota(1), iota(0)
@@ -354,12 +366,12 @@
             j = k % PER_ROW
             tile = got_ref[parents[box], k // PER_ROW]
             at = GROUP * j + 1 + part // 2
-            mid_ref[box, k] = jnp.take_along_axis(tile, at, axis=1)
+            mid_ref[box, 8 * k : 8 * k + 8] = jnp.take_along_axis(tile, at, axis=1)
             at = GROUP * j + jnp.where(part < 8, 0, 9)
-            tip_ref[box, k] = jnp.take_along_axis(tile, at, axis=1)
-
-    def row(ref, box, k, s):
-        return jnp.broadcast_to(ref[box, k, s : s + 1, :], (8, 128))
+            tip_ref[box, 8 * k : 8 * k + 8] = jnp.take_along_axis(tile, at, axis=1)
+
+    def every(ref, box, k, row, step=1):
+        return ref[box, pl.ds(8 * k + row, 8, stride=8 * step)]
 
     def by_y(items):
         return jnp.where(
@@ -368,41 +380,46 @@
             jnp.where(yc == 2, items[2], items[3]),
         )
 
-    def by_x(items):
-        return jnp.where(
-            xc < 2,
-            jnp.where(xc == 0, items[0], items[1]),
-            jnp.where(xc == 2, items[2], items[3]),
-        )
-
-    def inside(box, f):
-        return by_x([by_y([row(mid_ref, box, 4 * f + x, 2 + y) for y in range(4)]) for x in range(4)])
-
-    def old_ghosts(box, f):
-        low = by_y([row(mid_ref, box, 4 * f + y // 2, 7 * (y % 2)) for y in range(4)])
-        high = by_y([row(mid_ref, box, 4 * f + 2 + y // 2, 7 * (y % 2)) for y in range(4)])
-        along_x = jnp.where(sub < 4, low, high)
-        low = by_x([row(mid_ref, box, 4 * f + x, 1) for x in range(4)])
-        high = by_x([row(mid_ref, box, 4 * f + x, 6) for x in range(4)])
-        along_y = jnp.where(lane < 64, low, high)
-        along_z = by_x(
-            [by_y([row(tip_ref, box, 4 * f + x, 2 + y) for y in range(4)]) for x in range(4)]
-        )
-        return along_x, along_y, along_z
-
-    def new_ghosts(box, f):
-        k = OLD + 2 * f
-        low = by_y([row(mid_ref, box, k, 2 + y) for y in range(4)])
-        high = by_y([row(mid_ref, box, k + 1, 2 + y) for y in range(4)])
-        along_x = jnp.where(sub < 4, low, high)
-        spots = ((k, 1, 6), (k, 0, 7), (k + 1, 0, 7), (k + 1, 1, 6))
-        low = by_x([row(mid_ref, box, at, one) for at, one, _ in spots])
-        high = by_x([row(mid_ref, box, at, one) for at, _, one in spots])
-        along_y = jnp.where(lane < 64, low, high)
-        near, far = (2, 3, 4, 5), (0, 1, 6, 7)
-        spots = ((k, near), (k, far), (k + 1, far), (k + 1, near))
-        along_z = by_x([by_y([row(tip_ref, box, at, s) for s in rows]) for at, rows in spots])
-        return along_x, along_y, along_z
+    def spread(value, rows):
+        return jnp.take_along_axis(value, rows, axis=0)
+
+    side, low_y = (sub >= 4).astype(jnp.int32), lane < 64
+    outer_x = (xc == 0) | (xc == 3)
+    half_x = (xc >= 2).astype(jnp.int32)
+
+    def old_parts(box):
+        inside, along_x, along_y, along_z = [], [], [], []
+        for f in range(5):
+            if f % 2 == 0:
+                middle = by_y([every(mid_ref, box, 4 * f, 2 + y) for y in range(4)])
+                sides = jnp.where(low_y, every(mid_ref, box, 4 * f, 1), every(mid_ref, box, 4 * f, 6))
+                tips = by_y([every(tip_ref, box, 4 * f, 2 + y) for y in range(4)])
+            if f % 4 == 0:
+                faces = by_y(
+                    [every(mid_ref, box, 4 * f + y // 2, 7 * (y % 2), 2) for y in range(4)]
+                )
+            at = 4 * (f % 2) + xc
+            inside.append(spread(middle, at))
+            along_y.append(spread(sides, at))
+            along_z.append(spread(tips, at))
+            along_x.append(spread(faces, 2 * (f % 4) + side))
+        return inside, [along_x, along_y, along_z]
+
+    def new_parts(box):
+        along_x, along_y, along_z = [], [], []
+        for f in range(5):
+            if f % 4 == 0:
+                k = OLD + 2 * f
+                faces = by_y([every(mid_ref, box, k, 2 + y) for y in range(4)])
+                sides_near = jnp.where(low_y, every(mid_ref, box, k, 1), every(mid_ref, box, k, 6))
+                sides_far = jnp.where(low_y, every(mid_ref, box, k, 0), every(mid_ref, box, k, 7))
+                tips_near = by_y([every(tip_ref, box, k, 2 + y) for y in range(4)])
+                tips_far = by_y([every(tip_ref, box, k, row) for row in (0, 1, 6, 7)])
+            at = 2 * (f % 4) + half_x
+            along_x.append(spread(faces, 2 * (f % 4) + side))
+            along_y.append(jnp.where(outer_x, spread(sides_near, at), spread(sides_far, at)))
+            along_z.append(jnp.where(outer_x, spread(tips_near, at), spread(tips_far, at)))
+        return [along_x, along_y, along_z]
 
     directions = (
         (0, 1, sub == 0, sub == 7, 4, sub >= 4),
@@ -410,13 +427,13 @@
         (1, 1, part == 0, part == 15, 8, part >= 8),
     )
 
-    def changes(fields, ghosts, bounds):
+    def changes(fields, step_index):
         total = None
         for normal, (axis, step, first, last, park, parked) in enumerate(directions):
             high, low, up = [[], []], [[], []], [[], []]
             for box in range(2):
                 for f in range(5):
-                    here, ghost = fields[box][f], ghosts[box][normal][f]
+                    here, ghost = fields[box][f], ghost_ref[step_index, box, normal, f]
                     after = jnp.where(last, ghost, roll(here, -step, axis))
                     before = jnp.where(first, ghost, roll(here, step, axis))
                     one, other = edges(before, here, after)
@@ -424,7 +441,7 @@
                     low[box].append(other)
                     up[box].append(jnp.where(last, ghost, roll(other, -step, axis)))
             right = [jnp.where(parked, roll(b, park, axis), a) for a, b in zip(low[0], low[1])]
-            bottom = hllc(bounds[normal], right, normal)
+            bottom = hllc([bound_ref[step_index, normal, f] for f in range(5)], right, normal)
             found = []
             for box in range(2):
                 flux = hllc(high[box], up[box], normal)
@@ -439,50 +456,42 @@
             )
         return total
 
-    def lower_bounds(ghosts):
-        return [
-            [
-                jnp.where(parked, roll(ghosts[1][normal][f], park, axis), ghosts[0][normal][f])
-                for f in range(5)
-            ]
-            for normal, (axis, _, _, _, park, parked) in enumerate(directions)
-        ]
-
-    def substep(states, fields, ghosts):
-        bounds = lower_bounds(ghosts)
-        moved = changes(fields, ghosts, bounds)
-        section = [[s - 0.05 * m for s, m in zip(states[b], moved[b])] for b in range(2)]
-        moved = changes([primitive(item) for item in section], ghosts, bounds)
-        return [
-            [
-                0.5 * s + 0.5 * (t - 0.05 * m)
-                for s, t, m in zip(states[b], section[b], moved[b])
-            ]
-            for b in range(2)
-        ]
-
-    ghosts, fields = [], []
+    def keep(step_index, ghosts):
+        for normal, (axis, _, _, _, park, parked) in enumerate(directions):
+            for f in range(5):
+                for box in range(2):
+                    ghost_ref[step_index, box, normal, f] = ghosts[box][normal][f]
+                bound_ref[step_index, normal, f] = jnp.where(
+                    parked, roll(ghosts[1][normal][f], park, axis), ghosts[0][normal][f]
+                )
+
+    ghosts, states, later = [], [], []
     for box in range(2):
-        found = [old_ghosts(box, f) for f in range(5)]
-        ghosts.append([[found[f][d] for f in range(5)] for d in range(3)])
+        inside, found = old_parts(box)
+        ghosts.append(found)
         details = [rho_ref[box], vel_ref[0, box], vel_ref[1, box], vel_ref[2, box], p_ref[box]]
-        fields.append([inside(box, f) + details[f] for f in range(5)])
-    states = substep([conserved(item) for item in fields], fields, ghosts)
-    later = []
-    for box in range(2):
-        found = [new_ghosts(box, f) for f in range(5)]
+        states.append(conserved([a + b for a, b in zip(inside, details)]))
         later.append(
             [
-                primitive(
-                    [
-                        0.5 * (a + b)
-                        for a, b in zip(conserved(ghosts[box][d]), [found[f][d] for f in range(5)])
-                    ]
-                )
-                for d in range(3)
+                primitive([0.5 * (a + b) for a, b in zip(conserved(old), new)])
+                for old, new in zip(found, new_parts(box))
             ]
         )
-    states = substep(states, [primitive(item) for item in states], later)
+    keep(0, ghosts)
+    keep(1, later)
+
+    def stage(i, carry):
+        start, state = carry
+        again = lax.rem(i, 2) == 1
+        weight = jnp.where(again, 0.5, 1.0).astype(F32)
+        start = jax.tree.map(lambda a, b: jnp.where(again, a, b), start, state)
+        moved = changes([primitive(item) for item in state], i // 2)
+        state = jax.tree.map(
+            lambda s, t, m: (1.0 - weight) * s + weight * (t - 0.05 * m), start, state, moved
+        )
+        return start, state
+
+    _, states = lax.fori_loop(0, 4, stage, (states, states), unroll=4)
     for box in range(2):
         packed = None
         for f in range(5):
@@ -507,26 +516,26 @@
     gz = place_ref[1]
     lane = iota(1)
 
-    def add(owner, carry):
-        hit = parent_ref[2 * owner] == gz
-        other = parent_ref[2 * owner + 1] == gz
-        shift = jnp.where(hit, shift_ref[2 * owner], shift_ref[2 * owner + 1])
-
-        def covered(carry):
-            count, sums = carry
+    def add(turn, carry):
+        count, sums = carry
+        for k_owner in range(ADDS):
+            owner = ADDS * turn + k_owner
+            hit = parent_ref[2 * owner] == gz
+            other = parent_ref[2 * owner + 1] == gz
+            shift = jnp.where(hit, shift_ref[2 * owner], shift_ref[2 * owner + 1])
+            shift = jnp.where(hit | other, shift, 256)
             inside = (lane >= shift) & (lane < shift + 8)
             value = got_ref[owner]
-            parts = [
+            count = count + jnp.where(inside, 1.0, 0.0)
+            sums = [
                 item
                 + jnp.where(inside, pltpu.roll(value, lax.rem(shift + 128 - 8 * k, 128), 1), 0.0)
                 for k, item in enumerate(sums)
             ]
-            return count + jnp.where(inside, 1.0, 0.0), parts
-
-        return lax.cond(hit | other, covered, lambda same: same, carry)
+        return count, sums
 
     zero = jnp.zeros((8, 128), F32)
-    count, sums = lax.fori_loop(0, 16, add, (zero, [zero] * 16))
+    count, sums = lax.fori_loop(0, 16 // ADDS, add, (zero, [zero] * 16))
     share = inverse(jnp.maximum(count, 1.0))
     for k in range(16):
         sum_ref[8 * k : 8 * k + 8] = sums[k] * share
@@ -535,6 +544,9 @@
             start = (0 if f == 4 else 32 * f) + 2 * x + (1 if f == 4 else 0)
             value = sum_ref[pl.ds(start, 4, stride=8)]
             out_ref[f, x] = jnp.where(count[0:4] > 0.0, value, new_ref[f, x])
+
+
+FINE_SCRATCH = ((2, 352, 128), (2, 352, 128), (2, 2, 3, 5, 8, 128), (2, 3, 5, 8, 128))
 
 
 def shape(*dims):
@@ -563,12 +575,24 @@
 ):
     assert density.shape == (4, 4, 128) and fine_density.shape == (1, 1, 2, 8, 128)
     place = jnp.stack([lax.axis_index("gy"), lax.axis_index("gz")]).astype(jnp.int32)
-    parents, shifts = box_parent.reshape(32), box_shift.reshape(32)
-    ends = call(ends_kernel, shape(5, 4, 128), 0, 3)(density, velocity, pressure)
+    table = jax.ShapeDtypeStruct((32,), jnp.int32)
+    ends, main, parents, shifts = pl.pallas_call(
+        ends_kernel,
+        out_shape=(shape(5, 4, 128), shape(20, 4, 128), table, table),
+        in_specs=[pl.BlockSpec(memory_space=pltpu.HBM)] * 5,
+        out_specs=(pl.BlockSpec(memory_space=pltpu.VMEM),) * 4,
+        scratch_shapes=[
+            pltpu.VMEM((4, 4, 128), F32),
+            pltpu.VMEM((3, 4, 4, 128), F32),
+            pltpu.VMEM((4, 4, 128), F32),
+            pltpu.SemaphoreType.DMA((5,)),
+        ],
+        compiler_params=pltpu.CompilerParams(vmem_limit_bytes=56 * 1024 * 1024),
+    )(density, velocity, pressure, box_parent.reshape(32), box_shift.reshape(32))
     before, after = shifted(ends, "gz", 1), shifted(ends, "gz", -1)
     block, for_up, for_down = call(
-        block_kernel, (shape(4, 25, 4, 128), shape(10, 4, 128), shape(10, 4, 128)), 0, 6
-    )(ends, before, after, density, velocity, pressure)
+        block_kernel, (shape(4, 25, 4, 128), shape(10, 4, 128), shape(10, 4, 128)), 0, 4
+    )(ends, before, after, main)
     far_prior, far_next = shifted(for_up, "gx", 2), shifted(for_down, "gx", -2)
     own = lax.all_to_all(block, "gy", 0, 0, tiled=True)
     prior, following = shifted(own, "gx", 1), shifted(own, "gx", -1)
@@ -595,7 +619,7 @@
         (shape(5, 2, 8, 128), shape(16, 8, 128)),
         2,
         4,
-        ((2, 30, 8, 128), (2, 30, 8, 128)),
+        FINE_SCRATCH,
     )(
         place,
         parents,

time: 88.7 us -> 85.5 us (0.964)
  Pallas kernels: 14.7 us -> 11.8 us
    pallas_call x1, Pallas kernels: 10 us -> 5.6 us  [on_device(): call(coarse_kernel, (shape(5, 4, 4, 128), shape(16, TILES, 8, 128)), 3, 5...]
    pallas_call x2, Pallas kernels: 2.94 us -> 4.27 us  [the longest x1 2.75 us: on_device(): call(fine_kernel, (shape(5, 2, 8, 128), shape(16, 8, 128)), 2, 4, FINE_SC...]
    unnamed x16 -> x14, local copies, waits for them, and re-layouts: 2.81 us -> 2.12 us
where the time goes in v1:
time: 85.5 us; the launch traced here: 85 us
  blocking collectives  39 us (46%)
  starting transfers between devices  29 us (34%)
  Pallas kernels  11.8 us (14%)
  waiting for transfers between devices  2.27 us (3%)
  local copies, waits for them, and re-layouts  2.12 us (2%)
    ppermute x6, starting transfers between devices, shifted(): lax.ppermute(value, axis, [(i, (i + step) % size) for i in range(size)])  29 us
    all_to_all x1, blocking collectives, on_device(): got = lax.all_to_all(message, 'gz', 0, 0, tiled=True)  21 us
    all_to_all x1, blocking collectives, on_device(): incoming = lax.all_to_all(means, 'gz', 0, 0, tiled=True)  10.5 us
    all_to_all x1, blocking collectives, on_device(): own = lax.all_to_all(block, 'gy', 0, 0, tiled=True)  7.59 us
    pallas_call x1, Pallas kernels, on_device(): call(coarse_kernel, (shape(5, 4, 4, 128), shape(16, TILES, 8, 128)), 3, 5...  5.6 us
    pallas_call x1, Pallas kernels, on_device(): call(fine_kernel, (shape(5, 2, 8, 128), shape(16, 8, 128)), 2, 4, FINE_SC...  2.75 us
    ppermute x6, waiting for transfers between devices, shifted(): lax.ppermute(value, axis, [(i, (i + step) % size) for i in range(size)])  2.27 us
    unnamed x14, local copies, waits for them, and re-layouts  2.12 us
  transfers between devices with their start and end apart: 6, of which 3 were waited for; matrix products, arithmetic and copies ran while one was open for 0% of the time, Pallas kernels for 0%

profile of v1, /device:TPU:1, one launch (start us, length us, event | category | flops | bytes accessed | tf_op | source)
XLA Modules:
  0.0 85.0 jit_solution(14609937918184025642)
XLA Ops:
  0.6 1.5 %shard_map.95 = (f32[5,4,128]{2,1,0:T(4,128)}, f32[20,4,128]{2,1,0:T(4,128)}, s32[32]{0:T(128)}, s32[32]{0:T(128)}) custom-call(f32[4,4,128]{2,1,0:T(4,128)} %rho_hbm.1, f32[3,4,4,128]{3,2,1,0:T(4,128)} %vel_hbm.1, f32[4,4,128]{2,1,0:T(4,128)} %p_hbm.1, s32[32]{0:T(128)} %bitcast.13, s32[32]{0:T(128)} %bitcast.14), custom_call_target="tpu_custom_call" | custom-call | tf_op jit(solution)/shard_map/pallas_call | solution.py:579
  2.2 10.5 %collective-permute-start.1 = (f32[5,4,128]{2,1,0:T(4,128)}, f32[5,4,128]{2,1,0:T(4,128)S(1)}, u32[]{:S(2)}, u32[]{:S(2)}) collective-permute-start(f32[5,4,128]{2,1,0:T(4,128)} %get-tuple-element.15.ends_ref), channel_id=1, source_target_pairs={{0,15},{1,0},{2,1},{3,2},{4,3},{5,4},{6,5},{7,6},{8,7},{9,8},{10,9... | collective-permute-start | bytes 30728 | tf_op jit(solution)/shard_map/ppermute | solution.py:570
  12.7 0.0 collective-permute-start
  12.7 1.0 %collective-permute-done.1.after_ref = f32[5,4,128]{2,1,0:T(4,128)S(1)} collective-permute-done((f32[5,4,128]{2,1,0:T(4,128)}, f32[5,4,128]{2,1,0:T(4,128)S(1)}, u32[]{:S(2)}, u32[]{:S(2)}) %collective-permute-start.1) | collective-permute-done | bytes 10272 | tf_op jit(solution)/shard_map/ppermute | solution.py:570
  13.7 0.3 collective-permute-done.before_ref
  14.1 0.0 copy-start
  14.1 0.8 copy-done
  14.9 0.0 copy-start.2
  14.9 0.7 copy-done.2
  15.6 0.1 shard_map.96
  15.6 7.6 %all_to_all.15.own_ref = f32[4,25,4,128]{3,2,1,0:T(4,128)S(1)} all-to-all(f32[4,25,4,128]{3,2,1,0:T(4,128)S(1)} %get-tuple-element.17), channel_id=1, replica_groups=mesh['gx'=12,'gy'=4,'gz'=16] {'gy'}, dimensions={0} | all-to-all | bytes 409600 | tf_op jit(solution)/shard_map/all_to_all | solution.py:597
  23.2 9.1 %collective-permute-start.3 = (f32[4,25,4,128]{3,2,1,0:T(4,128)S(1)}, f32[4,25,4,128]{3,2,1,0:T(4,128)S(1)}, u32[]{:S(2)}, u32[]{:S(2)}) collective-permute-start(f32[4,25,4,128]{3,2,1,0:T(4,128)S(1)} %all_to_all.15.own_ref), channel_id=1, source_target_pairs={{0,704},{64,0},{128,64},{192,128},{256,192},{320,256},{384,320},{4... | collective-permute-start | bytes 614408 | tf_op jit(solution)/shard_map/ppermute | solution.py:570
  32.4 1.9 %collective-permute-start.2 = (f32[4,25,4,128]{3,2,1,0:T(4,128)S(1)}, f32[4,25,4,128]{3,2,1,0:T(4,128)S(1)}, u32[]{:S(2)}, u32[]{:S(2)}) collective-permute-start(f32[4,25,4,128]{3,2,1,0:T(4,128)S(1)} %all_to_all.15.own_ref), channel_id=1, source_target_pairs={{0,64},{64,128},{128,192},{192,256},{256,320},{320,384},{384,448},... | collective-permute-start | bytes 614408 | tf_op jit(solution)/shard_map/ppermute | solution.py:570
  34.3 1.9 %collective-permute-start.4 = (f32[10,4,128]{2,1,0:T(4,128)S(1)}, f32[10,4,128]{2,1,0:T(4,128)S(1)}, u32[]{:S(2)}, u32[]{:S(2)}) collective-permute-start(f32[10,4,128]{2,1,0:T(4,128)S(1)} %get-tuple-element.18), channel_id=1, source_target_pairs={{0,128},{64,192},{128,256},{192,320},{256,384},{320,448},{384,512}... | collective-permute-start | bytes 61448 | tf_op jit(solution)/shard_map/ppermute | solution.py:570
  36.2 5.5 %collective-permute-start.5 = (f32[10,4,128]{2,1,0:T(4,128)S(1)}, f32[10,4,128]{2,1,0:T(4,128)S(1)}, u32[]{:S(2)}, u32[]{:S(2)}) collective-permute-start(f32[10,4,128]{2,1,0:T(4,128)S(1)} %get-tuple-element.19), channel_id=1, source_target_pairs={{0,640},{64,704},{128,0},{192,64},{256,128},{320,192},{384,256},{4... | collective-permute-start | bytes 61448 | tf_op jit(solution)/shard_map/ppermute | solution.py:570
  41.7 0.1 pad_add_fusion.place_ref
  41.8 0.0 collective-permute-done.4.far_prior_ref
  41.8 0.9 %collective-permute-done.5.far_next_ref = f32[10,4,128]{2,1,0:T(4,128)S(1)} collective-permute-done((f32[10,4,128]{2,1,0:T(4,128)S(1)}, f32[10,4,128]{2,1,0:T(4,128)S(1)}, u32[]{:S(2)}, u32[]{:S(2)}) %collective-permute-start.5) | collective-permute-done | bytes 20512 | tf_op jit(solution)/shard_map/ppermute | solution.py:570
  42.7 0.0 collective-permute-done.3.next_ref
  42.7 0.0 collective-permute-done.2.prior_ref
  42.7 0.0 copy-start.5
  42.7 0.0 copy-start.6
  42.7 0.6 copy-done.5
  43.3 0.0 copy-done.6
  43.3 5.6 %shard_map.97 = (f32[5,4,4,128]{3,2,1,0:T(4,128)S(1)}, f32[16,3,8,128]{3,2,1,0:T(8,128)S(1)}) custom-call(s32[2]{0:T(128)S(1)} %pad_add_fusion.place_ref, s32[32]{0:T(128)S(1)} %copy-done.5, s32[32]{0:T(128)S(1)} %copy-done.6, f32[4,25,4,128]{3,2,1,0:T(4,128)S(1)} %all_to_all.15.own_ref, f32[4,25,4,128]{3,2,1,0:T(4,128)S(1)} %collective-permute-done.2.prior_ref, ...), custom_call_target="tpu_custom_call" | custom-call | tf_op jit(solution)/shard_map/pallas_call | solution.py:599
  48.9 0.0 copy-start.1
  48.9 0.0 copy-start.3
  48.9 0.0 copy-start.4
  48.9 21.0 %all_to_all.16.got_ref = f32[16,3,8,128]{3,2,1,0:T(8,128)S(1)} all-to-all(f32[16,3,8,128]{3,2,1,0:T(8,128)S(1)} %get-tuple-element.21), channel_id=1, replica_groups=mesh['gx'=12,'gy'=4,'gz'=16] {'gz'}, dimensions={0} | all-to-all | bytes 393216 | tf_op jit(solution)/shard_map/all_to_all | solution.py:616
  69.9 0.0 copy-done.1
  69.9 0.0 copy-done.3
  69.9 0.0 copy-done.4
  69.9 2.8 %shard_map.98 = (f32[5,2,8,128]{3,2,1,0:T(8,128)}, f32[16,8,128]{2,1,0:T(8,128)S(1)}) custom-call(s32[2]{0:T(128)S(1)} %pad_add_fusion.place_ref, s32[32]{0:T(128)S(1)} %copy-done.5, f32[16,3,8,128]{3,2,1,0:T(8,128)S(1)} %all_to_all.16.got_ref, f32[2,8,128]{2,1,0:T(8,128)S(1)} %bitcast.11, f32[3,2,8,128]{3,2,1,0:T(8,128)S(1)} %bitcast.10, ...), custom_call_target="tpu_custom_call" | custom-call | tf_op jit(solution)/shard_map/pallas_call | solution.py:617
  72.7 10.5 %all_to_all.17.got_ref = f32[16,8,128]{2,1,0:T(8,128)S(1)} all-to-all(f32[16,8,128]{2,1,0:T(8,128)S(1)} %get-tuple-element.22), channel_id=1, replica_groups=mesh['gx'=12,'gy'=4,'gz'=16] {'gz'}, dimensions={0} | all-to-all | bytes 131072 | tf_op jit(solution)/shard_map/all_to_all | solution.py:631
  83.1 1.8 %shard_map.99 = f32[5,4,4,128]{3,2,1,0:T(4,128)} custom-call(s32[2]{0:T(128)S(1)} %pad_add_fusion.place_ref, s32[32]{0:T(128)S(1)} %copy-done.5, s32[32]{0:T(128)S(1)} %copy-done.6, f32[5,4,4,128]{3,2,1,0:T(4,128)S(1)} %get-tuple-element.20.new_ref, f32[16,8,128]{2,1,0:T(8,128)S(1)} %all_to_all.17.got_ref), custom_call_target="tpu_custom_call" | custom-call | tf_op jit(solution)/shard_map/pallas_call | solution.py:632
Async XLA Ops:
  2.2 11.6 %collective-permute-start.1 = (f32[5,4,128]{2,1,0:T(4,128)}, f32[5,4,128]{2,1,0:T(4,128)S(1)}, u32[]{:S(2)}, u32[]{:S(2)}) collective-permute-start(f32[5,4,128]{2,1,0:T(4,128)} %get-tuple-element.15.ends_ref), channel_id=1, source_target_pairs={{0,15},{1,0},{2,1},{3,2},{4,3},{5,4},{6,5},{7,6},{8,7},{9,8},{10,9... | collective-permute-start | bytes 30728 | tf_op jit(solution)/shard_map/ppermute | solution.py:570
  12.7 1.4 %collective-permute-start = (f32[5,4,128]{2,1,0:T(4,128)}, f32[5,4,128]{2,1,0:T(4,128)S(1)}, u32[]{:S(2)}, u32[]{:S(2)}) collective-permute-start(f32[5,4,128]{2,1,0:T(4,128)} %get-tuple-element.15.ends_ref), channel_id=1, source_target_pairs={{0,1},{1,2},{2,3},{3,4},{4,5},{5,6},{6,7},{7,8},{8,9},{9,10},{10,1... | collective-permute-start | bytes 30728 | tf_op jit(solution)/shard_map/ppermute | solution.py:570
  14.1 0.8 copy-start
  14.9 0.7 copy-start.2
  23.2 19.4 %collective-permute-start.3 = (f32[4,25,4,128]{3,2,1,0:T(4,128)S(1)}, f32[4,25,4,128]{3,2,1,0:T(4,128)S(1)}, u32[]{:S(2)}, u32[]{:S(2)}) collective-permute-start(f32[4,25,4,128]{3,2,1,0:T(4,128)S(1)} %all_to_all.15.own_ref), channel_id=1, source_target_pairs={{0,704},{64,0},{128,64},{192,128},{256,192},{320,256},{384,320},{4... | collective-permute-start | bytes 614408 | tf_op jit(solution)/shard_map/ppermute | solution.py:570
  32.4 10.3 %collective-permute-start.2 = (f32[4,25,4,128]{3,2,1,0:T(4,128)S(1)}, f32[4,25,4,128]{3,2,1,0:T(4,128)S(1)}, u32[]{:S(2)}, u32[]{:S(2)}) collective-permute-start(f32[4,25,4,128]{3,2,1,0:T(4,128)S(1)} %all_to_all.15.own_ref), channel_id=1, source_target_pairs={{0,64},{64,128},{128,192},{192,256},{256,320},{320,384},{384,448},... | collective-permute-start | bytes 614408 | tf_op jit(solution)/shard_map/ppermute | solution.py:570
  34.3 7.5 %collective-permute-start.4 = (f32[10,4,128]{2,1,0:T(4,128)S(1)}, f32[10,4,128]{2,1,0:T(4,128)S(1)}, u32[]{:S(2)}, u32[]{:S(2)}) collective-permute-start(f32[10,4,128]{2,1,0:T(4,128)S(1)} %get-tuple-element.18), channel_id=1, source_target_pairs={{0,128},{64,192},{128,256},{192,320},{256,384},{320,448},{384,512}... | collective-permute-start | bytes 61448 | tf_op jit(solution)/shard_map/ppermute | solution.py:570
  36.2 6.4 %collective-permute-start.5 = (f32[10,4,128]{2,1,0:T(4,128)S(1)}, f32[10,4,128]{2,1,0:T(4,128)S(1)}, u32[]{:S(2)}, u32[]{:S(2)}) collective-permute-start(f32[10,4,128]{2,1,0:T(4,128)S(1)} %get-tuple-element.19), channel_id=1, source_target_pairs={{0,640},{64,704},{128,0},{192,64},{256,128},{320,192},{384,256},{4... | collective-permute-start | bytes 61448 | tf_op jit(solution)/shard_map/ppermute | solution.py:570
  42.7 0.6 copy-start.5
  42.7 0.6 copy-start.6
  48.9 21.0 %copy-start.1 = (f32[3,1,1,2,8,128]{5,4,3,2,1,0:T(8,128)S(1)}, f32[3,1,1,2,8,128]{5,4,3,2,1,0:T(8,128)}, u32[]{:S(2)}) copy-start(f32[3,1,1,2,8,128]{5,4,3,2,1,0:T(8,128)} %param.12) | copy-start | bytes 73732
  48.9 21.0 %copy-start.3 = (f32[1,1,2,8,128]{4,3,2,1,0:T(8,128)S(1)}, f32[1,1,2,8,128]{4,3,2,1,0:T(8,128)}, u32[]{:S(2)}) copy-start(f32[1,1,2,8,128]{4,3,2,1,0:T(8,128)} %param.11) | copy-start | bytes 24580
  48.9 21.0 %copy-start.4 = (f32[1,1,2,8,128]{4,3,2,1,0:T(8,128)S(1)}, f32[1,1,2,8,128]{4,3,2,1,0:T(8,128)}, u32[]{:S(2)}) copy-start(f32[1,1,2,8,128]{4,3,2,1,0:T(8,128)} %param.13) | copy-start | bytes 24580

commit v2 on v1

--- a/solution.py
+++ b/solution.py
@@ -16,6 +16,14 @@
 
 def iota(dim, shape=(8, 128)):
     return lax.broadcasted_iota(jnp.int32, shape, dim)
+
+
+class Table:
+    def __init__(self, ref, base):
+        self.ref, self.base = ref, base
+
+    def __getitem__(self, k):
+        return self.ref[self.base + k]
 
 
 def roll(value, shift, axis):
@@ -133,42 +141,25 @@
     }
 
 
-def ends_kernel(
-    rho_hbm, vel_hbm, p_hbm, parent_hbm, shift_hbm, out_ref, main_ref, parent_ref, shift_ref,
-    rho_ref, vel_ref, p_ref, done,
-):
-    pairs = (
-        (rho_hbm, rho_ref),
-        (vel_hbm, vel_ref),
-        (p_hbm, p_ref),
-        (parent_hbm, parent_ref),
-        (shift_hbm, shift_ref),
-    )
-    copies = [pltpu.make_async_copy(a, b, done.at[k]) for k, (a, b) in enumerate(pairs)]
-    for copy in copies:
-        copy.start()
-    for copy in copies:
-        copy.wait()
+def ends_kernel(prim_ref, out_ref, up_ref, down_ref):
     lane = iota(1, (4, 128))
     for f in range(5):
         total = None
         for x in range(4):
-            row = rho_ref[x] if f == 0 else (p_ref[x] if f == 4 else vel_ref[f - 1, x])
-            main_ref[5 * x + f] = row
+            row = prim_ref[f, x]
             part = lane - 32 * x
             first = roll(row, 32 * x + 8, 1)
             last = roll(row, 32 * x + 24, 1)
             piece = jnp.where(part < 16, first, last)
             total = piece if total is None else jnp.where(part < 0, total, piece)
         out_ref[f] = total
-
-
-def block_kernel(ends_ref, before_ref, after_ref, main_ref, out_ref, up_ref, down_ref):
+        for ref, x in ((up_ref, 3), (down_ref, 0)):
+            ref[f] = prim_ref[f, x]
+            ref[5 + f] = total
+
+
+def block_kernel(ends_ref, before_ref, after_ref, prim_ref, _, __, out_ref):
     lane = iota(1, (4, 128)) % 32
-    for copy in range(4):
-        out_ref[copy, 0:20] = main_ref[...]
-    up_ref[0:5] = main_ref[15:20]
-    down_ref[0:5] = main_ref[0:5]
     for f in range(5):
         edge = jnp.where(
             lane < 8,
@@ -177,30 +168,68 @@
         )
         for copy in range(4):
             out_ref[copy, 20 + f] = edge
-        up_ref[5 + f] = edge
-        down_ref[5 + f] = edge
+            for x in range(4):
+                out_ref[copy, 5 * x + f] = prim_ref[f, x]
+
+
+def near_kernel(place_ref, own_ref, up_ref, down_ref):
+    gy = place_ref[0]
+    over, under = lax.rem(gy + 1, 4), lax.rem(gy + 3, 4)
+    for ref, xs in ((up_ref, (3, 2, 1, 0)), (down_ref, (0, 1, 2, 3))):
+
+        def take(block, distance):
+            start = 5 * xs[distance - 1] if distance else 20
+            return own_ref[block, start : start + 5]
+
+        for k, distance in ((0, 1), (9, 0)):
+            for j, block in enumerate((gy, over, under)):
+                ref[5 * (k + j) : 5 * (k + j) + 5] = take(block, distance)
+        for k, distance in ((3, 3), (5, 2), (6, 4)):
+            ref[5 * k : 5 * k + 5] = take(gy, distance)
+        ref[20:25, 0:2] = take(under, 3)[:, 2:4]
+        ref[20:25, 2:4] = take(over, 3)[:, 0:2]
+        ref[35:40, 0:3] = take(under, 2)[:, 1:4]
+        ref[35:40, 3:4] = take(under, 4)[:, 3:4]
+        ref[40:45, 0:3] = take(over, 2)[:, 0:3]
+        ref[40:45, 3:4] = take(over, 4)[:, 0:1]
 
 
 def coarse_kernel(
-    place_ref, parent_ref, shift_ref, own_ref, prior_ref, next_ref, far_prior_ref, far_next_ref,
+    place_ref, own_ref, prior_ref, next_ref, far_prior_ref, far_next_ref,
     new_ref, message_ref,
     prim_ref, edge_ref, section_ref, section_edge_ref, made_ref, made_edge_ref,
     old_pack_ref, body_ref, tips_ref,
 ):
     gy, gz = place_ref[0], place_ref[1]
+    parent_ref, shift_ref = Table(place_ref, 2), Table(place_ref, 34)
     for k in range(4):
         source = lax.rem(gy + k, 4)
-        for base, ref, tile in ((5, prior_ref, 5), (25, own_ref, 10), (45, next_ref, 15)):
-            rows, tips = ref[source, 0:20], ref[source, 20:25]
+        rows, tips = own_ref[source, 0:20], own_ref[source, 20:25]
+        for ref, base, count, value in ((prim_ref, 25, 20, rows), (edge_ref, 10, 5, tips)):
             if k < 3:
-                at = 2 + 4 * k
-                prim_ref[base : base + 20, at : at + 4] = rows
-                edge_ref[tile : tile + 5, at : at + 4] = tips
+                ref[base : base + count, 2 + 4 * k : 6 + 4 * k] = value
             else:
-                prim_ref[base : base + 20, 14:16] = rows[:, 0:2]
-                prim_ref[base : base + 20, 0:2] = rows[:, 2:4]
-                edge_ref[tile : tile + 5, 14:16] = tips[:, 0:2]
-                edge_ref[tile : tile + 5, 0:2] = tips[:, 2:4]
+                ref[base : base + count, 14:16] = value[:, 0:2]
+                ref[base : base + count, 0:2] = value[:, 2:4]
+    for got_ref, tile, bases in (
+        (prior_ref, 5, (20, 15, 10, 5)),
+        (next_ref, 15, (45, 50, 55, 60)),
+    ):
+        got = [got_ref[5 * k : 5 * k + 5] for k in range(12)]
+        for ref, base, first in ((prim_ref, bases[0], 0), (edge_ref, tile, 9)):
+            ref[base : base + 5, 2:6] = got[first]
+            ref[base : base + 5, 6:10] = got[first + 1]
+            ref[base : base + 5, 14:16] = got[first + 2][:, 0:2]
+            ref[base : base + 5, 0:2] = got[first + 2][:, 2:4]
+        for base, first in ((bases[2], 3), (bases[1], 5), (bases[3], 6)):
+            prim_ref[base : base + 5, 2:6] = got[first]
+        prim_ref[bases[2] : bases[2] + 5, 0:2] = got[4][:, 0:2]
+        prim_ref[bases[2] : bases[2] + 5, 6:8] = got[4][:, 2:4]
+        prim_ref[bases[1] : bases[1] + 5, 15:16] = got[7][:, 0:1]
+        prim_ref[bases[1] : bases[1] + 5, 0:2] = got[7][:, 1:3]
+        prim_ref[bases[1] : bases[1] + 5, 6:9] = got[8][:, 0:3]
+        prim_ref[bases[3] : bases[3] + 5, 1:2] = got[7][:, 3:4]
+        prim_ref[bases[3] : bases[3] + 5, 6:7] = got[8][:, 3:4]
     prim_ref[0:5, 2:6] = far_prior_ref[0:5]
     edge_ref[0:5, 2:6] = far_prior_ref[5:10]
     prim_ref[65:70, 2:6] = far_next_ref[0:5]
@@ -345,26 +374,39 @@
                             pltpu.roll(body_ref[k - OLD], amount, 1),
                         )
                     total = piece if total is None else jnp.where(lane < GROUP * j, total, piece)
-                message_ref[owner, tile] = total
+                if tile < TILES - 1:
+                    message_ref[owner, 2 * tile] = total[0:4]
+                    message_ref[owner, 2 * tile + 1] = total[4:8]
+                else:
+                    message_ref[owner, 2 * tile] = jnp.where(
+                        iota(1, (4, 128)) < 60, total[0:4], roll(total, 60, 1)[4:8]
+                    )
         return carry
 
     lax.fori_loop(0, 16 // SENDS, send, 0)
 
 
 def fine_kernel(
-    place_ref, parent_ref, got_ref, rho_ref, vel_ref, p_ref, out_ref, message_ref,
+    place_ref, got_ref, rho_ref, vel_ref, p_ref, out_ref, message_ref,
     mid_ref, tip_ref, ghost_ref, bound_ref,
 ):
     gz = place_ref[1]
+    parent_ref = Table(place_ref, 2)
     lane, sub = iota(1), iota(0)
     part = lane % 16
     yc, xc = lane // 32, sub // 2
     parents = [parent_ref[2 * gz + box] for box in range(2)]
 
     for box in range(2):
+        tiles = [
+            jnp.concatenate([got_ref[parents[box], 2 * t], got_ref[parents[box], 2 * t + 1]])
+            for t in range(TILES - 1)
+        ]
+        short = got_ref[parents[box], 2 * TILES - 2]
+        tiles.append(jnp.concatenate([short, roll(short, -60, 1)]))
         for k in range(OLD + 10):
             j = k % PER_ROW
-            tile = got_ref[parents[box], k // PER_ROW]
+            tile = tiles[k // PER_ROW]
             at = GROUP * j + 1 + part // 2
             mid_ref[box, 8 * k : 8 * k + 8] = jnp.take_along_axis(tile, at, axis=1)
             at = GROUP * j + jnp.where(part < 8, 0, 9)
@@ -512,8 +554,9 @@
         message_ref[parents[box]] = packed
 
 
-def final_kernel(place_ref, parent_ref, shift_ref, new_ref, got_ref, out_ref, sum_ref):
+def final_kernel(place_ref, new_ref, got_ref, out_ref, sum_ref):
     gz = place_ref[1]
+    parent_ref, shift_ref = Table(place_ref, 2), Table(place_ref, 34)
     lane = iota(1)
 
     def add(turn, carry):
@@ -575,31 +618,23 @@
 ):
     assert density.shape == (4, 4, 128) and fine_density.shape == (1, 1, 2, 8, 128)
     place = jnp.stack([lax.axis_index("gy"), lax.axis_index("gz")]).astype(jnp.int32)
-    table = jax.ShapeDtypeStruct((32,), jnp.int32)
-    ends, main, parents, shifts = pl.pallas_call(
-        ends_kernel,
-        out_shape=(shape(5, 4, 128), shape(20, 4, 128), table, table),
-        in_specs=[pl.BlockSpec(memory_space=pltpu.HBM)] * 5,
-        out_specs=(pl.BlockSpec(memory_space=pltpu.VMEM),) * 4,
-        scratch_shapes=[
-            pltpu.VMEM((4, 4, 128), F32),
-            pltpu.VMEM((3, 4, 4, 128), F32),
-            pltpu.VMEM((4, 4, 128), F32),
-            pltpu.SemaphoreType.DMA((5,)),
-        ],
-        compiler_params=pltpu.CompilerParams(vmem_limit_bytes=56 * 1024 * 1024),
-    )(density, velocity, pressure, box_parent.reshape(32), box_shift.reshape(32))
+    place = jnp.concatenate([place, box_parent.reshape(32), box_shift.reshape(32)])
+    prim = jnp.concatenate([density[None], velocity, pressure[None]])
+    ends, for_up, for_down = call(
+        ends_kernel, (shape(5, 4, 128), shape(10, 4, 128), shape(10, 4, 128)), 0, 1
+    )(prim)
+    far_prior, far_next = shifted(for_up, "gx", 2), shifted(for_down, "gx", -2)
     before, after = shifted(ends, "gz", 1), shifted(ends, "gz", -1)
-    block, for_up, for_down = call(
-        block_kernel, (shape(4, 25, 4, 128), shape(10, 4, 128), shape(10, 4, 128)), 0, 4
-    )(ends, before, after, main)
-    far_prior, far_next = shifted(for_up, "gx", 2), shifted(for_down, "gx", -2)
+    block = call(block_kernel, shape(4, 25, 4, 128), 0, 6)(
+        ends, before, after, prim, far_prior, far_next
+    )
     own = lax.all_to_all(block, "gy", 0, 0, tiled=True)
-    prior, following = shifted(own, "gx", 1), shifted(own, "gx", -1)
+    for_up, for_down = call(near_kernel, (shape(60, 4, 128), shape(60, 4, 128)), 1, 1)(place, own)
+    prior, following = shifted(for_up, "gx", 1), shifted(for_down, "gx", -1)
     updated, message = call(
         coarse_kernel,
-        (shape(5, 4, 4, 128), shape(16, TILES, 8, 128)),
-        3,
+        (shape(5, 4, 4, 128), shape(16, 2 * TILES - 1, 4, 128)),
+        1,
         5,
         (
             (70, 16, 128),
@@ -612,26 +647,23 @@
             (10, 8, 128),
             (3, 10, 8, 128),
         ),
-    )(place, parents, shifts, own, prior, following, far_prior, far_next)
+    )(place, own, prior, following, far_prior, far_next)
     got = lax.all_to_all(message, "gz", 0, 0, tiled=True)
     fine, means = call(
         fine_kernel,
         (shape(5, 2, 8, 128), shape(16, 8, 128)),
-        2,
+        1,
         4,
         FINE_SCRATCH,
     )(
         place,
-        parents,
         got,
         fine_density.reshape(2, 8, 128),
         fine_velocity.reshape(3, 2, 8, 128),
         fine_pressure.reshape(2, 8, 128),
     )
     incoming = lax.all_to_all(means, "gz", 0, 0, tiled=True)
-    coarse = call(final_kernel, shape(5, 4, 4, 128), 3, 2, ((128, 128),))(
-        place, parents, shifts, updated, incoming
-    )
+    coarse = call(final_kernel, shape(5, 4, 4, 128), 1, 2, ((128, 128),))(place, updated, incoming)
     return coarse, fine.reshape(5, 1, 1, 2, 8, 128)
 
 

time: 85.5 us -> 84.7 us (level)
  blocking collectives: 39 us -> 31 us
  waiting for transfers between devices: 2.27 us -> 8.79 us
  local copies, waits for them, and re-layouts: 2.12 us -> 0.69 us
    all_to_all x1 -> x0, blocking collectives: 7.59 us -> none  [on_device(): own = lax.all_to_all(block, 'gy', 0, 0, tiled=True)]
    all_to_all x0 -> x1, waiting for transfers between devices: none -> 4.47 us  [on_device(): own = lax.all_to_all(block, 'gy', 0, 0, tiled=True)]
    all_to_all x0 -> x1, starting transfers between devices: none -> 4.01 us  [on_device(): own = lax.all_to_all(block, 'gy', 0, 0, tiled=True)]
    ppermute x6, starting transfers between devices: 29 us -> 25.7 us  [shifted(): lax.ppermute(value, axis, [(i, (i + step) % size) for i in range(size)])]
    ppermute x6, waiting for transfers between devices: 2.27 us -> 4.32 us  [shifted(): lax.ppermute(value, axis, [(i, (i + step) % size) for i in range(size)])]
    unnamed x14 -> x10, local copies, waits for them, and re-layouts: 2.12 us -> 0.69 us
    pallas_call x5 -> x6, Pallas kernels: 11.8 us -> 12.4 us  [the longest x1 6.36 us: on_device(): call(coarse_kernel, (shape(5, 4, 4, 128), shape(16, 2 * TILES - 1, 4, 128...]
  transfers between devices with their start and end apart: 6 -> 7, of which waited for: 3 -> 5; matrix products, arithmetic and copies ran while one was open for 0% -> 0% of each run, Pallas kernels for 0% -> 0%
where the time goes in v2:
time: 84.7 us; the launch traced here: 84.2 us
  blocking collectives  31 us (37%)
  starting transfers between devices  29.7 us (35%)
  Pallas kernels  12.4 us (15%)
  waiting for transfers between devices  8.79 us (10%)
    ppermute x6, starting transfers between devices, shifted(): lax.ppermute(value, axis, [(i, (i + step) % size) for i in range(size)])  25.7 us
    all_to_all x1, blocking collectives, on_device(): got = lax.all_to_all(message, 'gz', 0, 0, tiled=True)  20.6 us
    all_to_all x1, blocking collectives, on_device(): incoming = lax.all_to_all(means, 'gz', 0, 0, tiled=True)  10.4 us
    pallas_call x1, Pallas kernels, on_device(): call(coarse_kernel, (shape(5, 4, 4, 128), shape(16, 2 * TILES - 1, 4, 128...  6.36 us
    all_to_all x1, waiting for transfers between devices, on_device(): own = lax.all_to_all(block, 'gy', 0, 0, tiled=True)  4.47 us
    ppermute x6, waiting for transfers between devices, shifted(): lax.ppermute(value, axis, [(i, (i + step) % size) for i in range(size)])  4.32 us
    all_to_all x1, starting transfers between devices, on_device(): own = lax.all_to_all(block, 'gy', 0, 0, tiled=True)  4.01 us
    pallas_call x1, Pallas kernels, on_device(): call(fine_kernel, (shape(5, 2, 8, 128), shape(16, 8, 128)), 1, 4, FINE_SC...  2.76 us
  transfers between devices with their start and end apart: 7, of which 5 were waited for; matrix products, arithmetic and copies ran while one was open for 0% of the time, Pallas kernels for 0%

profile of v2, /device:TPU:1, one launch (start us, length us, event | category | flops | bytes accessed | tf_op | source)
XLA Modules:
  0.0 84.2 jit_solution(17409678050678862659)
XLA Ops:
  0.6 0.8 pad_maximum_fusion.prim_ref
  1.4 0.1 shard_map.95
  1.5 6.6 %collective-permute-start.2 = (f32[10,4,128]{2,1,0:T(4,128)S(1)}, f32[10,4,128]{2,1,0:T(4,128)S(1)}, u32[]{:S(2)}, u32[]{:S(2)}) collective-permute-start(f32[10,4,128]{2,1,0:T(4,128)S(1)} %get-tuple-element.12), channel_id=1, source_target_pairs={{0,128},{64,192},{128,256},{192,320},{256,384},{320,448},{384,512}... | collective-permute-start | bytes 61448 | tf_op jit(solution)/shard_map/ppermute | solution.py:613
  8.2 10.4 %collective-permute-start.3 = (f32[10,4,128]{2,1,0:T(4,128)S(1)}, f32[10,4,128]{2,1,0:T(4,128)S(1)}, u32[]{:S(2)}, u32[]{:S(2)}) collective-permute-start(f32[10,4,128]{2,1,0:T(4,128)S(1)} %get-tuple-element.13), channel_id=1, source_target_pairs={{0,640},{64,704},{128,0},{192,64},{256,128},{320,192},{384,256},{4... | collective-permute-start | bytes 61448 | tf_op jit(solution)/shard_map/ppermute | solution.py:613
  18.6 1.4 %collective-permute-start.1 = (f32[5,4,128]{2,1,0:T(4,128)S(1)}, f32[5,4,128]{2,1,0:T(4,128)S(1)}, u32[]{:S(2)}, u32[]{:S(2)}) collective-permute-start(f32[5,4,128]{2,1,0:T(4,128)S(1)} %get-tuple-element.11.ends_ref), channel_id=1, source_target_pairs={{0,15},{1,0},{2,1},{3,2},{4,3},{5,4},{6,5},{7,6},{8,7},{9,8},{10,9... | collective-permute-start | bytes 30728 | tf_op jit(solution)/shard_map/ppermute | solution.py:613
  20.0 0.7 collective-permute-start
  20.8 1.3 %collective-permute-done.1.after_ref = f32[5,4,128]{2,1,0:T(4,128)S(1)} collective-permute-done((f32[5,4,128]{2,1,0:T(4,128)S(1)}, f32[5,4,128]{2,1,0:T(4,128)S(1)}, u32[]{:S(2)}, u32[]{:S(2)}) %collective-permute-start.1) | collective-permute-done | bytes 10272 | tf_op jit(solution)/shard_map/ppermute | solution.py:613
  22.1 0.8 collective-permute-done.before_ref
  22.8 0.0 collective-permute-done.2._.far_prior_ref
  22.8 0.0 collective-permute-done.3.__.far_next_ref
  22.8 0.8 shard_map.96
  23.6 4.0 %all-to-all-start = ((f32[4,25,4,128]{3,2,1,0:T(4,128)}), f32[4,25,4,128]{3,2,1,0:T(4,128)S(1)}, u32[]{:S(2)}, u32[]{:S(2)}) async-start(f32[4,25,4,128]{3,2,1,0:T(4,128)} %shard_map.96), calls=%async_computation | async-start | bytes 409600 | tf_op jit(solution)/shard_map/all_to_all | solution.py:631
  27.6 0.0 copy-start.3
  27.6 0.0 copy-start.4
  27.6 0.7 copy-done.3
  28.3 0.0 copy-done.4
  28.3 0.1 pad_add_fusion.place_ref
  28.4 4.5 %all-to-all-done.own_ref = f32[4,25,4,128]{3,2,1,0:T(4,128)S(1)} async-done(((f32[4,25,4,128]{3,2,1,0:T(4,128)}), f32[4,25,4,128]{3,2,1,0:T(4,128)S(1)}, u32[]{:S(2)}, u32[]{:S(2)}) %all-to-all-start) | async-done | bytes 204832 | tf_op jit(solution)/shard_map/all_to_all | solution.py:631
  32.8 0.6 shard_map.97
  33.4 3.1 %collective-permute-start.4 = (f32[60,4,128]{2,1,0:T(4,128)S(1)}, f32[60,4,128]{2,1,0:T(4,128)S(1)}, u32[]{:S(2)}, u32[]{:S(2)}) collective-permute-start(f32[60,4,128]{2,1,0:T(4,128)S(1)} %get-tuple-element.14), channel_id=1, source_target_pairs={{0,64},{64,128},{128,192},{192,256},{256,320},{320,384},{384,448},... | collective-permute-start | bytes 368648 | tf_op jit(solution)/shard_map/ppermute | solution.py:613
  36.5 3.4 %collective-permute-start.5 = (f32[60,4,128]{2,1,0:T(4,128)S(1)}, f32[60,4,128]{2,1,0:T(4,128)S(1)}, u32[]{:S(2)}, u32[]{:S(2)}) collective-permute-start(f32[60,4,128]{2,1,0:T(4,128)S(1)} %get-tuple-element.15), channel_id=1, source_target_pairs={{0,704},{64,0},{128,64},{192,128},{256,192},{320,256},{384,320},{4... | collective-permute-start | bytes 368648 | tf_op jit(solution)/shard_map/ppermute | solution.py:613
  39.9 0.3 collective-permute-done.4.prior_ref
  40.3 1.9 %collective-permute-done.5.next_ref = f32[60,4,128]{2,1,0:T(4,128)S(1)} collective-permute-done((f32[60,4,128]{2,1,0:T(4,128)S(1)}, f32[60,4,128]{2,1,0:T(4,128)S(1)}, u32[]{:S(2)}, u32[]{:S(2)}) %collective-permute-start.5) | collective-permute-done | bytes 122912 | tf_op jit(solution)/shard_map/ppermute | solution.py:613
  42.2 6.4 %shard_map.98 = (f32[5,4,4,128]{3,2,1,0:T(4,128)S(1)}, f32[16,5,4,128]{3,2,1,0:T(4,128)S(1)}) custom-call(s32[66]{0:T(128)S(1)} %pad_add_fusion.place_ref, f32[4,25,4,128]{3,2,1,0:T(4,128)S(1)} %all-to-all-done.own_ref, f32[60,4,128]{2,1,0:T(4,128)S(1)} %collective-permute-done.4.prior_ref, f32[60,4,128]{2,1,0:T(4,128)S(1)} %collective-permute-done.5.next_ref, ...), custom_call_target="tpu_custom_call" | custom-call | tf_op jit(solution)/shard_map/pallas_call | solution.py:634
  48.5 0.0 copy-start
  48.5 0.0 copy-start.1
  48.6 0.0 copy-start.2
  48.6 20.6 %all_to_all.15.got_ref = f32[16,5,4,128]{3,2,1,0:T(4,128)S(1)} all-to-all(f32[16,5,4,128]{3,2,1,0:T(4,128)S(1)} %get-tuple-element.17), channel_id=1, replica_groups=mesh['gx'=12,'gy'=4,'gz'=16] {'gz'}, dimensions={0} | all-to-all | bytes 327680 | tf_op jit(solution)/shard_map/all_to_all | solution.py:651
  69.2 0.0 copy-done
  69.2 0.0 copy-done.1
  69.2 0.0 copy-done.2
  69.2 2.8 %shard_map.99 = (f32[5,2,8,128]{3,2,1,0:T(8,128)}, f32[16,8,128]{2,1,0:T(8,128)S(1)}) custom-call(s32[66]{0:T(128)S(1)} %pad_add_fusion.place_ref, f32[16,5,4,128]{3,2,1,0:T(4,128)S(1)} %all_to_all.15.got_ref, f32[2,8,128]{2,1,0:T(8,128)S(1)} %bitcast.13, f32[3,2,8,128]{3,2,1,0:T(8,128)S(1)} %bitcast.12, f32[2,8,128]{2,1,0:T(8,128)S(1)} %bitcast.14), custom_call_target="tpu_custom_call" | custom-call | tf_op jit(solution)/shard_map/pallas_call | solution.py:652
  71.9 10.4 %all_to_all.16.got_ref = f32[16,8,128]{2,1,0:T(8,128)S(1)} all-to-all(f32[16,8,128]{2,1,0:T(8,128)S(1)} %get-tuple-element.18), channel_id=1, replica_groups=mesh['gx'=12,'gy'=4,'gz'=16] {'gz'}, dimensions={0} | all-to-all | bytes 131072 | tf_op jit(solution)/shard_map/all_to_all | solution.py:665
  82.4 1.8 %shard_map.100 = f32[5,4,4,128]{3,2,1,0:T(4,128)} custom-call(s32[66]{0:T(128)S(1)} %pad_add_fusion.place_ref, f32[5,4,4,128]{3,2,1,0:T(4,128)S(1)} %get-tuple-element.16.new_ref, f32[16,8,128]{2,1,0:T(8,128)S(1)} %all_to_all.16.got_ref), custom_call_target="tpu_custom_call" | custom-call | tf_op jit(solution)/shard_map/pallas_call | solution.py:666
Async XLA Ops:
  1.5 21.3 %collective-permute-start.2 = (f32[10,4,128]{2,1,0:T(4,128)S(1)}, f32[10,4,128]{2,1,0:T(4,128)S(1)}, u32[]{:S(2)}, u32[]{:S(2)}) collective-permute-start(f32[10,4,128]{2,1,0:T(4,128)S(1)} %get-tuple-element.12), channel_id=1, source_target_pairs={{0,128},{64,192},{128,256},{192,320},{256,384},{320,448},{384,512}... | collective-permute-start | bytes 61448 | tf_op jit(solution)/shard_map/ppermute | solution.py:613
  8.2 14.7 %collective-permute-start.3 = (f32[10,4,128]{2,1,0:T(4,128)S(1)}, f32[10,4,128]{2,1,0:T(4,128)S(1)}, u32[]{:S(2)}, u32[]{:S(2)}) collective-permute-start(f32[10,4,128]{2,1,0:T(4,128)S(1)} %get-tuple-element.13), channel_id=1, source_target_pairs={{0,640},{64,704},{128,0},{192,64},{256,128},{320,192},{384,256},{4... | collective-permute-start | bytes 61448 | tf_op jit(solution)/shard_map/ppermute | solution.py:613
  18.6 3.5 %collective-permute-start.1 = (f32[5,4,128]{2,1,0:T(4,128)S(1)}, f32[5,4,128]{2,1,0:T(4,128)S(1)}, u32[]{:S(2)}, u32[]{:S(2)}) collective-permute-start(f32[5,4,128]{2,1,0:T(4,128)S(1)} %get-tuple-element.11.ends_ref), channel_id=1, source_target_pairs={{0,15},{1,0},{2,1},{3,2},{4,3},{5,4},{6,5},{7,6},{8,7},{9,8},{10,9... | collective-permute-start | bytes 30728 | tf_op jit(solution)/shard_map/ppermute | solution.py:613
  20.0 2.8 %collective-permute-start = (f32[5,4,128]{2,1,0:T(4,128)S(1)}, f32[5,4,128]{2,1,0:T(4,128)S(1)}, u32[]{:S(2)}, u32[]{:S(2)}) collective-permute-start(f32[5,4,128]{2,1,0:T(4,128)S(1)} %get-tuple-element.11.ends_ref), channel_id=1, source_target_pairs={{0,1},{1,2},{2,3},{3,4},{4,5},{5,6},{6,7},{7,8},{8,9},{9,10},{10,1... | collective-permute-start | bytes 30728 | tf_op jit(solution)/shard_map/ppermute | solution.py:613
  23.6 9.2 %all-to-all-start = ((f32[4,25,4,128]{3,2,1,0:T(4,128)}), f32[4,25,4,128]{3,2,1,0:T(4,128)S(1)}, u32[]{:S(2)}, u32[]{:S(2)}) async-start(f32[4,25,4,128]{3,2,1,0:T(4,128)} %shard_map.96), calls=%async_computation | async-start | bytes 409600 | tf_op jit(solution)/shard_map/all_to_all | solution.py:631
  27.6 0.7 copy-start.3
  27.6 0.7 copy-start.4
  33.4 6.8 %collective-permute-start.4 = (f32[60,4,128]{2,1,0:T(4,128)S(1)}, f32[60,4,128]{2,1,0:T(4,128)S(1)}, u32[]{:S(2)}, u32[]{:S(2)}) collective-permute-start(f32[60,4,128]{2,1,0:T(4,128)S(1)} %get-tuple-element.14), channel_id=1, source_target_pairs={{0,64},{64,128},{128,192},{192,256},{256,320},{320,384},{384,448},... | collective-permute-start | bytes 368648 | tf_op jit(solution)/shard_map/ppermute | solution.py:613
  36.5 5.6 %collective-permute-start.5 = (f32[60,4,128]{2,1,0:T(4,128)S(1)}, f32[60,4,128]{2,1,0:T(4,128)S(1)}, u32[]{:S(2)}, u32[]{:S(2)}) collective-permute-start(f32[60,4,128]{2,1,0:T(4,128)S(1)} %get-tuple-element.15), channel_id=1, source_target_pairs={{0,704},{64,0},{128,64},{192,128},{256,192},{320,256},{384,320},{4... | collective-permute-start | bytes 368648 | tf_op jit(solution)/shard_map/ppermute | solution.py:613
  48.5 20.6 %copy-start = (f32[3,1,1,2,8,128]{5,4,3,2,1,0:T(8,128)S(1)}, f32[3,1,1,2,8,128]{5,4,3,2,1,0:T(8,128)}, u32[]{:S(2)}) copy-start(f32[3,1,1,2,8,128]{5,4,3,2,1,0:T(8,128)} %param.12) | copy-start | bytes 73732
  48.5 20.6 %copy-start.1 = (f32[1,1,2,8,128]{4,3,2,1,0:T(8,128)S(1)}, f32[1,1,2,8,128]{4,3,2,1,0:T(8,128)}, u32[]{:S(2)}) copy-start(f32[1,1,2,8,128]{4,3,2,1,0:T(8,128)} %param.11) | copy-start | bytes 24580
  48.6 20.6 %copy-start.2 = (f32[1,1,2,8,128]{4,3,2,1,0:T(8,128)S(1)}, f32[1,1,2,8,128]{4,3,2,1,0:T(8,128)}, u32[]{:S(2)}) copy-start(f32[1,1,2,8,128]{4,3,2,1,0:T(8,128)} %param.13) | copy-start | bytes 24580

commit v3 on v2

--- a/solution.py
+++ b/solution.py
@@ -141,7 +141,7 @@
     }
 
 
-def ends_kernel(prim_ref, out_ref, up_ref, down_ref):
+def ends_kernel(prim_ref, out_ref):
     lane = iota(1, (4, 128))
     for f in range(5):
         total = None
@@ -153,12 +153,9 @@
             piece = jnp.where(part < 16, first, last)
             total = piece if total is None else jnp.where(part < 0, total, piece)
         out_ref[f] = total
-        for ref, x in ((up_ref, 3), (down_ref, 0)):
-            ref[f] = prim_ref[f, x]
-            ref[5 + f] = total
-
-
-def block_kernel(ends_ref, before_ref, after_ref, prim_ref, _, __, out_ref):
+
+
+def block_kernel(_, ends_ref, before_ref, after_ref, prim_ref, out_ref, up_ref, down_ref):
     lane = iota(1, (4, 128)) % 32
     for f in range(5):
         edge = jnp.where(
@@ -170,9 +167,12 @@
             out_ref[copy, 20 + f] = edge
             for x in range(4):
                 out_ref[copy, 5 * x + f] = prim_ref[f, x]
-
-
-def near_kernel(place_ref, own_ref, up_ref, down_ref):
+        for ref, x in ((up_ref, 3), (down_ref, 0)):
+            ref[f] = prim_ref[f, x]
+            ref[5 + f] = edge
+
+
+def near_kernel(place_ref, own_ref, _, __, up_ref, down_ref):
     gy = place_ref[0]
     over, under = lax.rem(gy + 1, 4), lax.rem(gy + 3, 4)
     for ref, xs in ((up_ref, (3, 2, 1, 0)), (down_ref, (0, 1, 2, 3))):
@@ -620,16 +620,16 @@
     place = jnp.stack([lax.axis_index("gy"), lax.axis_index("gz")]).astype(jnp.int32)
     place = jnp.concatenate([place, box_parent.reshape(32), box_shift.reshape(32)])
     prim = jnp.concatenate([density[None], velocity, pressure[None]])
-    ends, for_up, for_down = call(
-        ends_kernel, (shape(5, 4, 128), shape(10, 4, 128), shape(10, 4, 128)), 0, 1
-    )(prim)
+    ends = call(ends_kernel, shape(5, 4, 128), 0, 1)(prim)
+    before, after = shifted(ends, "gz", 1), shifted(ends, "gz", -1)
+    block, for_up, for_down = call(
+        block_kernel, (shape(4, 25, 4, 128), shape(10, 4, 128), shape(10, 4, 128)), 1, 4
+    )(place, ends, before, after, prim)
+    own = lax.all_to_all(block, "gy", 0, 0, tiled=True)
     far_prior, far_next = shifted(for_up, "gx", 2), shifted(for_down, "gx", -2)
-    before, after = shifted(ends, "gz", 1), shifted(ends, "gz", -1)
-    block = call(block_kernel, shape(4, 25, 4, 128), 0, 6)(
-        ends, before, after, prim, far_prior, far_next
-    )
-    own = lax.all_to_all(block, "gy", 0, 0, tiled=True)
-    for_up, for_down = call(near_kernel, (shape(60, 4, 128), shape(60, 4, 128)), 1, 1)(place, own)
+    for_up, for_down = call(near_kernel, (shape(60, 4, 128), shape(60, 4, 128)), 1, 3)(
+        place, own, far_prior, far_next
+    )
     prior, following = shifted(for_up, "gx", 1), shifted(for_down, "gx", -1)
     updated, message = call(
         coarse_kernel,

time: 84.7 us -> 80.8 us (0.954)
  waiting for transfers between devices: 8.79 us -> 3.15 us
  starting transfers between devices: 29.7 us -> 31.8 us
  blocking collectives: 31 us -> 30.1 us
    all_to_all x1, waiting for transfers between devices: 4.47 us -> 0.01 us  [on_device(): own = lax.all_to_all(block, 'gy', 0, 0, tiled=True)]
    ppermute x6, starting transfers between devices: 25.7 us -> 28.5 us  [shifted(): lax.ppermute(value, axis, [(i, (i + step) % size) for i in range(size)])]
    ppermute x6, waiting for transfers between devices: 4.32 us -> 3.15 us  [shifted(): lax.ppermute(value, axis, [(i, (i + step) % size) for i in range(size)])]
    all_to_all x1, blocking collectives: 20.6 us -> 19.7 us  [on_device(): got = lax.all_to_all(message, 'gz', 0, 0, tiled=True)]
where the time goes in v3:
time: 80.8 us; the launch traced here: 80.3 us
  starting transfers between devices  31.8 us (39%)
  blocking collectives  30.1 us (37%)
  Pallas kernels  12.9 us (16%)
  waiting for transfers between devices  3.15 us (4%)
  other arithmetic  0.84 us (1%)
    ppermute x6, starting transfers between devices, shifted(): lax.ppermute(value, axis, [(i, (i + step) % size) for i in range(size)])  28.5 us
    all_to_all x1, blocking collectives, on_device(): got = lax.all_to_all(message, 'gz', 0, 0, tiled=True)  19.7 us
    all_to_all x1, blocking collectives, on_device(): incoming = lax.all_to_all(means, 'gz', 0, 0, tiled=True)  10.4 us
    pallas_call x1, Pallas kernels, on_device(): call(coarse_kernel, (shape(5, 4, 4, 128), shape(16, 2 * TILES - 1, 4, 128...  6.36 us
    all_to_all x1, starting transfers between devices, on_device(): own = lax.all_to_all(block, 'gy', 0, 0, tiled=True)  3.37 us
    ppermute x6, waiting for transfers between devices, shifted(): lax.ppermute(value, axis, [(i, (i + step) % size) for i in range(size)])  3.15 us
    pallas_call x1, Pallas kernels, on_device(): call(fine_kernel, (shape(5, 2, 8, 128), shape(16, 8, 128)), 1, 4, FINE_SC...  2.76 us
    pallas_call x1, Pallas kernels, on_device(): call(final_kernel, shape(5, 4, 4, 128), 1, 2, ((128, 128),))  1.82 us
  transfers between devices with their start and end apart: 7, of which 5 were waited for; matrix products, arithmetic and copies ran while one was open for 0% of the time, Pallas kernels for 0%

profile of v3, /device:TPU:1, one launch (start us, length us, event | category | flops | bytes accessed | tf_op | source)
XLA Modules:
  0.0 80.3 jit_solution(10477524316868325671)
XLA Ops:
  0.6 0.8 pad_maximum_fusion.prim_ref
  1.4 0.1 shard_map.95.ends_ref
  1.5 10.5 %collective-permute-start.1 = (f32[5,4,128]{2,1,0:T(4,128)S(1)}, f32[5,4,128]{2,1,0:T(4,128)S(1)}, u32[]{:S(2)}, u32[]{:S(2)}) collective-permute-start(f32[5,4,128]{2,1,0:T(4,128)S(1)} %shard_map.95.ends_ref), channel_id=1, source_target_pairs={{0,15},{1,0},{2,1},{3,2},{4,3},{5,4},{6,5},{7,6},{8,7},{9,8},{10,9... | collective-permute-start | bytes 30728 | tf_op jit(solution)/shard_map/ppermute | solution.py:613
  12.0 0.0 collective-permute-start
  12.0 0.0 copy-start.3
  12.0 0.0 copy-start.4
  12.0 0.7 copy-done.3
  12.7 0.0 copy-done.4
  12.7 0.1 pad_add_fusion._.place_ref
  12.8 0.1 collective-permute-done.1.after_ref
  12.9 0.3 collective-permute-done.before_ref
  13.2 1.3 %shard_map.96 = (f32[4,25,4,128]{3,2,1,0:T(4,128)}, f32[10,4,128]{2,1,0:T(4,128)S(1)}, f32[10,4,128]{2,1,0:T(4,128)S(1)}) custom-call(s32[66]{0:T(128)S(1)} %pad_add_fusion._.place_ref, f32[5,4,128]{2,1,0:T(4,128)S(1)} %shard_map.95.ends_ref, f32[5,4,128]{2,1,0:T(4,128)S(1)} %collective-permute-done.before_ref, ...), custom_call_target="tpu_custom_call" | custom-call | tf_op jit(solution)/shard_map/pallas_call | solution.py:625
  14.5 3.4 %all-to-all-start = ((f32[4,25,4,128]{3,2,1,0:T(4,128)}), f32[4,25,4,128]{3,2,1,0:T(4,128)S(1)}, u32[]{:S(2)}, u32[]{:S(2)}) async-start(f32[4,25,4,128]{3,2,1,0:T(4,128)} %get-tuple-element.11), calls=%async_computation | async-start | bytes 409600 | tf_op jit(solution)/shard_map/all_to_all | solution.py:628
  17.9 1.9 %collective-permute-start.2 = (f32[10,4,128]{2,1,0:T(4,128)S(1)}, f32[10,4,128]{2,1,0:T(4,128)S(1)}, u32[]{:S(2)}, u32[]{:S(2)}) collective-permute-start(f32[10,4,128]{2,1,0:T(4,128)S(1)} %get-tuple-element.12), channel_id=1, source_target_pairs={{0,128},{64,192},{128,256},{192,320},{256,384},{320,448},{384,512}... | collective-permute-start | bytes 61448 | tf_op jit(solution)/shard_map/ppermute | solution.py:613
  19.8 8.3 %collective-permute-start.3 = (f32[10,4,128]{2,1,0:T(4,128)S(1)}, f32[10,4,128]{2,1,0:T(4,128)S(1)}, u32[]{:S(2)}, u32[]{:S(2)}) collective-permute-start(f32[10,4,128]{2,1,0:T(4,128)S(1)} %get-tuple-element.13), channel_id=1, source_target_pairs={{0,640},{64,704},{128,0},{192,64},{256,128},{320,192},{384,256},{4... | collective-permute-start | bytes 61448 | tf_op jit(solution)/shard_map/ppermute | solution.py:613
  28.1 0.0 collective-permute-done.2._.far_prior_ref
  28.1 0.9 %collective-permute-done.3.__.far_next_ref = f32[10,4,128]{2,1,0:T(4,128)S(1)} collective-permute-done((f32[10,4,128]{2,1,0:T(4,128)S(1)}, f32[10,4,128]{2,1,0:T(4,128)S(1)}, u32[]{:S(2)}, u32[]{:S(2)}) %collective-permute-start.3) | collective-permute-done | bytes 20512 | tf_op jit(solution)/shard_map/ppermute | solution.py:613
  29.0 0.0 all-to-all-done.own_ref
  29.0 0.6 shard_map.97
  29.6 3.1 %collective-permute-start.4 = (f32[60,4,128]{2,1,0:T(4,128)S(1)}, f32[60,4,128]{2,1,0:T(4,128)S(1)}, u32[]{:S(2)}, u32[]{:S(2)}) collective-permute-start(f32[60,4,128]{2,1,0:T(4,128)S(1)} %get-tuple-element.14), channel_id=1, source_target_pairs={{0,64},{64,128},{128,192},{192,256},{256,320},{320,384},{384,448},... | collective-permute-start | bytes 368648 | tf_op jit(solution)/shard_map/ppermute | solution.py:613
  32.7 4.6 %collective-permute-start.5 = (f32[60,4,128]{2,1,0:T(4,128)S(1)}, f32[60,4,128]{2,1,0:T(4,128)S(1)}, u32[]{:S(2)}, u32[]{:S(2)}) collective-permute-start(f32[60,4,128]{2,1,0:T(4,128)S(1)} %get-tuple-element.15), channel_id=1, source_target_pairs={{0,704},{64,0},{128,64},{192,128},{256,192},{320,256},{384,320},{4... | collective-permute-start | bytes 368648 | tf_op jit(solution)/shard_map/ppermute | solution.py:613
  37.3 0.3 collective-permute-done.4.prior_ref
  37.7 1.5 %collective-permute-done.5.next_ref = f32[60,4,128]{2,1,0:T(4,128)S(1)} collective-permute-done((f32[60,4,128]{2,1,0:T(4,128)S(1)}, f32[60,4,128]{2,1,0:T(4,128)S(1)}, u32[]{:S(2)}, u32[]{:S(2)}) %collective-permute-start.5) | collective-permute-done | bytes 122912 | tf_op jit(solution)/shard_map/ppermute | solution.py:613
  39.2 6.4 %shard_map.98 = (f32[5,4,4,128]{3,2,1,0:T(4,128)S(1)}, f32[16,5,4,128]{3,2,1,0:T(4,128)S(1)}) custom-call(s32[66]{0:T(128)S(1)} %pad_add_fusion._.place_ref, f32[4,25,4,128]{3,2,1,0:T(4,128)S(1)} %all-to-all-done.own_ref, f32[60,4,128]{2,1,0:T(4,128)S(1)} %collective-permute-done.4.prior_ref, f32[60,4,128]{2,1,0:T(4,128)S(1)} %collective-permute-done.5.next_ref, ...), custom_call_target="tpu_custom_call" | custom-call | tf_op jit(solution)/shard_map/pallas_call | solution.py:634
  45.6 0.0 copy-start
  45.6 0.0 copy-start.1
  45.6 0.0 copy-start.2
  45.6 19.7 %all_to_all.15.got_ref = f32[16,5,4,128]{3,2,1,0:T(4,128)S(1)} all-to-all(f32[16,5,4,128]{3,2,1,0:T(4,128)S(1)} %get-tuple-element.17), channel_id=1, replica_groups=mesh['gx'=12,'gy'=4,'gz'=16] {'gz'}, dimensions={0} | all-to-all | bytes 327680 | tf_op jit(solution)/shard_map/all_to_all | solution.py:651
  65.3 0.0 copy-done
  65.3 0.0 copy-done.1
  65.3 0.0 copy-done.2
  65.3 2.8 %shard_map.99 = (f32[5,2,8,128]{3,2,1,0:T(8,128)}, f32[16,8,128]{2,1,0:T(8,128)S(1)}) custom-call(s32[66]{0:T(128)S(1)} %pad_add_fusion._.place_ref, f32[16,5,4,128]{3,2,1,0:T(4,128)S(1)} %all_to_all.15.got_ref, f32[2,8,128]{2,1,0:T(8,128)S(1)} %bitcast.13, f32[3,2,8,128]{3,2,1,0:T(8,128)S(1)} %bitcast.12, f32[2,8,128]{2,1,0:T(8,128)S(1)} %bitcast.14), custom_call_target="tpu_custom_call" | custom-call | tf_op jit(solution)/shard_map/pallas_call | solution.py:652
  68.1 10.4 %all_to_all.16.got_ref = f32[16,8,128]{2,1,0:T(8,128)S(1)} all-to-all(f32[16,8,128]{2,1,0:T(8,128)S(1)} %get-tuple-element.18), channel_id=1, replica_groups=mesh['gx'=12,'gy'=4,'gz'=16] {'gz'}, dimensions={0} | all-to-all | bytes 131072 | tf_op jit(solution)/shard_map/all_to_all | solution.py:665
  78.5 1.8 %shard_map.100 = f32[5,4,4,128]{3,2,1,0:T(4,128)} custom-call(s32[66]{0:T(128)S(1)} %pad_add_fusion._.place_ref, f32[5,4,4,128]{3,2,1,0:T(4,128)S(1)} %get-tuple-element.16.new_ref, f32[16,8,128]{2,1,0:T(8,128)S(1)} %all_to_all.16.got_ref), custom_call_target="tpu_custom_call" | custom-call | tf_op jit(solution)/shard_map/pallas_call | solution.py:666
Async XLA Ops:
  1.5 11.4 %collective-permute-start.1 = (f32[5,4,128]{2,1,0:T(4,128)S(1)}, f32[5,4,128]{2,1,0:T(4,128)S(1)}, u32[]{:S(2)}, u32[]{:S(2)}) collective-permute-start(f32[5,4,128]{2,1,0:T(4,128)S(1)} %shard_map.95.ends_ref), channel_id=1, source_target_pairs={{0,15},{1,0},{2,1},{3,2},{4,3},{5,4},{6,5},{7,6},{8,7},{9,8},{10,9... | collective-permute-start | bytes 30728 | tf_op jit(solution)/shard_map/ppermute | solution.py:613
  12.0 1.2 %collective-permute-start = (f32[5,4,128]{2,1,0:T(4,128)S(1)}, f32[5,4,128]{2,1,0:T(4,128)S(1)}, u32[]{:S(2)}, u32[]{:S(2)}) collective-permute-start(f32[5,4,128]{2,1,0:T(4,128)S(1)} %shard_map.95.ends_ref), channel_id=1, source_target_pairs={{0,1},{1,2},{2,3},{3,4},{4,5},{5,6},{6,7},{7,8},{8,9},{9,10},{10,1... | collective-permute-start | bytes 30728 | tf_op jit(solution)/shard_map/ppermute | solution.py:613
  12.0 0.7 copy-start.3
  12.0 0.7 copy-start.4
  14.5 14.5 %all-to-all-start = ((f32[4,25,4,128]{3,2,1,0:T(4,128)}), f32[4,25,4,128]{3,2,1,0:T(4,128)S(1)}, u32[]{:S(2)}, u32[]{:S(2)}) async-start(f32[4,25,4,128]{3,2,1,0:T(4,128)} %get-tuple-element.11), calls=%async_computation | async-start | bytes 409600 | tf_op jit(solution)/shard_map/all_to_all | solution.py:628
  17.9 10.2 %collective-permute-start.2 = (f32[10,4,128]{2,1,0:T(4,128)S(1)}, f32[10,4,128]{2,1,0:T(4,128)S(1)}, u32[]{:S(2)}, u32[]{:S(2)}) collective-permute-start(f32[10,4,128]{2,1,0:T(4,128)S(1)} %get-tuple-element.12), channel_id=1, source_target_pairs={{0,128},{64,192},{128,256},{192,320},{256,384},{320,448},{384,512}... | collective-permute-start | bytes 61448 | tf_op jit(solution)/shard_map/ppermute | solution.py:613
  19.8 9.2 %collective-permute-start.3 = (f32[10,4,128]{2,1,0:T(4,128)S(1)}, f32[10,4,128]{2,1,0:T(4,128)S(1)}, u32[]{:S(2)}, u32[]{:S(2)}) collective-permute-start(f32[10,4,128]{2,1,0:T(4,128)S(1)} %get-tuple-element.13), channel_id=1, source_target_pairs={{0,640},{64,704},{128,0},{192,64},{256,128},{320,192},{384,256},{4... | collective-permute-start | bytes 61448 | tf_op jit(solution)/shard_map/ppermute | solution.py:613
  29.6 8.0 %collective-permute-start.4 = (f32[60,4,128]{2,1,0:T(4,128)S(1)}, f32[60,4,128]{2,1,0:T(4,128)S(1)}, u32[]{:S(2)}, u32[]{:S(2)}) collective-permute-start(f32[60,4,128]{2,1,0:T(4,128)S(1)} %get-tuple-element.14), channel_id=1, source_target_pairs={{0,64},{64,128},{128,192},{192,256},{256,320},{320,384},{384,448},... | collective-permute-start | bytes 368648 | tf_op jit(solution)/shard_map/ppermute | solution.py:613
  32.7 6.5 %collective-permute-start.5 = (f32[60,4,128]{2,1,0:T(4,128)S(1)}, f32[60,4,128]{2,1,0:T(4,128)S(1)}, u32[]{:S(2)}, u32[]{:S(2)}) collective-permute-start(f32[60,4,128]{2,1,0:T(4,128)S(1)} %get-tuple-element.15), channel_id=1, source_target_pairs={{0,704},{64,0},{128,64},{192,128},{256,192},{320,256},{384,320},{4... | collective-permute-start | bytes 368648 | tf_op jit(solution)/shard_map/ppermute | solution.py:613
  45.6 19.7 %copy-start = (f32[3,1,1,2,8,128]{5,4,3,2,1,0:T(8,128)S(1)}, f32[3,1,1,2,8,128]{5,4,3,2,1,0:T(8,128)}, u32[]{:S(2)}) copy-start(f32[3,1,1,2,8,128]{5,4,3,2,1,0:T(8,128)} %param.12) | copy-start | bytes 73732
  45.6 19.7 %copy-start.1 = (f32[1,1,2,8,128]{4,3,2,1,0:T(8,128)S(1)}, f32[1,1,2,8,128]{4,3,2,1,0:T(8,128)}, u32[]{:S(2)}) copy-start(f32[1,1,2,8,128]{4,3,2,1,0:T(8,128)} %param.11) | copy-start | bytes 24580
  45.6 19.7 %copy-start.2 = (f32[1,1,2,8,128]{4,3,2,1,0:T(8,128)S(1)}, f32[1,1,2,8,128]{4,3,2,1,0:T(8,128)}, u32[]{:S(2)}) copy-start(f32[1,1,2,8,128]{4,3,2,1,0:T(8,128)} %param.13) | copy-start | bytes 24580

commit v4 on v3

--- a/solution.py
+++ b/solution.py
@@ -141,7 +141,7 @@
     }
 
 
-def ends_kernel(prim_ref, out_ref):
+def ends_kernel(prim_ref, out_ref, up_ref):
     lane = iota(1, (4, 128))
     for f in range(5):
         total = None
@@ -153,9 +153,11 @@
             piece = jnp.where(part < 16, first, last)
             total = piece if total is None else jnp.where(part < 0, total, piece)
         out_ref[f] = total
-
-
-def block_kernel(_, ends_ref, before_ref, after_ref, prim_ref, out_ref, up_ref, down_ref):
+        up_ref[f] = prim_ref[f, 3]
+        up_ref[5 + f] = total
+
+
+def block_kernel(_, ends_ref, before_ref, after_ref, prim_ref, __, out_ref, down_ref):
     lane = iota(1, (4, 128)) % 32
     for f in range(5):
         edge = jnp.where(
@@ -167,12 +169,11 @@
             out_ref[copy, 20 + f] = edge
             for x in range(4):
                 out_ref[copy, 5 * x + f] = prim_ref[f, x]
-        for ref, x in ((up_ref, 3), (down_ref, 0)):
-            ref[f] = prim_ref[f, x]
-            ref[5 + f] = edge
-
-
-def near_kernel(place_ref, own_ref, _, __, up_ref, down_ref):
+        down_ref[f] = prim_ref[f, 0]
+        down_ref[5 + f] = edge
+
+
+def near_kernel(place_ref, own_ref, _, up_ref, down_ref):
     gy = place_ref[0]
     over, under = lax.rem(gy + 1, 4), lax.rem(gy + 3, 4)
     for ref, xs in ((up_ref, (3, 2, 1, 0)), (down_ref, (0, 1, 2, 3))):
@@ -620,15 +621,16 @@
     place = jnp.stack([lax.axis_index("gy"), lax.axis_index("gz")]).astype(jnp.int32)
     place = jnp.concatenate([place, box_parent.reshape(32), box_shift.reshape(32)])
     prim = jnp.concatenate([density[None], velocity, pressure[None]])
-    ends = call(ends_kernel, shape(5, 4, 128), 0, 1)(prim)
+    ends, for_up = call(ends_kernel, (shape(5, 4, 128), shape(10, 4, 128)), 0, 1)(prim)
     before, after = shifted(ends, "gz", 1), shifted(ends, "gz", -1)
-    block, for_up, for_down = call(
-        block_kernel, (shape(4, 25, 4, 128), shape(10, 4, 128), shape(10, 4, 128)), 1, 4
-    )(place, ends, before, after, prim)
+    far_prior = shifted(for_up, "gx", 2)
+    block, for_down = call(block_kernel, (shape(4, 25, 4, 128), shape(10, 4, 128)), 1, 5)(
+        place, ends, before, after, prim, far_prior
+    )
     own = lax.all_to_all(block, "gy", 0, 0, tiled=True)
-    far_prior, far_next = shifted(for_up, "gx", 2), shifted(for_down, "gx", -2)
-    for_up, for_down = call(near_kernel, (shape(60, 4, 128), shape(60, 4, 128)), 1, 3)(
-        place, own, far_prior, far_next
+    far_next = shifted(for_down, "gx", -2)
+    for_up, for_down = call(near_kernel, (shape(60, 4, 128), shape(60, 4, 128)), 1, 2)(
+        place, own, far_next
     )
     prior, following = shifted(for_up, "gx", 1), shifted(for_down, "gx", -1)
     updated, message = call(

time: 80.8 us -> 82.3 us (1.019)
  waiting for transfers between devices: 3.15 us -> 7.82 us
  starting transfers between devices: 31.8 us -> 28.5 us
    ppermute x6, waiting for transfers between devices: 3.15 us -> 7.81 us  [shifted(): lax.ppermute(value, axis, [(i, (i + step) % size) for i in range(size)])]
    ppermute x6, starting transfers between devices: 28.5 us -> 24.5 us  [shifted(): lax.ppermute(value, axis, [(i, (i + step) % size) for i in range(size)])]
  transfers between devices with their start and end apart: 7 -> 7, of which waited for: 5 -> 4; matrix products, arithmetic and copies ran while one was open for 0% -> 0% of each run, Pallas kernels for 0% -> 0%
where the time goes in v4:
time: 82.3 us; the launch traced here: 81.8 us
  blocking collectives  30.3 us (37%)
  starting transfers between devices  28.5 us (35%)
  Pallas kernels  12.9 us (16%)
  waiting for transfers between devices  7.82 us (10%)
  other arithmetic  0.84 us (1%)
    ppermute x6, starting transfers between devices, shifted(): lax.ppermute(value, axis, [(i, (i + step) % size) for i in range(size)])  24.5 us
    all_to_all x1, blocking collectives, on_device(): got = lax.all_to_all(message, 'gz', 0, 0, tiled=True)  19.9 us
    all_to_all x1, blocking collectives, on_device(): incoming = lax.all_to_all(means, 'gz', 0, 0, tiled=True)  10.4 us
    ppermute x6, waiting for transfers between devices, shifted(): lax.ppermute(value, axis, [(i, (i + step) % size) for i in range(size)])  7.81 us
    pallas_call x1, Pallas kernels, on_device(): call(coarse_kernel, (shape(5, 4, 4, 128), shape(16, 2 * TILES - 1, 4, 128...  6.36 us
    all_to_all x1, starting transfers between devices, on_device(): own = lax.all_to_all(block, 'gy', 0, 0, tiled=True)  4.01 us
    pallas_call x1, Pallas kernels, on_device(): call(fine_kernel, (shape(5, 2, 8, 128), shape(16, 8, 128)), 1, 4, FINE_SC...  2.76 us
    pallas_call x1, Pallas kernels, on_device(): call(final_kernel, shape(5, 4, 4, 128), 1, 2, ((128, 128),))  1.82 us
  transfers between devices with their start and end apart: 7, of which 4 were waited for; matrix products, arithmetic and copies ran while one was open for 0% of the time, Pallas kernels for 0%

profile of v4, /device:TPU:1, one launch (start us, length us, event | category | flops | bytes accessed | tf_op | source)
XLA Modules:
  0.0 81.8 jit_solution(13902582871945798717)
XLA Ops:
  0.6 0.8 pad_maximum_fusion.prim_ref
  1.4 0.1 shard_map.95
  1.5 10.5 %collective-permute-start.1 = (f32[5,4,128]{2,1,0:T(4,128)S(1)}, f32[5,4,128]{2,1,0:T(4,128)S(1)}, u32[]{:S(2)}, u32[]{:S(2)}) collective-permute-start(f32[5,4,128]{2,1,0:T(4,128)S(1)} %get-tuple-element.12.ends_ref), channel_id=1, source_target_pairs={{0,15},{1,0},{2,1},{3,2},{4,3},{5,4},{6,5},{7,6},{8,7},{9,8},{10,9... | collective-permute-start | bytes 30728 | tf_op jit(solution)/shard_map/ppermute | solution.py:614
  12.0 0.0 collective-permute-start
  12.0 1.9 %collective-permute-start.2 = (f32[10,4,128]{2,1,0:T(4,128)S(1)}, f32[10,4,128]{2,1,0:T(4,128)S(1)}, u32[]{:S(2)}, u32[]{:S(2)}) collective-permute-start(f32[10,4,128]{2,1,0:T(4,128)S(1)} %get-tuple-element.13), channel_id=1, source_target_pairs={{0,128},{64,192},{128,256},{192,320},{256,384},{320,448},{384,512}... | collective-permute-start | bytes 61448 | tf_op jit(solution)/shard_map/ppermute | solution.py:614
  14.0 0.0 copy-start.3
  14.0 0.0 copy-start.4
  14.0 0.6 copy-done.3
  14.6 0.0 copy-done.4
  14.6 0.1 pad_add_fusion._.place_ref
  14.7 0.0 collective-permute-done.1.after_ref
  14.7 0.0 collective-permute-done.before_ref
  14.7 5.0 %collective-permute-done.2.__.far_prior_ref = f32[10,4,128]{2,1,0:T(4,128)S(1)} collective-permute-done((f32[10,4,128]{2,1,0:T(4,128)S(1)}, f32[10,4,128]{2,1,0:T(4,128)S(1)}, u32[]{:S(2)}, u32[]{:S(2)}) %collective-permute-start.2) | collective-permute-done | bytes 20512 | tf_op jit(solution)/shard_map/ppermute | solution.py:614
  19.7 1.3 %shard_map.96 = (f32[4,25,4,128]{3,2,1,0:T(4,128)}, f32[10,4,128]{2,1,0:T(4,128)S(1)}) custom-call(s32[66]{0:T(128)S(1)} %pad_add_fusion._.place_ref, f32[5,4,128]{2,1,0:T(4,128)S(1)} %get-tuple-element.12.ends_ref, f32[5,4,128]{2,1,0:T(4,128)S(1)} %collective-permute-done.before_ref, f32[5,4,128]{2,1,0:T(4,128)S(1)} %collective-permute-done.1.after_ref, ...), custom_call_target="tpu_custom_call" | custom-call | tf_op jit(solution)/shard_map/pallas_call | solution.py:627
  21.0 4.0 %all-to-all-start = ((f32[4,25,4,128]{3,2,1,0:T(4,128)}), f32[4,25,4,128]{3,2,1,0:T(4,128)S(1)}, u32[]{:S(2)}, u32[]{:S(2)}) async-start(f32[4,25,4,128]{3,2,1,0:T(4,128)} %get-tuple-element.14), calls=%async_computation | async-start | bytes 409600 | tf_op jit(solution)/shard_map/all_to_all | solution.py:630
  25.0 4.4 %collective-permute-start.3 = (f32[10,4,128]{2,1,0:T(4,128)S(1)}, f32[10,4,128]{2,1,0:T(4,128)S(1)}, u32[]{:S(2)}, u32[]{:S(2)}) collective-permute-start(f32[10,4,128]{2,1,0:T(4,128)S(1)} %get-tuple-element.15), channel_id=1, source_target_pairs={{0,640},{64,704},{128,0},{192,64},{256,128},{320,192},{384,256},{4... | collective-permute-start | bytes 61448 | tf_op jit(solution)/shard_map/ppermute | solution.py:614
  29.5 1.0 %collective-permute-done.3._.far_next_ref = f32[10,4,128]{2,1,0:T(4,128)S(1)} collective-permute-done((f32[10,4,128]{2,1,0:T(4,128)S(1)}, f32[10,4,128]{2,1,0:T(4,128)S(1)}, u32[]{:S(2)}, u32[]{:S(2)}) %collective-permute-start.3) | collective-permute-done | bytes 20512 | tf_op jit(solution)/shard_map/ppermute | solution.py:614
  30.4 0.0 all-to-all-done.own_ref
  30.4 0.6 shard_map.97
  31.0 3.3 %collective-permute-start.4 = (f32[60,4,128]{2,1,0:T(4,128)S(1)}, f32[60,4,128]{2,1,0:T(4,128)S(1)}, u32[]{:S(2)}, u32[]{:S(2)}) collective-permute-start(f32[60,4,128]{2,1,0:T(4,128)S(1)} %get-tuple-element.16), channel_id=1, source_target_pairs={{0,64},{64,128},{128,192},{192,256},{256,320},{320,384},{384,448},... | collective-permute-start | bytes 368648 | tf_op jit(solution)/shard_map/ppermute | solution.py:614
  34.3 4.3 %collective-permute-start.5 = (f32[60,4,128]{2,1,0:T(4,128)S(1)}, f32[60,4,128]{2,1,0:T(4,128)S(1)}, u32[]{:S(2)}, u32[]{:S(2)}) collective-permute-start(f32[60,4,128]{2,1,0:T(4,128)S(1)} %get-tuple-element.17), channel_id=1, source_target_pairs={{0,704},{64,0},{128,64},{192,128},{256,192},{320,256},{384,320},{4... | collective-permute-start | bytes 368648 | tf_op jit(solution)/shard_map/ppermute | solution.py:614
  38.6 0.3 collective-permute-done.4.prior_ref
  39.0 1.5 %collective-permute-done.5.next_ref = f32[60,4,128]{2,1,0:T(4,128)S(1)} collective-permute-done((f32[60,4,128]{2,1,0:T(4,128)S(1)}, f32[60,4,128]{2,1,0:T(4,128)S(1)}, u32[]{:S(2)}, u32[]{:S(2)}) %collective-permute-start.5) | collective-permute-done | bytes 122912 | tf_op jit(solution)/shard_map/ppermute | solution.py:614
  40.5 6.4 %shard_map.98 = (f32[5,4,4,128]{3,2,1,0:T(4,128)S(1)}, f32[16,5,4,128]{3,2,1,0:T(4,128)S(1)}) custom-call(s32[66]{0:T(128)S(1)} %pad_add_fusion._.place_ref, f32[4,25,4,128]{3,2,1,0:T(4,128)S(1)} %all-to-all-done.own_ref, f32[60,4,128]{2,1,0:T(4,128)S(1)} %collective-permute-done.4.prior_ref, f32[60,4,128]{2,1,0:T(4,128)S(1)} %collective-permute-done.5.next_ref, ...), custom_call_target="tpu_custom_call" | custom-call | tf_op jit(solution)/shard_map/pallas_call | solution.py:636
  46.9 0.0 copy-start
  46.9 0.0 copy-start.1
  46.9 0.0 copy-start.2
  46.9 19.9 %all_to_all.15.got_ref = f32[16,5,4,128]{3,2,1,0:T(4,128)S(1)} all-to-all(f32[16,5,4,128]{3,2,1,0:T(4,128)S(1)} %get-tuple-element.19), channel_id=1, replica_groups=mesh['gx'=12,'gy'=4,'gz'=16] {'gz'}, dimensions={0} | all-to-all | bytes 327680 | tf_op jit(solution)/shard_map/all_to_all | solution.py:653
  66.8 0.0 copy-done
  66.8 0.0 copy-done.1
  66.8 0.0 copy-done.2
  66.8 2.8 %shard_map.99 = (f32[5,2,8,128]{3,2,1,0:T(8,128)}, f32[16,8,128]{2,1,0:T(8,128)S(1)}) custom-call(s32[66]{0:T(128)S(1)} %pad_add_fusion._.place_ref, f32[16,5,4,128]{3,2,1,0:T(4,128)S(1)} %all_to_all.15.got_ref, f32[2,8,128]{2,1,0:T(8,128)S(1)} %bitcast.13, f32[3,2,8,128]{3,2,1,0:T(8,128)S(1)} %bitcast.12, f32[2,8,128]{2,1,0:T(8,128)S(1)} %bitcast.14), custom_call_target="tpu_custom_call" | custom-call | tf_op jit(solution)/shard_map/pallas_call | solution.py:654
  69.5 10.4 %all_to_all.16.got_ref = f32[16,8,128]{2,1,0:T(8,128)S(1)} all-to-all(f32[16,8,128]{2,1,0:T(8,128)S(1)} %get-tuple-element.20), channel_id=1, replica_groups=mesh['gx'=12,'gy'=4,'gz'=16] {'gz'}, dimensions={0} | all-to-all | bytes 131072 | tf_op jit(solution)/shard_map/all_to_all | solution.py:667
  80.0 1.8 %shard_map.100 = f32[5,4,4,128]{3,2,1,0:T(4,128)} custom-call(s32[66]{0:T(128)S(1)} %pad_add_fusion._.place_ref, f32[5,4,4,128]{3,2,1,0:T(4,128)S(1)} %get-tuple-element.18.new_ref, f32[16,8,128]{2,1,0:T(8,128)S(1)} %all_to_all.16.got_ref), custom_call_target="tpu_custom_call" | custom-call | tf_op jit(solution)/shard_map/pallas_call | solution.py:668
Async XLA Ops:
  1.5 13.2 %collective-permute-start.1 = (f32[5,4,128]{2,1,0:T(4,128)S(1)}, f32[5,4,128]{2,1,0:T(4,128)S(1)}, u32[]{:S(2)}, u32[]{:S(2)}) collective-permute-start(f32[5,4,128]{2,1,0:T(4,128)S(1)} %get-tuple-element.12.ends_ref), channel_id=1, source_target_pairs={{0,15},{1,0},{2,1},{3,2},{4,3},{5,4},{6,5},{7,6},{8,7},{9,8},{10,9... | collective-permute-start | bytes 30728 | tf_op jit(solution)/shard_map/ppermute | solution.py:614
  12.0 2.7 %collective-permute-start = (f32[5,4,128]{2,1,0:T(4,128)S(1)}, f32[5,4,128]{2,1,0:T(4,128)S(1)}, u32[]{:S(2)}, u32[]{:S(2)}) collective-permute-start(f32[5,4,128]{2,1,0:T(4,128)S(1)} %get-tuple-element.12.ends_ref), channel_id=1, source_target_pairs={{0,1},{1,2},{2,3},{3,4},{4,5},{5,6},{6,7},{7,8},{8,9},{9,10},{10,1... | collective-permute-start | bytes 30728 | tf_op jit(solution)/shard_map/ppermute | solution.py:614
  12.0 7.7 %collective-permute-start.2 = (f32[10,4,128]{2,1,0:T(4,128)S(1)}, f32[10,4,128]{2,1,0:T(4,128)S(1)}, u32[]{:S(2)}, u32[]{:S(2)}) collective-permute-start(f32[10,4,128]{2,1,0:T(4,128)S(1)} %get-tuple-element.13), channel_id=1, source_target_pairs={{0,128},{64,192},{128,256},{192,320},{256,384},{320,448},{384,512}... | collective-permute-start | bytes 61448 | tf_op jit(solution)/shard_map/ppermute | solution.py:614
  14.0 0.7 copy-start.3
  14.0 0.7 copy-start.4
  21.0 9.4 %all-to-all-start = ((f32[4,25,4,128]{3,2,1,0:T(4,128)}), f32[4,25,4,128]{3,2,1,0:T(4,128)S(1)}, u32[]{:S(2)}, u32[]{:S(2)}) async-start(f32[4,25,4,128]{3,2,1,0:T(4,128)} %get-tuple-element.14), calls=%async_computation | async-start | bytes 409600 | tf_op jit(solution)/shard_map/all_to_all | solution.py:630
  25.0 5.4 %collective-permute-start.3 = (f32[10,4,128]{2,1,0:T(4,128)S(1)}, f32[10,4,128]{2,1,0:T(4,128)S(1)}, u32[]{:S(2)}, u32[]{:S(2)}) collective-permute-start(f32[10,4,128]{2,1,0:T(4,128)S(1)} %get-tuple-element.15), channel_id=1, source_target_pairs={{0,640},{64,704},{128,0},{192,64},{256,128},{320,192},{384,256},{4... | collective-permute-start | bytes 61448 | tf_op jit(solution)/shard_map/ppermute | solution.py:614
  31.0 7.9 %collective-permute-start.4 = (f32[60,4,128]{2,1,0:T(4,128)S(1)}, f32[60,4,128]{2,1,0:T(4,128)S(1)}, u32[]{:S(2)}, u32[]{:S(2)}) collective-permute-start(f32[60,4,128]{2,1,0:T(4,128)S(1)} %get-tuple-element.16), channel_id=1, source_target_pairs={{0,64},{64,128},{128,192},{192,256},{256,320},{320,384},{384,448},... | collective-permute-start | bytes 368648 | tf_op jit(solution)/shard_map/ppermute | solution.py:614
  34.3 6.2 %collective-permute-start.5 = (f32[60,4,128]{2,1,0:T(4,128)S(1)}, f32[60,4,128]{2,1,0:T(4,128)S(1)}, u32[]{:S(2)}, u32[]{:S(2)}) collective-permute-start(f32[60,4,128]{2,1,0:T(4,128)S(1)} %get-tuple-element.17), channel_id=1, source_target_pairs={{0,704},{64,0},{128,64},{192,128},{256,192},{320,256},{384,320},{4... | collective-permute-start | bytes 368648 | tf_op jit(solution)/shard_map/ppermute | solution.py:614
  46.9 19.9 %copy-start = (f32[3,1,1,2,8,128]{5,4,3,2,1,0:T(8,128)S(1)}, f32[3,1,1,2,8,128]{5,4,3,2,1,0:T(8,128)}, u32[]{:S(2)}) copy-start(f32[3,1,1,2,8,128]{5,4,3,2,1,0:T(8,128)} %param.12) | copy-start | bytes 73732
  46.9 19.9 %copy-start.1 = (f32[1,1,2,8,128]{4,3,2,1,0:T(8,128)S(1)}, f32[1,1,2,8,128]{4,3,2,1,0:T(8,128)}, u32[]{:S(2)}) copy-start(f32[1,1,2,8,128]{4,3,2,1,0:T(8,128)} %param.11) | copy-start | bytes 24580
  46.9 19.9 %copy-start.2 = (f32[1,1,2,8,128]{4,3,2,1,0:T(8,128)S(1)}, f32[1,1,2,8,128]{4,3,2,1,0:T(8,128)}, u32[]{:S(2)}) copy-start(f32[1,1,2,8,128]{4,3,2,1,0:T(8,128)} %param.13) | copy-start | bytes 24580

commit v5 on v3

--- a/solution.py
+++ b/solution.py
@@ -330,13 +330,13 @@
             face = olds[-1 if x < 2 else 4][0]
             top, bottom = (-2, 4) if x % 2 == 0 else (-4, 2)
             for kind in range(3):
-                old_pack_ref[kind, 4 * f + x] = jnp.where(
+                old_pack_ref[kind, 4 * f + x] = roll(jnp.where(
                     sub == 0,
                     roll(face, top, 0),
                     jnp.where(sub == 7, roll(face, bottom, 0), olds[x][kind]),
-                )
+                ), GROUP * ((4 * f + x) % PER_ROW), 1)
         for half, (out, near, far) in enumerate(((-1, 0, 1), (4, 3, 2))):
-            body_ref[2 * f + half] = jnp.where(
+            body_ref[2 * f + half] = roll(jnp.where(
                 inner,
                 news[out][0],
                 jnp.where(
@@ -344,13 +344,13 @@
                     roll(news[far][0], -1, 0),
                     jnp.where(sub == 7, roll(news[far][0], 1, 0), news[near][0]),
                 ),
-            )
+            ), GROUP * ((OLD + 2 * f + half) % PER_ROW), 1)
             for kind in range(3):
-                tips_ref[kind, 2 * f + half] = jnp.where(
+                tips_ref[kind, 2 * f + half] = roll(jnp.where(
                     inner,
                     news[near][kind],
                     jnp.where(sub < 2, roll(news[far][kind], -2, 0), roll(news[far][kind], 2, 0)),
-                )
+                ), GROUP * ((OLD + 2 * f + half) % PER_ROW), 1)
 
     def send(turn, carry):
         for k_owner in range(SENDS):
@@ -358,22 +358,22 @@
             hit = parent_ref[2 * owner] == gz
             shift = jnp.where(hit, shift_ref[2 * owner], shift_ref[2 * owner + 1])
             kind = jnp.where(shift == 0, 1, jnp.where(shift == 120, 2, 0))
+            place = (lane + (129 - shift)) & 127
+            group = (place * 205) >> 11
+            within = place - GROUP * group
+            ends = (within == 0) | (within == GROUP - 1)
             for tile in range(TILES):
                 total = None
                 for j in range(PER_ROW):
                     k = tile * PER_ROW + j
                     if k >= OLD + 10:
                         break
-                    amount = lax.rem(GROUP * j + 129 - shift, 128)
                     if k < OLD:
-                        piece = pltpu.roll(old_pack_ref[kind, k], amount, 1)
+                        piece = old_pack_ref[kind, k]
                     else:
-                        piece = jnp.where(
-                            (lane == GROUP * j) | (lane == GROUP * j + 9),
-                            pltpu.roll(tips_ref[kind, k - OLD], amount, 1),
-                            pltpu.roll(body_ref[k - OLD], amount, 1),
-                        )
-                    total = piece if total is None else jnp.where(lane < GROUP * j, total, piece)
+                        piece = jnp.where(ends, tips_ref[kind, k - OLD], body_ref[k - OLD])
+                    total = piece if total is None else jnp.where(group == j, piece, total)
+                total = pltpu.roll(total, lax.rem(129 - shift, 128), 1)
                 if tile < TILES - 1:
                     message_ref[owner, 2 * tile] = total[0:4]
                     message_ref[owner, 2 * tile + 1] = total[4:8]
@@ -567,21 +567,17 @@
             other = parent_ref[2 * owner + 1] == gz
             shift = jnp.where(hit, shift_ref[2 * owner], shift_ref[2 * owner + 1])
             shift = jnp.where(hit | other, shift, 256)
-            inside = (lane >= shift) & (lane < shift + 8)
-            value = got_ref[owner]
-            count = count + jnp.where(inside, 1.0, 0.0)
-            sums = [
-                item
-                + jnp.where(inside, pltpu.roll(value, lax.rem(shift + 128 - 8 * k, 128), 1), 0.0)
-                for k, item in enumerate(sums)
-            ]
+            count = count + jnp.where((lane >= shift) & (lane < shift + 8), 1.0, 0.0)
+            value = pltpu.roll(got_ref[owner], lax.rem(shift, 128), 1)
+            group = jnp.where(shift < 256, ((lane + (256 - shift)) & 127) >> 3, 16)
+            sums = [item + jnp.where(group == k, value, 0.0) for k, item in enumerate(sums)]
         return count, sums
 
     zero = jnp.zeros((8, 128), F32)
     count, sums = lax.fori_loop(0, 16 // ADDS, add, (zero, [zero] * 16))
     share = inverse(jnp.maximum(count, 1.0))
     for k in range(16):
-        sum_ref[8 * k : 8 * k + 8] = sums[k] * share
+        sum_ref[8 * k : 8 * k + 8] = roll(sums[k], -8 * k, 1) * share
     for f in range(5):
         for x in range(4):
             start = (0 if f == 4 else 32 * f) + 2 * x + (1 if f == 4 else 0)

time: 80.8 us -> 79.7 us (0.986)
  Pallas kernels: 12.9 us -> 11.8 us
where the time goes in v5:
time: 79.7 us; the launch traced here: 79.2 us
  starting transfers between devices  31.8 us (40%)
  blocking collectives  30.1 us (38%)
  Pallas kernels  11.8 us (15%)
  waiting for transfers between devices  3.15 us (4%)
  other arithmetic  0.84 us (1%)
    ppermute x6, starting transfers between devices, shifted(): lax.ppermute(value, axis, [(i, (i + step) % size) for i in range(size)])  28.5 us
    all_to_all x1, blocking collectives, on_device(): got = lax.all_to_all(message, 'gz', 0, 0, tiled=True)  19.7 us
    all_to_all x1, blocking collectives, on_device(): incoming = lax.all_to_all(means, 'gz', 0, 0, tiled=True)  10.4 us
    pallas_call x1, Pallas kernels, on_device(): call(coarse_kernel, (shape(5, 4, 4, 128), shape(16, 2 * TILES - 1, 4, 128...  5.62 us
    all_to_all x1, starting transfers between devices, on_device(): own = lax.all_to_all(block, 'gy', 0, 0, tiled=True)  3.37 us
    ppermute x6, waiting for transfers between devices, shifted(): lax.ppermute(value, axis, [(i, (i + step) % size) for i in range(size)])  3.15 us
    pallas_call x1, Pallas kernels, on_device(): call(fine_kernel, (shape(5, 2, 8, 128), shape(16, 8, 128)), 1, 4, FINE_SC...  2.76 us
  transfers between devices with their start and end apart: 7, of which 5 were waited for; matrix products, arithmetic and copies ran while one was open for 0% of the time, Pallas kernels for 0%

profile of v5, /device:TPU:1, one launch (start us, length us, event | category | flops | bytes accessed | tf_op | source)
XLA Modules:
  0.0 79.2 jit_solution(12690956829717673973)
XLA Ops:
  0.6 0.8 pad_maximum_fusion.prim_ref
  1.4 0.1 shard_map.95.ends_ref
  1.5 10.5 %collective-permute-start.1 = (f32[5,4,128]{2,1,0:T(4,128)S(1)}, f32[5,4,128]{2,1,0:T(4,128)S(1)}, u32[]{:S(2)}, u32[]{:S(2)}) collective-permute-start(f32[5,4,128]{2,1,0:T(4,128)S(1)} %shard_map.95.ends_ref), channel_id=1, source_target_pairs={{0,15},{1,0},{2,1},{3,2},{4,3},{5,4},{6,5},{7,6},{8,7},{9,8},{10,9... | collective-permute-start | bytes 30728 | tf_op jit(solution)/shard_map/ppermute | solution.py:609
  12.0 0.0 collective-permute-start
  12.0 0.0 copy-start.3
  12.0 0.0 copy-start.4
  12.0 0.7 copy-done.3
  12.7 0.0 copy-done.4
  12.7 0.1 pad_add_fusion._.place_ref
  12.8 0.1 collective-permute-done.1.after_ref
  12.9 0.3 collective-permute-done.before_ref
  13.2 1.3 %shard_map.96 = (f32[4,25,4,128]{3,2,1,0:T(4,128)}, f32[10,4,128]{2,1,0:T(4,128)S(1)}, f32[10,4,128]{2,1,0:T(4,128)S(1)}) custom-call(s32[66]{0:T(128)S(1)} %pad_add_fusion._.place_ref, f32[5,4,128]{2,1,0:T(4,128)S(1)} %shard_map.95.ends_ref, f32[5,4,128]{2,1,0:T(4,128)S(1)} %collective-permute-done.before_ref, ...), custom_call_target="tpu_custom_call" | custom-call | tf_op jit(solution)/shard_map/pallas_call | solution.py:621
  14.5 3.4 %all-to-all-start = ((f32[4,25,4,128]{3,2,1,0:T(4,128)}), f32[4,25,4,128]{3,2,1,0:T(4,128)S(1)}, u32[]{:S(2)}, u32[]{:S(2)}) async-start(f32[4,25,4,128]{3,2,1,0:T(4,128)} %get-tuple-element.11), calls=%async_computation | async-start | bytes 409600 | tf_op jit(solution)/shard_map/all_to_all | solution.py:624
  17.9 1.9 %collective-permute-start.2 = (f32[10,4,128]{2,1,0:T(4,128)S(1)}, f32[10,4,128]{2,1,0:T(4,128)S(1)}, u32[]{:S(2)}, u32[]{:S(2)}) collective-permute-start(f32[10,4,128]{2,1,0:T(4,128)S(1)} %get-tuple-element.12), channel_id=1, source_target_pairs={{0,128},{64,192},{128,256},{192,320},{256,384},{320,448},{384,512}... | collective-permute-start | bytes 61448 | tf_op jit(solution)/shard_map/ppermute | solution.py:609
  19.8 8.3 %collective-permute-start.3 = (f32[10,4,128]{2,1,0:T(4,128)S(1)}, f32[10,4,128]{2,1,0:T(4,128)S(1)}, u32[]{:S(2)}, u32[]{:S(2)}) collective-permute-start(f32[10,4,128]{2,1,0:T(4,128)S(1)} %get-tuple-element.13), channel_id=1, source_target_pairs={{0,640},{64,704},{128,0},{192,64},{256,128},{320,192},{384,256},{4... | collective-permute-start | bytes 61448 | tf_op jit(solution)/shard_map/ppermute | solution.py:609
  28.1 0.0 collective-permute-done.2._.far_prior_ref
  28.1 0.9 %collective-permute-done.3.__.far_next_ref = f32[10,4,128]{2,1,0:T(4,128)S(1)} collective-permute-done((f32[10,4,128]{2,1,0:T(4,128)S(1)}, f32[10,4,128]{2,1,0:T(4,128)S(1)}, u32[]{:S(2)}, u32[]{:S(2)}) %collective-permute-start.3) | collective-permute-done | bytes 20512 | tf_op jit(solution)/shard_map/ppermute | solution.py:609
  29.0 0.0 all-to-all-done.own_ref
  29.0 0.6 shard_map.97
  29.6 3.1 %collective-permute-start.4 = (f32[60,4,128]{2,1,0:T(4,128)S(1)}, f32[60,4,128]{2,1,0:T(4,128)S(1)}, u32[]{:S(2)}, u32[]{:S(2)}) collective-permute-start(f32[60,4,128]{2,1,0:T(4,128)S(1)} %get-tuple-element.14), channel_id=1, source_target_pairs={{0,64},{64,128},{128,192},{192,256},{256,320},{320,384},{384,448},... | collective-permute-start | bytes 368648 | tf_op jit(solution)/shard_map/ppermute | solution.py:609
  32.7 4.6 %collective-permute-start.5 = (f32[60,4,128]{2,1,0:T(4,128)S(1)}, f32[60,4,128]{2,1,0:T(4,128)S(1)}, u32[]{:S(2)}, u32[]{:S(2)}) collective-permute-start(f32[60,4,128]{2,1,0:T(4,128)S(1)} %get-tuple-element.15), channel_id=1, source_target_pairs={{0,704},{64,0},{128,64},{192,128},{256,192},{320,256},{384,320},{4... | collective-permute-start | bytes 368648 | tf_op jit(solution)/shard_map/ppermute | solution.py:609
  37.3 0.3 collective-permute-done.4.prior_ref
  37.7 1.5 %collective-permute-done.5.next_ref = f32[60,4,128]{2,1,0:T(4,128)S(1)} collective-permute-done((f32[60,4,128]{2,1,0:T(4,128)S(1)}, f32[60,4,128]{2,1,0:T(4,128)S(1)}, u32[]{:S(2)}, u32[]{:S(2)}) %collective-permute-start.5) | collective-permute-done | bytes 122912 | tf_op jit(solution)/shard_map/ppermute | solution.py:609
  39.2 5.6 %shard_map.98 = (f32[5,4,4,128]{3,2,1,0:T(4,128)S(1)}, f32[16,5,4,128]{3,2,1,0:T(4,128)S(1)}) custom-call(s32[66]{0:T(128)S(1)} %pad_add_fusion._.place_ref, f32[4,25,4,128]{3,2,1,0:T(4,128)S(1)} %all-to-all-done.own_ref, f32[60,4,128]{2,1,0:T(4,128)S(1)} %collective-permute-done.4.prior_ref, f32[60,4,128]{2,1,0:T(4,128)S(1)} %collective-permute-done.5.next_ref, ...), custom_call_target="tpu_custom_call" | custom-call | tf_op jit(solution)/shard_map/pallas_call | solution.py:630
  44.8 0.0 copy-start
  44.8 0.0 copy-start.1
  44.8 0.0 copy-start.2
  44.8 19.7 %all_to_all.15.got_ref = f32[16,5,4,128]{3,2,1,0:T(4,128)S(1)} all-to-all(f32[16,5,4,128]{3,2,1,0:T(4,128)S(1)} %get-tuple-element.17), channel_id=1, replica_groups=mesh['gx'=12,'gy'=4,'gz'=16] {'gz'}, dimensions={0} | all-to-all | bytes 327680 | tf_op jit(solution)/shard_map/all_to_all | solution.py:647
  64.5 0.0 copy-done
  64.5 0.0 copy-done.1
  64.5 0.0 copy-done.2
  64.5 2.8 %shard_map.99 = (f32[5,2,8,128]{3,2,1,0:T(8,128)}, f32[16,8,128]{2,1,0:T(8,128)S(1)}) custom-call(s32[66]{0:T(128)S(1)} %pad_add_fusion._.place_ref, f32[16,5,4,128]{3,2,1,0:T(4,128)S(1)} %all_to_all.15.got_ref, f32[2,8,128]{2,1,0:T(8,128)S(1)} %bitcast.13, f32[3,2,8,128]{3,2,1,0:T(8,128)S(1)} %bitcast.12, f32[2,8,128]{2,1,0:T(8,128)S(1)} %bitcast.14), custom_call_target="tpu_custom_call" | custom-call | tf_op jit(solution)/shard_map/pallas_call | solution.py:648
  67.3 10.4 %all_to_all.16.got_ref = f32[16,8,128]{2,1,0:T(8,128)S(1)} all-to-all(f32[16,8,128]{2,1,0:T(8,128)S(1)} %get-tuple-element.18), channel_id=1, replica_groups=mesh['gx'=12,'gy'=4,'gz'=16] {'gz'}, dimensions={0} | all-to-all | bytes 131072 | tf_op jit(solution)/shard_map/all_to_all | solution.py:661
  77.7 1.4 %shard_map.100 = f32[5,4,4,128]{3,2,1,0:T(4,128)} custom-call(s32[66]{0:T(128)S(1)} %pad_add_fusion._.place_ref, f32[5,4,4,128]{3,2,1,0:T(4,128)S(1)} %get-tuple-element.16.new_ref, f32[16,8,128]{2,1,0:T(8,128)S(1)} %all_to_all.16.got_ref), custom_call_target="tpu_custom_call" | custom-call | tf_op jit(solution)/shard_map/pallas_call | solution.py:662
Async XLA Ops:
  1.5 11.4 %collective-permute-start.1 = (f32[5,4,128]{2,1,0:T(4,128)S(1)}, f32[5,4,128]{2,1,0:T(4,128)S(1)}, u32[]{:S(2)}, u32[]{:S(2)}) collective-permute-start(f32[5,4,128]{2,1,0:T(4,128)S(1)} %shard_map.95.ends_ref), channel_id=1, source_target_pairs={{0,15},{1,0},{2,1},{3,2},{4,3},{5,4},{6,5},{7,6},{8,7},{9,8},{10,9... | collective-permute-start | bytes 30728 | tf_op jit(solution)/shard_map/ppermute | solution.py:609
  12.0 1.2 %collective-permute-start = (f32[5,4,128]{2,1,0:T(4,128)S(1)}, f32[5,4,128]{2,1,0:T(4,128)S(1)}, u32[]{:S(2)}, u32[]{:S(2)}) collective-permute-start(f32[5,4,128]{2,1,0:T(4,128)S(1)} %shard_map.95.ends_ref), channel_id=1, source_target_pairs={{0,1},{1,2},{2,3},{3,4},{4,5},{5,6},{6,7},{7,8},{8,9},{9,10},{10,1... | collective-permute-start | bytes 30728 | tf_op jit(solution)/shard_map/ppermute | solution.py:609
  12.0 0.7 copy-start.3
  12.0 0.7 copy-start.4
  14.5 14.5 %all-to-all-start = ((f32[4,25,4,128]{3,2,1,0:T(4,128)}), f32[4,25,4,128]{3,2,1,0:T(4,128)S(1)}, u32[]{:S(2)}, u32[]{:S(2)}) async-start(f32[4,25,4,128]{3,2,1,0:T(4,128)} %get-tuple-element.11), calls=%async_computation | async-start | bytes 409600 | tf_op jit(solution)/shard_map/all_to_all | solution.py:624
  17.9 10.2 %collective-permute-start.2 = (f32[10,4,128]{2,1,0:T(4,128)S(1)}, f32[10,4,128]{2,1,0:T(4,128)S(1)}, u32[]{:S(2)}, u32[]{:S(2)}) collective-permute-start(f32[10,4,128]{2,1,0:T(4,128)S(1)} %get-tuple-element.12), channel_id=1, source_target_pairs={{0,128},{64,192},{128,256},{192,320},{256,384},{320,448},{384,512}... | collective-permute-start | bytes 61448 | tf_op jit(solution)/shard_map/ppermute | solution.py:609
  19.8 9.2 %collective-permute-start.3 = (f32[10,4,128]{2,1,0:T(4,128)S(1)}, f32[10,4,128]{2,1,0:T(4,128)S(1)}, u32[]{:S(2)}, u32[]{:S(2)}) collective-permute-start(f32[10,4,128]{2,1,0:T(4,128)S(1)} %get-tuple-element.13), channel_id=1, source_target_pairs={{0,640},{64,704},{128,0},{192,64},{256,128},{320,192},{384,256},{4... | collective-permute-start | bytes 61448 | tf_op jit(solution)/shard_map/ppermute | solution.py:609
  29.6 8.0 %collective-permute-start.4 = (f32[60,4,128]{2,1,0:T(4,128)S(1)}, f32[60,4,128]{2,1,0:T(4,128)S(1)}, u32[]{:S(2)}, u32[]{:S(2)}) collective-permute-start(f32[60,4,128]{2,1,0:T(4,128)S(1)} %get-tuple-element.14), channel_id=1, source_target_pairs={{0,64},{64,128},{128,192},{192,256},{256,320},{320,384},{384,448},... | collective-permute-start | bytes 368648 | tf_op jit(solution)/shard_map/ppermute | solution.py:609
  32.7 6.5 %collective-permute-start.5 = (f32[60,4,128]{2,1,0:T(4,128)S(1)}, f32[60,4,128]{2,1,0:T(4,128)S(1)}, u32[]{:S(2)}, u32[]{:S(2)}) collective-permute-start(f32[60,4,128]{2,1,0:T(4,128)S(1)} %get-tuple-element.15), channel_id=1, source_target_pairs={{0,704},{64,0},{128,64},{192,128},{256,192},{320,256},{384,320},{4... | collective-permute-start | bytes 368648 | tf_op jit(solution)/shard_map/ppermute | solution.py:609
  44.8 19.7 %copy-start = (f32[3,1,1,2,8,128]{5,4,3,2,1,0:T(8,128)S(1)}, f32[3,1,1,2,8,128]{5,4,3,2,1,0:T(8,128)}, u32[]{:S(2)}) copy-start(f32[3,1,1,2,8,128]{5,4,3,2,1,0:T(8,128)} %param.12) | copy-start | bytes 73732
  44.8 19.7 %copy-start.1 = (f32[1,1,2,8,128]{4,3,2,1,0:T(8,128)S(1)}, f32[1,1,2,8,128]{4,3,2,1,0:T(8,128)}, u32[]{:S(2)}) copy-start(f32[1,1,2,8,128]{4,3,2,1,0:T(8,128)} %param.11) | copy-start | bytes 24580
  44.8 19.7 %copy-start.2 = (f32[1,1,2,8,128]{4,3,2,1,0:T(8,128)S(1)}, f32[1,1,2,8,128]{4,3,2,1,0:T(8,128)}, u32[]{:S(2)}) copy-start(f32[1,1,2,8,128]{4,3,2,1,0:T(8,128)} %param.13) | copy-start | bytes 24580

commit v6 on v5

--- a/solution.py
+++ b/solution.py
@@ -172,8 +172,8 @@
             ref[5 + f] = edge
 
 
-def near_kernel(place_ref, own_ref, _, __, up_ref, down_ref):
-    gy = place_ref[0]
+def near_kernel(own_ref, _, __, up_ref, down_ref):
+    gy = lax.axis_index("gy")
     over, under = lax.rem(gy + 1, 4), lax.rem(gy + 3, 4)
     for ref, xs in ((up_ref, (3, 2, 1, 0)), (down_ref, (0, 1, 2, 3))):
 
@@ -195,12 +195,14 @@
 
 
 def coarse_kernel(
-    place_ref, own_ref, prior_ref, next_ref, far_prior_ref, far_next_ref,
+    table_ref, own_ref, prior_ref, next_ref, far_prior_ref, far_next_ref,
     new_ref, message_ref,
     prim_ref, edge_ref, section_ref, section_edge_ref, made_ref, made_edge_ref,
-    old_pack_ref, body_ref, tips_ref,
+    old_pack_ref, body_ref, tips_ref, place_ref, done,
 ):
-    gy, gz = place_ref[0], place_ref[1]
+    gy, gz = lax.axis_index("gy"), lax.axis_index("gz")
+    fetch = pltpu.make_async_copy(table_ref, place_ref, done)
+    fetch.start()
     parent_ref, shift_ref = Table(place_ref, 2), Table(place_ref, 34)
     for k in range(4):
         source = lax.rem(gy + k, 4)
@@ -383,6 +385,7 @@
                     )
         return carry
 
+    fetch.wait()
     lax.fori_loop(0, 16 // SENDS, send, 0)
 
 
@@ -599,7 +602,7 @@
         in_specs=[pl.BlockSpec(memory_space=pltpu.SMEM)] * scalars
         + [pl.BlockSpec(memory_space=pltpu.VMEM)] * arrays,
         out_specs=jax.tree.map(lambda _: pl.BlockSpec(memory_space=pltpu.VMEM), outs),
-        scratch_shapes=[pltpu.VMEM(dims, F32) for dims in scratch],
+        scratch_shapes=[pltpu.VMEM(k, F32) if isinstance(k, tuple) else k for k in scratch],
         compiler_params=pltpu.CompilerParams(vmem_limit_bytes=32 * 1024 * 1024),
     )
 
@@ -619,19 +622,19 @@
     ends = call(ends_kernel, shape(5, 4, 128), 0, 1)(prim)
     before, after = shifted(ends, "gz", 1), shifted(ends, "gz", -1)
     block, for_up, for_down = call(
-        block_kernel, (shape(4, 25, 4, 128), shape(10, 4, 128), shape(10, 4, 128)), 1, 4
+        block_kernel, (shape(4, 25, 4, 128), shape(10, 4, 128), shape(10, 4, 128)), 0, 5
     )(place, ends, before, after, prim)
     own = lax.all_to_all(block, "gy", 0, 0, tiled=True)
     far_prior, far_next = shifted(for_up, "gx", 2), shifted(for_down, "gx", -2)
-    for_up, for_down = call(near_kernel, (shape(60, 4, 128), shape(60, 4, 128)), 1, 3)(
-        place, own, far_prior, far_next
+    for_up, for_down = call(near_kernel, (shape(60, 4, 128), shape(60, 4, 128)), 0, 3)(
+        own, far_prior, far_next
     )
     prior, following = shifted(for_up, "gx", 1), shifted(for_down, "gx", -1)
     updated, message = call(
         coarse_kernel,
         (shape(5, 4, 4, 128), shape(16, 2 * TILES - 1, 4, 128)),
-        1,
-        5,
+        0,
+        6,
         (
             (70, 16, 128),
             (25, 16, 128),
@@ -642,6 +645,8 @@
             (3, 20, 8, 128),
             (10, 8, 128),
             (3, 10, 8, 128),
+            pltpu.SMEM((66,), jnp.int32),
+            pltpu.SemaphoreType.DMA,
         ),
     )(place, own, prior, following, far_prior, far_next)
     got = lax.all_to_all(message, "gz", 0, 0, tiled=True)

time: 79.7 us -> 78.1 us (0.980)
  Pallas kernels: 11.8 us -> 10.2 us
where the time goes in v6:
time: 78.1 us; the launch traced here: 77.6 us
  starting transfers between devices  31.8 us (41%)
  blocking collectives  30.1 us (39%)
  Pallas kernels  10.2 us (13%)
  waiting for transfers between devices  3.15 us (4%)
  other arithmetic  0.84 us (1%)
    ppermute x6, starting transfers between devices, shifted(): lax.ppermute(value, axis, [(i, (i + step) % size) for i in range(size)])  28.5 us
    all_to_all x1, blocking collectives, on_device(): got = lax.all_to_all(message, 'gz', 0, 0, tiled=True)  19.7 us
    all_to_all x1, blocking collectives, on_device(): incoming = lax.all_to_all(means, 'gz', 0, 0, tiled=True)  10.4 us
    pallas_call x1, Pallas kernels, on_device(): call(coarse_kernel, (shape(5, 4, 4, 128), shape(16, 2 * TILES - 1, 4, 128...  5.11 us
    all_to_all x1, starting transfers between devices, on_device(): own = lax.all_to_all(block, 'gy', 0, 0, tiled=True)  3.37 us
    ppermute x6, waiting for transfers between devices, shifted(): lax.ppermute(value, axis, [(i, (i + step) % size) for i in range(size)])  3.15 us
    pallas_call x1, Pallas kernels, on_device(): call(fine_kernel, (shape(5, 2, 8, 128), shape(16, 8, 128)), 1, 4, FINE_SC...  2.76 us
  transfers between devices with their start and end apart: 7, of which 5 were waited for; matrix products, arithmetic and copies ran while one was open for 0% of the time, Pallas kernels for 0%

profile of v6, /device:TPU:1, one launch (start us, length us, event | category | flops | bytes accessed | tf_op | source)
XLA Modules:
  0.0 77.6 jit_solution(7262686186679706934)
XLA Ops:
  0.6 0.8 pad_maximum_fusion.prim_ref
  1.4 0.1 shard_map.95.ends_ref
  1.5 10.5 %collective-permute-start.1 = (f32[5,4,128]{2,1,0:T(4,128)S(1)}, f32[5,4,128]{2,1,0:T(4,128)S(1)}, u32[]{:S(2)}, u32[]{:S(2)}) collective-permute-start(f32[5,4,128]{2,1,0:T(4,128)S(1)} %shard_map.95.ends_ref), channel_id=1, source_target_pairs={{0,15},{1,0},{2,1},{3,2},{4,3},{5,4},{6,5},{7,6},{8,7},{9,8},{10,9... | collective-permute-start | bytes 30728 | tf_op jit(solution)/shard_map/ppermute | solution.py:612
  12.0 0.0 collective-permute-start
  12.0 0.0 copy-start.3
  12.0 0.0 copy-start.4
  12.0 0.7 copy-done.3
  12.7 0.0 copy-done.4
  12.7 0.1 pad_add_fusion._.table_ref.place_ref
  12.8 0.1 collective-permute-done.1.after_ref
  12.9 0.3 collective-permute-done.before_ref
  13.2 0.8 shard_map.96
  14.0 3.4 %all-to-all-start = ((f32[4,25,4,128]{3,2,1,0:T(4,128)}), f32[4,25,4,128]{3,2,1,0:T(4,128)S(1)}, u32[]{:S(2)}, u32[]{:S(2)}) async-start(f32[4,25,4,128]{3,2,1,0:T(4,128)} %get-tuple-element.11), calls=%async_computation | async-start | bytes 409600 | tf_op jit(solution)/shard_map/all_to_all | solution.py:627
  17.4 1.9 %collective-permute-start.2 = (f32[10,4,128]{2,1,0:T(4,128)S(1)}, f32[10,4,128]{2,1,0:T(4,128)S(1)}, u32[]{:S(2)}, u32[]{:S(2)}) collective-permute-start(f32[10,4,128]{2,1,0:T(4,128)S(1)} %get-tuple-element.12), channel_id=1, source_target_pairs={{0,128},{64,192},{128,256},{192,320},{256,384},{320,448},{384,512}... | collective-permute-start | bytes 61448 | tf_op jit(solution)/shard_map/ppermute | solution.py:612
  19.3 8.3 %collective-permute-start.3 = (f32[10,4,128]{2,1,0:T(4,128)S(1)}, f32[10,4,128]{2,1,0:T(4,128)S(1)}, u32[]{:S(2)}, u32[]{:S(2)}) collective-permute-start(f32[10,4,128]{2,1,0:T(4,128)S(1)} %get-tuple-element.13), channel_id=1, source_target_pairs={{0,640},{64,704},{128,0},{192,64},{256,128},{320,192},{384,256},{4... | collective-permute-start | bytes 61448 | tf_op jit(solution)/shard_map/ppermute | solution.py:612
  27.6 0.0 collective-permute-done.2._.far_prior_ref
  27.6 0.9 %collective-permute-done.3.__.far_next_ref = f32[10,4,128]{2,1,0:T(4,128)S(1)} collective-permute-done((f32[10,4,128]{2,1,0:T(4,128)S(1)}, f32[10,4,128]{2,1,0:T(4,128)S(1)}, u32[]{:S(2)}, u32[]{:S(2)}) %collective-permute-start.3) | collective-permute-done | bytes 20512 | tf_op jit(solution)/shard_map/ppermute | solution.py:612
  28.5 0.0 all-to-all-done.own_ref
  28.5 3.1 %collective-permute-start.4 = (f32[60,4,128]{2,1,0:T(4,128)S(1)}, f32[60,4,128]{2,1,0:T(4,128)S(1)}, u32[]{:S(2)}, u32[]{:S(2)}) collective-permute-start(f32[60,4,128]{2,1,0:T(4,128)S(1)} %get-tuple-element.14), channel_id=1, source_target_pairs={{0,64},{64,128},{128,192},{192,256},{256,320},{320,384},{384,448},... | collective-permute-start | bytes 368648 | tf_op jit(solution)/shard_map/ppermute | solution.py:612
  31.6 4.6 %collective-permute-start.5 = (f32[60,4,128]{2,1,0:T(4,128)S(1)}, f32[60,4,128]{2,1,0:T(4,128)S(1)}, u32[]{:S(2)}, u32[]{:S(2)}) collective-permute-start(f32[60,4,128]{2,1,0:T(4,128)S(1)} %get-tuple-element.15), channel_id=1, source_target_pairs={{0,704},{64,0},{128,64},{192,128},{256,192},{320,256},{384,320},{4... | collective-permute-start | bytes 368648 | tf_op jit(solution)/shard_map/ppermute | solution.py:612
  36.3 0.3 collective-permute-done.4.prior_ref
  36.6 1.5 %collective-permute-done.5.next_ref = f32[60,4,128]{2,1,0:T(4,128)S(1)} collective-permute-done((f32[60,4,128]{2,1,0:T(4,128)S(1)}, f32[60,4,128]{2,1,0:T(4,128)S(1)}, u32[]{:S(2)}, u32[]{:S(2)}) %collective-permute-start.5) | collective-permute-done | bytes 122912 | tf_op jit(solution)/shard_map/ppermute | solution.py:612
  38.1 5.1 %shard_map.98 = (f32[5,4,4,128]{3,2,1,0:T(4,128)S(1)}, f32[16,5,4,128]{3,2,1,0:T(4,128)S(1)}) custom-call(s32[66]{0:T(128)S(1)} %pad_add_fusion._.table_ref.place_ref, f32[4,25,4,128]{3,2,1,0:T(4,128)S(1)} %all-to-all-done.own_ref, f32[60,4,128]{2,1,0:T(4,128)S(1)} %collective-permute-done.4.prior_ref, f32[60,4,128]{2,1,0:T(4,128)S(1)} %collective-permute-done.5.next_ref, ...), custom_call_target="tpu_custom_call" | custom-call | tf_op jit(solution)/shard_map/pallas_call | solution.py:633
  43.2 0.0 copy-start
  43.2 0.0 copy-start.1
  43.2 0.0 copy-start.2
  43.3 19.7 %all_to_all.15.got_ref = f32[16,5,4,128]{3,2,1,0:T(4,128)S(1)} all-to-all(f32[16,5,4,128]{3,2,1,0:T(4,128)S(1)} %get-tuple-element.17), channel_id=1, replica_groups=mesh['gx'=12,'gy'=4,'gz'=16] {'gz'}, dimensions={0} | all-to-all | bytes 327680 | tf_op jit(solution)/shard_map/all_to_all | solution.py:652
  63.0 0.0 copy-done
  63.0 0.0 copy-done.1
  63.0 0.0 copy-done.2
  63.0 2.8 %shard_map.99 = (f32[5,2,8,128]{3,2,1,0:T(8,128)}, f32[16,8,128]{2,1,0:T(8,128)S(1)}) custom-call(s32[66]{0:T(128)S(1)} %pad_add_fusion._.table_ref.place_ref, f32[16,5,4,128]{3,2,1,0:T(4,128)S(1)} %all_to_all.15.got_ref, f32[2,8,128]{2,1,0:T(8,128)S(1)} %bitcast.13, f32[3,2,8,128]{3,2,1,0:T(8,128)S(1)} %bitcast.12, f32[2,8,128]{2,1,0:T(8,128)S(1)} %bitcast.14), custom_call_target="tpu_custom_call" | custom-call | tf_op jit(solution)/shard_map/pallas_call | solution.py:653
  65.7 10.4 %all_to_all.16.got_ref = f32[16,8,128]{2,1,0:T(8,128)S(1)} all-to-all(f32[16,8,128]{2,1,0:T(8,128)S(1)} %get-tuple-element.18), channel_id=1, replica_groups=mesh['gx'=12,'gy'=4,'gz'=16] {'gz'}, dimensions={0} | all-to-all | bytes 131072 | tf_op jit(solution)/shard_map/all_to_all | solution.py:666
  76.2 1.4 %shard_map.100 = f32[5,4,4,128]{3,2,1,0:T(4,128)} custom-call(s32[66]{0:T(128)S(1)} %pad_add_fusion._.table_ref.place_ref, f32[5,4,4,128]{3,2,1,0:T(4,128)S(1)} %get-tuple-element.16.new_ref, f32[16,8,128]{2,1,0:T(8,128)S(1)} %all_to_all.16.got_ref), custom_call_target="tpu_custom_call" | custom-call | tf_op jit(solution)/shard_map/pallas_call | solution.py:667
  (1 shorter events, 0.0 us)
Async XLA Ops:
  1.5 11.4 %collective-permute-start.1 = (f32[5,4,128]{2,1,0:T(4,128)S(1)}, f32[5,4,128]{2,1,0:T(4,128)S(1)}, u32[]{:S(2)}, u32[]{:S(2)}) collective-permute-start(f32[5,4,128]{2,1,0:T(4,128)S(1)} %shard_map.95.ends_ref), channel_id=1, source_target_pairs={{0,15},{1,0},{2,1},{3,2},{4,3},{5,4},{6,5},{7,6},{8,7},{9,8},{10,9... | collective-permute-start | bytes 30728 | tf_op jit(solution)/shard_map/ppermute | solution.py:612
  12.0 1.2 %collective-permute-start = (f32[5,4,128]{2,1,0:T(4,128)S(1)}, f32[5,4,128]{2,1,0:T(4,128)S(1)}, u32[]{:S(2)}, u32[]{:S(2)}) collective-permute-start(f32[5,4,128]{2,1,0:T(4,128)S(1)} %shard_map.95.ends_ref), channel_id=1, source_target_pairs={{0,1},{1,2},{2,3},{3,4},{4,5},{5,6},{6,7},{7,8},{8,9},{9,10},{10,1... | collective-permute-start | bytes 30728 | tf_op jit(solution)/shard_map/ppermute | solution.py:612
  12.0 0.7 copy-start.3
  12.0 0.7 copy-start.4
  14.0 14.5 %all-to-all-start = ((f32[4,25,4,128]{3,2,1,0:T(4,128)}), f32[4,25,4,128]{3,2,1,0:T(4,128)S(1)}, u32[]{:S(2)}, u32[]{:S(2)}) async-start(f32[4,25,4,128]{3,2,1,0:T(4,128)} %get-tuple-element.11), calls=%async_computation | async-start | bytes 409600 | tf_op jit(solution)/shard_map/all_to_all | solution.py:627
  17.4 10.2 %collective-permute-start.2 = (f32[10,4,128]{2,1,0:T(4,128)S(1)}, f32[10,4,128]{2,1,0:T(4,128)S(1)}, u32[]{:S(2)}, u32[]{:S(2)}) collective-permute-start(f32[10,4,128]{2,1,0:T(4,128)S(1)} %get-tuple-element.12), channel_id=1, source_target_pairs={{0,128},{64,192},{128,256},{192,320},{256,384},{320,448},{384,512}... | collective-permute-start | bytes 61448 | tf_op jit(solution)/shard_map/ppermute | solution.py:612
  19.3 9.2 %collective-permute-start.3 = (f32[10,4,128]{2,1,0:T(4,128)S(1)}, f32[10,4,128]{2,1,0:T(4,128)S(1)}, u32[]{:S(2)}, u32[]{:S(2)}) collective-permute-start(f32[10,4,128]{2,1,0:T(4,128)S(1)} %get-tuple-element.13), channel_id=1, source_target_pairs={{0,640},{64,704},{128,0},{192,64},{256,128},{320,192},{384,256},{4... | collective-permute-start | bytes 61448 | tf_op jit(solution)/shard_map/ppermute | solution.py:612
  28.5 8.0 %collective-permute-start.4 = (f32[60,4,128]{2,1,0:T(4,128)S(1)}, f32[60,4,128]{2,1,0:T(4,128)S(1)}, u32[]{:S(2)}, u32[]{:S(2)}) collective-permute-start(f32[60,4,128]{2,1,0:T(4,128)S(1)} %get-tuple-element.14), channel_id=1, source_target_pairs={{0,64},{64,128},{128,192},{192,256},{256,320},{320,384},{384,448},... | collective-permute-start | bytes 368648 | tf_op jit(solution)/shard_map/ppermute | solution.py:612
  31.6 6.5 %collective-permute-start.5 = (f32[60,4,128]{2,1,0:T(4,128)S(1)}, f32[60,4,128]{2,1,0:T(4,128)S(1)}, u32[]{:S(2)}, u32[]{:S(2)}) collective-permute-start(f32[60,4,128]{2,1,0:T(4,128)S(1)} %get-tuple-element.15), channel_id=1, source_target_pairs={{0,704},{64,0},{128,64},{192,128},{256,192},{320,256},{384,320},{4... | collective-permute-start | bytes 368648 | tf_op jit(solution)/shard_map/ppermute | solution.py:612
  43.2 19.7 %copy-start = (f32[3,1,1,2,8,128]{5,4,3,2,1,0:T(8,128)S(1)}, f32[3,1,1,2,8,128]{5,4,3,2,1,0:T(8,128)}, u32[]{:S(2)}) copy-start(f32[3,1,1,2,8,128]{5,4,3,2,1,0:T(8,128)} %param.12) | copy-start | bytes 73732
  43.2 19.7 %copy-start.1 = (f32[1,1,2,8,128]{4,3,2,1,0:T(8,128)S(1)}, f32[1,1,2,8,128]{4,3,2,1,0:T(8,128)}, u32[]{:S(2)}) copy-start(f32[1,1,2,8,128]{4,3,2,1,0:T(8,128)} %param.11) | copy-start | bytes 24580
  43.2 19.7 %copy-start.2 = (f32[1,1,2,8,128]{4,3,2,1,0:T(8,128)S(1)}, f32[1,1,2,8,128]{4,3,2,1,0:T(8,128)}, u32[]{:S(2)}) copy-start(f32[1,1,2,8,128]{4,3,2,1,0:T(8,128)} %param.13) | copy-start | bytes 24580

commit v7 on v6

--- a/solution.py
+++ b/solution.py
@@ -196,7 +196,7 @@
 
 def coarse_kernel(
     table_ref, own_ref, prior_ref, next_ref, far_prior_ref, far_next_ref,
-    new_ref, message_ref,
+    new_ref, message_ref, owned_ref, spots_ref,
     prim_ref, edge_ref, section_ref, section_edge_ref, made_ref, made_edge_ref,
     old_pack_ref, body_ref, tips_ref, place_ref, done,
 ):
@@ -386,26 +386,37 @@
         return carry
 
     fetch.wait()
+    for box in range(2):
+        owned_ref[box] = jnp.full((8, 128), parent_ref[2 * gz + box], jnp.int32)
+    for owner in range(16):
+        hit, other = parent_ref[2 * owner] == gz, parent_ref[2 * owner + 1] == gz
+        shift = jnp.where(hit, shift_ref[2 * owner], shift_ref[2 * owner + 1])
+        spots_ref[owner] = jnp.full((8, 128), jnp.where(hit | other, shift, 256), jnp.int32)
     lax.fori_loop(0, 16 // SENDS, send, 0)
 
 
 def fine_kernel(
-    place_ref, got_ref, rho_ref, vel_ref, p_ref, out_ref, message_ref,
+    owned_ref, got_ref, rho_ref, vel_ref, p_ref, out_ref, message_ref,
     mid_ref, tip_ref, ghost_ref, bound_ref,
 ):
-    gz = place_ref[1]
-    parent_ref = Table(place_ref, 2)
     lane, sub = iota(1), iota(0)
     part = lane % 16
     yc, xc = lane // 32, sub // 2
-    parents = [parent_ref[2 * gz + box] for box in range(2)]
+
+    def slot(box, tile):
+        named = owned_ref[box, 0:4]
+        found = got_ref[0, tile]
+        for parent in range(1, 16):
+            found = jnp.where(named == parent, got_ref[parent, tile], found)
+        return found
+
 
     for box in range(2):
         tiles = [
-            jnp.concatenate([got_ref[parents[box], 2 * t], got_ref[parents[box], 2 * t + 1]])
+            jnp.concatenate([slot(box, 2 * t), slot(box, 2 * t + 1)])
             for t in range(TILES - 1)
         ]
-        short = got_ref[parents[box], 2 * TILES - 2]
+        short = slot(box, 2 * TILES - 2)
         tiles.append(jnp.concatenate([short, roll(short, -60, 1)]))
         for k in range(OLD + 10):
             j = k % PER_ROW
@@ -537,6 +548,7 @@
         return start, state
 
     _, states = lax.fori_loop(0, 4, stage, (states, states), unroll=4)
+    means = []
     for box in range(2):
         packed = None
         for f in range(5):
@@ -554,25 +566,23 @@
                 packed = jnp.where(lane // 32 == f, value, packed)
             else:
                 packed = jnp.where((sub % 2 == 1) & (lane < 32), roll(value, 1, 0), packed)
-        message_ref[parents[box]] = packed
-
-
-def final_kernel(place_ref, new_ref, got_ref, out_ref, sum_ref):
-    gz = place_ref[1]
-    parent_ref, shift_ref = Table(place_ref, 2), Table(place_ref, 34)
+        means.append(packed)
+    for parent in range(16):
+        message_ref[parent] = jnp.where(owned_ref[0] == parent, means[0], means[1])
+
+
+def final_kernel(spots_ref, new_ref, got_ref, out_ref, sum_ref):
     lane = iota(1)
 
     def add(turn, carry):
         count, sums = carry
         for k_owner in range(ADDS):
             owner = ADDS * turn + k_owner
-            hit = parent_ref[2 * owner] == gz
-            other = parent_ref[2 * owner + 1] == gz
-            shift = jnp.where(hit, shift_ref[2 * owner], shift_ref[2 * owner + 1])
-            shift = jnp.where(hit | other, shift, 256)
+            shift = spots_ref[owner]
             count = count + jnp.where((lane >= shift) & (lane < shift + 8), 1.0, 0.0)
-            value = pltpu.roll(got_ref[owner], lax.rem(shift, 128), 1)
-            group = jnp.where(shift < 256, ((lane + (256 - shift)) & 127) >> 3, 16)
+            away = (lane + (256 - shift)) & 127
+            value = jnp.take_along_axis(got_ref[owner], away, axis=1)
+            group = jnp.where(shift < 256, away >> 3, 16)
             sums = [item + jnp.where(group == k, value, 0.0) for k, item in enumerate(sums)]
         return count, sums
 
@@ -630,9 +640,14 @@
         own, far_prior, far_next
     )
     prior, following = shifted(for_up, "gx", 1), shifted(for_down, "gx", -1)
-    updated, message = call(
+    updated, message, owned, spots = call(
         coarse_kernel,
-        (shape(5, 4, 4, 128), shape(16, 2 * TILES - 1, 4, 128)),
+        (
+            shape(5, 4, 4, 128),
+            shape(16, 2 * TILES - 1, 4, 128),
+            jax.ShapeDtypeStruct((2, 8, 128), jnp.int32),
+            jax.ShapeDtypeStruct((16, 8, 128), jnp.int32),
+        ),
         0,
         6,
         (
@@ -653,18 +668,18 @@
     fine, means = call(
         fine_kernel,
         (shape(5, 2, 8, 128), shape(16, 8, 128)),
-        1,
-        4,
+        0,
+        5,
         FINE_SCRATCH,
     )(
-        place,
+        owned,
         got,
         fine_density.reshape(2, 8, 128),
         fine_velocity.reshape(3, 2, 8, 128),
         fine_pressure.reshape(2, 8, 128),
     )
     incoming = lax.all_to_all(means, "gz", 0, 0, tiled=True)
-    coarse = call(final_kernel, shape(5, 4, 4, 128), 1, 2, ((128, 128),))(place, updated, incoming)
+    coarse = call(final_kernel, shape(5, 4, 4, 128), 0, 3, ((128, 128),))(spots, updated, incoming)
     return coarse, fine.reshape(5, 1, 1, 2, 8, 128)
 
 

time: 78.1 us -> 77.1 us (0.987)
  Pallas kernels: 10.2 us -> 9.22 us
    pallas_call x2, Pallas kernels: 4.19 us -> 3.17 us  [the longest x1 2.29 us: on_device(): call(fine_kernel, (shape(5, 2, 8, 128), shape(16, 8, 128)), 0, 5, FINE_SC...]
where the time goes in v7:
time: 77.1 us; the launch traced here: 76.6 us
  starting transfers between devices  31.8 us (41%)
  blocking collectives  30.1 us (39%)
  Pallas kernels  9.22 us (12%)
  waiting for transfers between devices  3.15 us (4%)
  other arithmetic  0.84 us (1%)
    ppermute x6, starting transfers between devices, shifted(): lax.ppermute(value, axis, [(i, (i + step) % size) for i in range(size)])  28.5 us
    all_to_all x1, blocking collectives, on_device(): got = lax.all_to_all(message, 'gz', 0, 0, tiled=True)  19.7 us
    all_to_all x1, blocking collectives, on_device(): incoming = lax.all_to_all(means, 'gz', 0, 0, tiled=True)  10.4 us
    pallas_call x1, Pallas kernels, on_device(): call(coarse_kernel, (shape(5, 4, 4, 128), shape(16, 2 * TILES - 1, 4, 128...  5.15 us
    all_to_all x1, starting transfers between devices, on_device(): own = lax.all_to_all(block, 'gy', 0, 0, tiled=True)  3.37 us
    ppermute x6, waiting for transfers between devices, shifted(): lax.ppermute(value, axis, [(i, (i + step) % size) for i in range(size)])  3.15 us
    pallas_call x1, Pallas kernels, on_device(): call(fine_kernel, (shape(5, 2, 8, 128), shape(16, 8, 128)), 0, 5, FINE_SC...  2.29 us
  transfers between devices with their start and end apart: 7, of which 5 were waited for; matrix products, arithmetic and copies ran while one was open for 0% of the time, Pallas kernels for 0%

profile of v7, /device:TPU:1, one launch (start us, length us, event | category | flops | bytes accessed | tf_op | source)
XLA Modules:
  0.0 76.6 jit_solution(16758523920710437705)
XLA Ops:
  0.6 0.8 pad_maximum_fusion.prim_ref
  1.4 0.1 shard_map.95.ends_ref
  1.5 10.5 %collective-permute-start.1 = (f32[5,4,128]{2,1,0:T(4,128)S(1)}, f32[5,4,128]{2,1,0:T(4,128)S(1)}, u32[]{:S(2)}, u32[]{:S(2)}) collective-permute-start(f32[5,4,128]{2,1,0:T(4,128)S(1)} %shard_map.95.ends_ref), channel_id=1, source_target_pairs={{0,15},{1,0},{2,1},{3,2},{4,3},{5,4},{6,5},{7,6},{8,7},{9,8},{10,9... | collective-permute-start | bytes 30728 | tf_op jit(solution)/shard_map/ppermute | solution.py:622
  12.0 0.0 collective-permute-start
  12.0 0.0 copy-start.3
  12.0 0.0 copy-start.4
  12.0 0.7 copy-done.3
  12.7 0.0 copy-done.4
  12.7 0.1 pad_add_fusion._.table_ref
  12.8 0.1 collective-permute-done.1.after_ref
  12.9 0.3 collective-permute-done.before_ref
  13.2 0.8 shard_map.96
  14.0 3.4 %all-to-all-start = ((f32[4,25,4,128]{3,2,1,0:T(4,128)}), f32[4,25,4,128]{3,2,1,0:T(4,128)S(1)}, u32[]{:S(2)}, u32[]{:S(2)}) async-start(f32[4,25,4,128]{3,2,1,0:T(4,128)} %get-tuple-element.13), calls=%async_computation | async-start | bytes 409600 | tf_op jit(solution)/shard_map/all_to_all | solution.py:637
  17.4 1.9 %collective-permute-start.2 = (f32[10,4,128]{2,1,0:T(4,128)S(1)}, f32[10,4,128]{2,1,0:T(4,128)S(1)}, u32[]{:S(2)}, u32[]{:S(2)}) collective-permute-start(f32[10,4,128]{2,1,0:T(4,128)S(1)} %get-tuple-element.14), channel_id=1, source_target_pairs={{0,128},{64,192},{128,256},{192,320},{256,384},{320,448},{384,512}... | collective-permute-start | bytes 61448 | tf_op jit(solution)/shard_map/ppermute | solution.py:622
  19.3 8.3 %collective-permute-start.3 = (f32[10,4,128]{2,1,0:T(4,128)S(1)}, f32[10,4,128]{2,1,0:T(4,128)S(1)}, u32[]{:S(2)}, u32[]{:S(2)}) collective-permute-start(f32[10,4,128]{2,1,0:T(4,128)S(1)} %get-tuple-element.15), channel_id=1, source_target_pairs={{0,640},{64,704},{128,0},{192,64},{256,128},{320,192},{384,256},{4... | collective-permute-start | bytes 61448 | tf_op jit(solution)/shard_map/ppermute | solution.py:622
  27.6 0.0 collective-permute-done.2._.far_prior_ref
  27.6 0.9 %collective-permute-done.3.__.far_next_ref = f32[10,4,128]{2,1,0:T(4,128)S(1)} collective-permute-done((f32[10,4,128]{2,1,0:T(4,128)S(1)}, f32[10,4,128]{2,1,0:T(4,128)S(1)}, u32[]{:S(2)}, u32[]{:S(2)}) %collective-permute-start.3) | collective-permute-done | bytes 20512 | tf_op jit(solution)/shard_map/ppermute | solution.py:622
  28.5 0.0 all-to-all-done.own_ref
  28.5 3.1 %collective-permute-start.4 = (f32[60,4,128]{2,1,0:T(4,128)S(1)}, f32[60,4,128]{2,1,0:T(4,128)S(1)}, u32[]{:S(2)}, u32[]{:S(2)}) collective-permute-start(f32[60,4,128]{2,1,0:T(4,128)S(1)} %get-tuple-element.16), channel_id=1, source_target_pairs={{0,64},{64,128},{128,192},{192,256},{256,320},{320,384},{384,448},... | collective-permute-start | bytes 368648 | tf_op jit(solution)/shard_map/ppermute | solution.py:622
  31.6 4.6 %collective-permute-start.5 = (f32[60,4,128]{2,1,0:T(4,128)S(1)}, f32[60,4,128]{2,1,0:T(4,128)S(1)}, u32[]{:S(2)}, u32[]{:S(2)}) collective-permute-start(f32[60,4,128]{2,1,0:T(4,128)S(1)} %get-tuple-element.17), channel_id=1, source_target_pairs={{0,704},{64,0},{128,64},{192,128},{256,192},{320,256},{384,320},{4... | collective-permute-start | bytes 368648 | tf_op jit(solution)/shard_map/ppermute | solution.py:622
  36.3 0.3 collective-permute-done.4.prior_ref
  36.6 1.5 %collective-permute-done.5.next_ref = f32[60,4,128]{2,1,0:T(4,128)S(1)} collective-permute-done((f32[60,4,128]{2,1,0:T(4,128)S(1)}, f32[60,4,128]{2,1,0:T(4,128)S(1)}, u32[]{:S(2)}, u32[]{:S(2)}) %collective-permute-start.5) | collective-permute-done | bytes 122912 | tf_op jit(solution)/shard_map/ppermute | solution.py:622
  38.1 5.2 %shard_map.98 = (f32[5,4,4,128]{3,2,1,0:T(4,128)S(1)}, f32[16,5,4,128]{3,2,1,0:T(4,128)S(1)}, s32[2,8,128]{2,1,0:T(8,128)S(1)}, s32[16,8,128]{2,1,0:T(8,128)S(1)}) custom-call(s32[66]{0:T(128)S(1)} %pad_add_fusion._.table_ref, f32[4,25,4,128]{3,2,1,0:T(4,128)S(1)} %all-to-all-done.own_ref, f32[60,4,128]{2,1,0:T(4,128)S(1)} %collective-permute-done.4.prior_ref, ...), custom_call_target="tpu_custom_call" | custom-call | tf_op jit(solution)/shard_map/pallas_call | solution.py:643
  43.3 0.0 copy-start
  43.3 0.0 copy-start.1
  43.3 0.0 copy-start.2
  43.3 19.7 %all_to_all.15.got_ref = f32[16,5,4,128]{3,2,1,0:T(4,128)S(1)} all-to-all(f32[16,5,4,128]{3,2,1,0:T(4,128)S(1)} %get-tuple-element.21), channel_id=1, replica_groups=mesh['gx'=12,'gy'=4,'gz'=16] {'gz'}, dimensions={0} | all-to-all | bytes 327680 | tf_op jit(solution)/shard_map/all_to_all | solution.py:667
  63.0 0.0 copy-done
  63.0 0.0 copy-done.1
  63.0 0.0 copy-done.2
  63.0 2.3 %shard_map.99 = (f32[5,2,8,128]{3,2,1,0:T(8,128)}, f32[16,8,128]{2,1,0:T(8,128)S(1)}) custom-call(s32[2,8,128]{2,1,0:T(8,128)S(1)} %get-tuple-element.20.owned_ref, f32[16,5,4,128]{3,2,1,0:T(4,128)S(1)} %all_to_all.15.got_ref, f32[2,8,128]{2,1,0:T(8,128)S(1)} %bitcast.13, f32[3,2,8,128]{3,2,1,0:T(8,128)S(1)} %bitcast.12, f32[2,8,128]{2,1,0:T(8,128)S(1)} %bitcast.14), custom_call_target="tpu_custom_call" | custom-call | tf_op jit(solution)/shard_map/pallas_call | solution.py:668
  65.3 10.4 %all_to_all.16.got_ref = f32[16,8,128]{2,1,0:T(8,128)S(1)} all-to-all(f32[16,8,128]{2,1,0:T(8,128)S(1)} %get-tuple-element.22), channel_id=1, replica_groups=mesh['gx'=12,'gy'=4,'gz'=16] {'gz'}, dimensions={0} | all-to-all | bytes 131072 | tf_op jit(solution)/shard_map/all_to_all | solution.py:681
  75.7 0.9 %shard_map.100 = f32[5,4,4,128]{3,2,1,0:T(4,128)} custom-call(s32[16,8,128]{2,1,0:T(8,128)S(1)} %get-tuple-element.18.spots_ref, f32[5,4,4,128]{3,2,1,0:T(4,128)S(1)} %get-tuple-element.19.new_ref, f32[16,8,128]{2,1,0:T(8,128)S(1)} %all_to_all.16.got_ref), custom_call_target="tpu_custom_call" | custom-call | tf_op jit(solution)/shard_map/pallas_call | solution.py:682
  (1 shorter events, 0.0 us)
Async XLA Ops:
  1.5 11.4 %collective-permute-start.1 = (f32[5,4,128]{2,1,0:T(4,128)S(1)}, f32[5,4,128]{2,1,0:T(4,128)S(1)}, u32[]{:S(2)}, u32[]{:S(2)}) collective-permute-start(f32[5,4,128]{2,1,0:T(4,128)S(1)} %shard_map.95.ends_ref), channel_id=1, source_target_pairs={{0,15},{1,0},{2,1},{3,2},{4,3},{5,4},{6,5},{7,6},{8,7},{9,8},{10,9... | collective-permute-start | bytes 30728 | tf_op jit(solution)/shard_map/ppermute | solution.py:622
  12.0 1.2 %collective-permute-start = (f32[5,4,128]{2,1,0:T(4,128)S(1)}, f32[5,4,128]{2,1,0:T(4,128)S(1)}, u32[]{:S(2)}, u32[]{:S(2)}) collective-permute-start(f32[5,4,128]{2,1,0:T(4,128)S(1)} %shard_map.95.ends_ref), channel_id=1, source_target_pairs={{0,1},{1,2},{2,3},{3,4},{4,5},{5,6},{6,7},{7,8},{8,9},{9,10},{10,1... | collective-permute-start | bytes 30728 | tf_op jit(solution)/shard_map/ppermute | solution.py:622
  12.0 0.7 copy-start.3
  12.0 0.7 copy-start.4
  14.0 14.5 %all-to-all-start = ((f32[4,25,4,128]{3,2,1,0:T(4,128)}), f32[4,25,4,128]{3,2,1,0:T(4,128)S(1)}, u32[]{:S(2)}, u32[]{:S(2)}) async-start(f32[4,25,4,128]{3,2,1,0:T(4,128)} %get-tuple-element.13), calls=%async_computation | async-start | bytes 409600 | tf_op jit(solution)/shard_map/all_to_all | solution.py:637
  17.4 10.2 %collective-permute-start.2 = (f32[10,4,128]{2,1,0:T(4,128)S(1)}, f32[10,4,128]{2,1,0:T(4,128)S(1)}, u32[]{:S(2)}, u32[]{:S(2)}) collective-permute-start(f32[10,4,128]{2,1,0:T(4,128)S(1)} %get-tuple-element.14), channel_id=1, source_target_pairs={{0,128},{64,192},{128,256},{192,320},{256,384},{320,448},{384,512}... | collective-permute-start | bytes 61448 | tf_op jit(solution)/shard_map/ppermute | solution.py:622
  19.3 9.2 %collective-permute-start.3 = (f32[10,4,128]{2,1,0:T(4,128)S(1)}, f32[10,4,128]{2,1,0:T(4,128)S(1)}, u32[]{:S(2)}, u32[]{:S(2)}) collective-permute-start(f32[10,4,128]{2,1,0:T(4,128)S(1)} %get-tuple-element.15), channel_id=1, source_target_pairs={{0,640},{64,704},{128,0},{192,64},{256,128},{320,192},{384,256},{4... | collective-permute-start | bytes 61448 | tf_op jit(solution)/shard_map/ppermute | solution.py:622
  28.5 8.0 %collective-permute-start.4 = (f32[60,4,128]{2,1,0:T(4,128)S(1)}, f32[60,4,128]{2,1,0:T(4,128)S(1)}, u32[]{:S(2)}, u32[]{:S(2)}) collective-permute-start(f32[60,4,128]{2,1,0:T(4,128)S(1)} %get-tuple-element.16), channel_id=1, source_target_pairs={{0,64},{64,128},{128,192},{192,256},{256,320},{320,384},{384,448},... | collective-permute-start | bytes 368648 | tf_op jit(solution)/shard_map/ppermute | solution.py:622
  31.6 6.5 %collective-permute-start.5 = (f32[60,4,128]{2,1,0:T(4,128)S(1)}, f32[60,4,128]{2,1,0:T(4,128)S(1)}, u32[]{:S(2)}, u32[]{:S(2)}) collective-permute-start(f32[60,4,128]{2,1,0:T(4,128)S(1)} %get-tuple-element.17), channel_id=1, source_target_pairs={{0,704},{64,0},{128,64},{192,128},{256,192},{320,256},{384,320},{4... | collective-permute-start | bytes 368648 | tf_op jit(solution)/shard_map/ppermute | solution.py:622
  43.3 19.7 %copy-start = (f32[3,1,1,2,8,128]{5,4,3,2,1,0:T(8,128)S(1)}, f32[3,1,1,2,8,128]{5,4,3,2,1,0:T(8,128)}, u32[]{:S(2)}) copy-start(f32[3,1,1,2,8,128]{5,4,3,2,1,0:T(8,128)} %param.12) | copy-start | bytes 73732
  43.3 19.7 %copy-start.1 = (f32[1,1,2,8,128]{4,3,2,1,0:T(8,128)S(1)}, f32[1,1,2,8,128]{4,3,2,1,0:T(8,128)}, u32[]{:S(2)}) copy-start(f32[1,1,2,8,128]{4,3,2,1,0:T(8,128)} %param.11) | copy-start | bytes 24580
  43.3 19.7 %copy-start.2 = (f32[1,1,2,8,128]{4,3,2,1,0:T(8,128)S(1)}, f32[1,1,2,8,128]{4,3,2,1,0:T(8,128)}, u32[]{:S(2)}) copy-start(f32[1,1,2,8,128]{4,3,2,1,0:T(8,128)} %param.13) | copy-start | bytes 24580
